TPU v7x, 256 devices: a whole 4x4x8 slice. The times are simulated.
256 devices in a mesh: doc: 32 (over z_lo, x, core), term: 8 (over y, z_hi).
Axes of the slice: x: 4, y: 4, z: 8 (z_hi: 2, z_lo: 4; z = z_hi * 4 + z_lo), core: 2. Of those that a mesh axis runs over, the one named last changes fastest.
Arguments:
- blocks: bfloat16 [32, 2560, 128, 128], P('doc', 'term'), may hold values from -6 to 6
- block_rows: int32 [32, 2560], P('doc', 'term'), may hold values from 0 to 63, as said below
- block_cols: int32 [32, 2560], P('doc', 'term'), may hold values from 0 to 63, as said below
- counts: int32 [32, 8], P('doc', 'term'), may hold values from 80 to 320, as said below
- start_panel: float32 [16, 65536], P(None, 'term'), may hold values from -6 to 6
Outputs:
- left_panel: float32 [16, 262144], P(None, 'doc')
- right_panel: float32 [16, 65536], P(None, 'term')
Inputs may be any that keep to these rules, and one draw needn't show every extreme that they name: `block_rows`: within one tile the slots name distinct blocks. `block_cols`: within one tile the slots name distinct blocks. Some tile uses all 320 slots; slots from counts on are unused.
All inputs are finite; a program needn't handle non-finite values.
Results may differ from a plain program's by a relative error of at most 0.0092.
Values sent between devices are 32-bit elements; how exact they have to be, the bound alone decides.
No kernel may reach another device: no remote copies, remote signals or barrier semaphores. Data moves between devices by JAX's collectives and lax.ppermute only.
A program may use at most 64 MiB of HBM per device.

v0:
```python
import functools

import jax
import jax.numpy as jnp
import numpy as np
from jax import lax
from jax.experimental import pallas as pl
from jax.experimental.pallas import tpu as pltpu
from jax.sharding import Mesh
from jax.sharding import PartitionSpec as P

BLK = 128
K = 16
BR = 64
NB = 320
GROUP = 32
SHARERS = 64
DOC = ("zl", "x", "c")
TERM = ("y", "zh")
F32 = jnp.float32
BF = jnp.bfloat16
HI = lax.Precision.HIGHEST
VMEM = pltpu.VMEM
SMEM = pltpu.SMEM
ANY = pl.ANY


def mm(a, b):
    return jnp.dot(a, b, precision=HI, preferred_element_type=F32)


def mmt(a, b):
    return lax.dot_general(a, b, (((1,), (1,)), ((), ())), precision=HI, preferred_element_type=F32)


def inverse_factor(gram):
    lane = lax.broadcasted_iota(jnp.int32, (K, BLK), 1)
    row = lax.broadcasted_iota(jnp.int32, (K, BLK), 0)
    left = columns(gram)
    result = jnp.where(lane == row, 1.0, 0.0)
    scale = jnp.zeros((K, BLK), F32)
    for j in range(K):
        pivot = left[j][j : j + 1, :]
        scale = jnp.where(row == j, lax.rsqrt(pivot), scale)
        if j == K - 1:
            break
        factor = jnp.where(row > j, left[j] * (1.0 / pivot), 0.0)
        result = result - factor * result[j : j + 1, :]
        for k in range(j + 1, K):
            left[k] = left[k] - factor * left[k][j : j + 1, :]
    return (result * scale)[:, 0:K]


def projected(ext, count):
    proj = ext[:, K : 2 * K] / count
    return proj, inverse_factor(ext[:, 0:K] / count - mmt(proj, proj))


def columns(matrix):
    return [jnp.broadcast_to(matrix[:, j : j + 1], (K, BLK)) for j in range(K)]


def combine(cols, piece):
    total = cols[0] * piece[0:1, :]
    for j in range(1, K):
        total = total + cols[j] * piece[j : j + 1, :]
    return total


def parts(value):
    high = value.astype(BF)
    rest = value - high.astype(F32)
    middle = rest.astype(BF)
    low = (rest - middle.astype(F32)).astype(BF)
    return high, middle, low


def stacked(value):
    return jnp.concatenate(parts(value), axis=0)


def split_store(split_ref, index, value):
    high, middle, low = parts(value)
    split_ref[index, 0:16, :] = high
    split_ref[index, 16:32, :] = middle
    split_ref[index, 32:48, :] = low


def each(count, body, unroll=4):
    def step(i, carry):
        body(i)
        return carry

    lax.fori_loop(0, count, step, 0, unroll=unroll)


def split_all(split_ref, base, piece, count):
    each(count, lambda i: split_store(split_ref, base + i, piece[i]), 8)


def cross(left, right):
    return lax.dot_general(left, right, (((1,), (1,)), ((), ())), preferred_element_type=F32)


def fold(wide):
    rows = (wide[32:48, :] + wide[16:32, :]) + wide[0:16, :]
    return (rows[:, 32:48] + rows[:, 16:32]) + rows[:, 0:16]


def pad_lanes(*pieces):
    width = sum(p.shape[1] for p in pieces)
    return jnp.concatenate([*pieces, jnp.zeros((K, BLK - width), F32)], axis=1)


def spin(index, step):
    return jnp.bitwise_and(index - step, 3)


def group_of(base, live, src_ref, tgt_ref, block, split, acc, place, spare):
    spots, values = [], []
    for u in range(GROUP):
        slot = base + u
        wide = jnp.dot(split[src_ref[0, slot]], block(slot), preferred_element_type=F32)
        values.append((wide[32:48, :] + wide[16:32, :]) + wide[0:16, :])
        spots.append(jnp.where(slot < live, place(tgt_ref[0, slot]), spare))
    for spot, value in zip(spots, values):
        acc[spot] += value


def term_place(y):
    def place(target):
        part = jnp.bitwise_and(lax.shift_right_logical(target, 4) - y, 3)
        return part * 17 + jnp.bitwise_and(target, 15)

    return place


def doc_place(x, core):
    def place(target):
        half = jnp.bitwise_xor(lax.shift_right_logical(target, 5), core)
        part = jnp.bitwise_and(lax.shift_right_logical(target, 3) - x, 3)
        return half * 36 + part * 9 + jnp.bitwise_and(target, 7)

    return place


def multiply(live, src_ref, tgt_ref, held, split, acc, place, spare):
    def step(g, carry):
        group_of(g * GROUP, live, src_ref, tgt_ref, lambda s: held[s], split, acc, place, spare)
        return carry

    lax.fori_loop(0, lax.div(live + (GROUP - 1), GROUP), step, 0)


def gram_step(count, value_of, total, unroll=8):
    def step(i, carry):
        value = value_of(i)
        return carry + cross(value, value)

    return lax.fori_loop(0, count, step, total, unroll=unroll)


def first_forward(
    rows_any, cols_any, counts_any, start_any, blocks, o0, o1, o2, o3, held, turned,
    rows, cols, counts, start, split, acc, sems, small_sems,
):
    groups = NB // GROUP
    small = [
        pltpu.make_async_copy(start_any, start, small_sems.at[0]),
        pltpu.make_async_copy(rows_any, rows, small_sems.at[1]),
        pltpu.make_async_copy(cols_any, cols, small_sems.at[2]),
        pltpu.make_async_copy(counts_any, counts, small_sems.at[3]),
    ]
    for copy in small:
        copy.start()
    for i in range(groups):
        part = pl.ds(i * GROUP, GROUP)
        pltpu.make_async_copy(blocks.at[0, part], held.at[part], sems.at[i]).start()
    acc[...] = jnp.zeros_like(acc)
    for copy in small:
        copy.wait()

    def prepare(i):
        value = stacked(start[:, pl.ds(pl.multiple_of(i * BLK, BLK), BLK)])
        split[i] = value
        return value

    ext = pad_lanes(fold(gram_step(BR, prepare, jnp.zeros((48, 48), F32), 16)))
    live = counts[0, 0]
    place = term_place(lax.axis_index("y"))

    def turn(slot):
        value = held[slot].T
        turned[slot] = value
        return value

    def step(i, carry):
        part = pl.ds(i * GROUP, GROUP)
        pltpu.make_async_copy(blocks.at[0, part], held.at[part], sems.at[i]).wait()

        @pl.when(i * GROUP < live)
        def _():
            group_of(i * GROUP, live, cols, rows, turn, split, acc, place, 16)

        return carry

    lax.fori_loop(0, groups, step, 0)
    for k, out in enumerate((o0, o1, o2, o3)):
        out[0:16] = acc[k * 17 : k * 17 + 16]
        out[16] = ext


def forward(rows, cols, counts, r0, r1, r2, r3, w0, w1, w2, w3, turned, o0, o1, o2, o3, split, acc, grams):
    x, core = lax.axis_index("x"), lax.axis_index("c")
    acc[...] = jnp.zeros_like(acc)
    for side, pieces in ((core, (r0, r1, r2, r3)), (1 - core, (w0, w1, w2, w3))):
        for k, piece in enumerate(pieces):
            base = side * 32 + spin(x, k) * 8
            split_all(split, base, piece, 8)
            grams[side * 4 + spin(x, k)] = piece[8]
    multiply(counts[0, 0], cols, rows, turned, split, acc, term_place(lax.axis_index("y")), 16)
    ext = grams[0]
    for i in range(1, 8):
        ext = ext + grams[i]
    for k, out in enumerate((o0, o1, o2, o3)):
        out[0:16] = acc[k * 17 : k * 17 + 16]
        out[16] = ext


def backward(rows, cols, counts, p0, p1, p2, p3, held, own, other, split, acc, grams):
    y = lax.axis_index("y")
    acc[...] = jnp.zeros_like(acc)
    for k, piece in enumerate((p0, p1, p2, p3)):
        base = spin(y, k) * 16
        split_all(split, base, piece, 16)
        grams[spin(y, k)] = piece[16]
    place = doc_place(lax.axis_index("x"), lax.axis_index("c"))
    multiply(counts[0, 0], rows, cols, held, split, acc, place, 8)
    ext = ((grams[0] + grams[1]) + grams[2]) + grams[3]
    for j in range(8):
        acc[j * 9 + 8] = ext
    own[...] = acc[0:36]
    other[...] = acc[36:72]


def left_first(mine, theirs, out, mr0, *, terms):
    inverse = inverse_factor((mine[16] + theirs[16])[:, 0:K] / terms)
    mr0[...] = pad_lanes(inverse)
    cols = columns(inverse)
    gram = jnp.zeros((48, 48), F32)
    for i in range(16):
        value = combine(cols, mine[i] + theirs[i])
        out[i] = value
        wide = stacked(value)
        gram = gram + cross(wide, wide)
    out[16] = pad_lanes(fold(gram))


def zl_total(t0, t1, t2, t3, order):
    zl = lax.axis_index("zl")
    for k, piece in enumerate((t0, t1, t2, t3)):
        order[spin(zl, k)] = piece[...]
    return lambda i: ((order[0, i] + order[1, i]) + order[2, i]) + order[3, i]


def right_first(t0, t1, t2, t3, start, mr0, out, ml1, right0, order, *, docs):
    total = zl_total(t0, t1, t2, t3, order)
    x, core = lax.axis_index("x"), lax.axis_index("c")
    first = (core * 32 + x * 8) * BLK
    inverse = inverse_factor(total(8)[:, 0:K] / docs)
    ml1[...] = pad_lanes(inverse)
    cols_0 = columns(mr0[:, 0:K])
    cols_1 = columns(inverse)
    gram = jnp.zeros((48, 48), F32)
    mixed = jnp.zeros((48, 48), F32)
    for i in range(8):
        source = pl.ds(pl.multiple_of(first + i * BLK, BLK), BLK)
        prior = combine(cols_0, start[:, source])
        right0[i] = prior
        value = combine(cols_1, total(i))
        out[i] = value
        wide = stacked(value)
        gram = gram + cross(wide, wide)
        mixed = mixed + cross(wide, stacked(prior))
    out[8] = pad_lanes(fold(gram), fold(mixed))


def left_second(mine, theirs, left_raw, ml1, out, mr1, h1, *, terms):
    proj, inverse = projected(mine[16] + theirs[16], terms)
    mr1[...] = pad_lanes(inverse)
    h1[...] = pad_lanes(proj)
    cols_l = columns(ml1[:, 0:K])
    cols_h = columns(proj)
    for i in range(16):
        out[i] = (mine[i] + theirs[i]) - combine(cols_h, left_raw[i])
    cols_m = columns(inverse)
    gram = jnp.zeros((48, 48), F32)
    mixed = jnp.zeros((48, 48), F32)
    for i in range(16):
        prior = stacked(combine(cols_l, left_raw[i]))
        value = combine(cols_m, out[i])
        out[i] = value
        wide = stacked(value)
        gram = gram + cross(wide, wide)
        mixed = mixed + cross(wide, prior)
    out[16] = pad_lanes(fold(gram), fold(mixed))


def right_second(t0, t1, t2, t3, right_raw, prior, out, ext_out, ml2, h2, order, *, docs):
    total = zl_total(t0, t1, t2, t3, order)
    first = lax.axis_index("c") * 32 + lax.axis_index("x") * 8
    proj, inverse = projected(total(8), docs)
    ml2[...] = pad_lanes(inverse)
    h2[...] = pad_lanes(proj)
    cols_h = columns(proj)
    for i in range(8):
        out[i] = total(i) - combine(cols_h, right_raw[i])
    cols_m = columns(inverse)
    gram = jnp.zeros((48, 48), F32)
    mixed = jnp.zeros((48, 48), F32)
    for i in range(8):
        value = combine(cols_m, out[i])
        out[i] = value
        wide = stacked(value)
        gram = gram + cross(wide, wide)
        mixed = mixed + cross(wide, prior[first + i])
    both = jnp.concatenate([fold(gram), fold(mixed)], axis=1)
    ext_out[...] = jnp.broadcast_to(
        jnp.concatenate([both[0:8], both[8:16], jnp.zeros((8, 64), F32)], axis=1)[None], (SHARERS, 8, BLK)
    )


def lanes(index):
    return pl.ds(pl.multiple_of(index * BLK, BLK), BLK)


def factor_parts(*matrices):
    tall = [jnp.concatenate([p.astype(F32) for p in parts(m)], axis=0) for m in matrices]
    return jnp.concatenate([t for t in tall for _ in range(3)], axis=1).astype(BF)


def mix(factors, first, second):
    wide = jnp.dot(factors, jnp.concatenate([first, second], axis=0), preferred_element_type=F32)
    return (wide[32:48, :] + wide[16:32, :]) + wide[0:16, :]


def left_result(a0, a1, a2, a3, b0, b1, b2, b3, ml1, ml2, h2, out):
    y = lax.axis_index("y")
    inverse = ml2[:, 0:K]
    factors = factor_parts(inverse, -mm(mm(inverse, h2[:, 0:K]), ml1[:, 0:K]))
    for k, (first, second) in enumerate(zip((a0, a1, a2, a3), (b0, b1, b2, b3))):
        base = spin(y, k) * 16

        def result(i, base=base, first=first, second=second):
            out[:, lanes(base + i)] = mix(factors, stacked(second[i]), stacked(first[i]))

        each(16, result, 8)


def by_side(pieces):
    x, core = lax.axis_index("x"), lax.axis_index("c")
    for n, piece in enumerate(pieces):
        side = core if n < 4 else 1 - core
        yield side * 32 + spin(x, n % 4) * 8, piece


def right_prior(r0, r1, r2, r3, w0, w1, w2, w3, start, mr0, mr1, h1, out, work):
    cols_0 = columns(mr0[:, 0:K])

    def from_start(i):
        work[i] = combine(cols_0, start[:, lanes(i)])

    each(BR, from_start)
    cols_h = columns(h1[:, 0:K])
    for base, piece in by_side((r0, r1, r2, r3, w0, w1, w2, w3)):

        def rest(i, base=base, piece=piece):
            work[base + i] = piece[i] - combine(cols_h, work[base + i])

        each(8, rest)
    cols_1 = columns(mr1[:, 0:K])

    def final(i):
        split_store(out, i, combine(cols_1, work[i]))

    each(BR, final)


def right_result(ext, r0, r1, r2, r3, w0, w1, w2, w3, right1, out, *, terms):
    total = ext[0]
    for i in range(1, SHARERS):
        total = total + ext[i]
    both = jnp.concatenate([total[:, 0 : 2 * K], total[:, 2 * K : 4 * K]], axis=0)
    proj, inverse = projected(both, terms)
    factors = factor_parts(inverse, -mm(inverse, proj))
    for base, piece in by_side((r0, r1, r2, r3, w0, w1, w2, w3)):

        def result(i, base=base, piece=piece):
            out[:, lanes(base + i)] = mix(factors, stacked(piece[i]), right1[base + i])

        each(8, result, 8)


def panel(n):
    return jax.ShapeDtypeStruct((n, K, BLK), F32)


SMALL = jax.ShapeDtypeStruct((K, BLK), F32)
WIDE = jax.ShapeDtypeStruct((K, BR * BLK), F32)
TILE = jax.ShapeDtypeStruct((NB, BLK, BLK), BF)
SPLIT = VMEM((BR, 48, BLK), BF)


def held_panel(n):
    return VMEM((n, K, BLK), F32)


def call(body, args, outs, scratch=(), spaces=None, limit=8, micros=2, **constants):
    def space(a):
        return SMEM if a.dtype == jnp.int32 else VMEM

    spaces = spaces or [space(a) for a in args]
    return pl.pallas_call(
        functools.partial(body, **constants) if constants else body,
        name=body.__name__,
        out_shape=outs,
        in_specs=[pl.BlockSpec(memory_space=s) for s in spaces],
        out_specs=jax.tree.map(lambda _: pl.BlockSpec(memory_space=VMEM), outs),
        scratch_shapes=list(scratch),
        cost_estimate=pl.CostEstimate(
            flops=micros * 1000000000, bytes_accessed=micros * 1000000, transcendentals=0
        ),
        compiler_params=pltpu.CompilerParams(vmem_limit_bytes=limit * 1024 * 1024),
    )(*args)


SWAP = [(0, 1), (1, 0)]


def shift(value, axis, k):
    return lax.ppermute(value, axis, [(i, (i + k) % 4) for i in range(4)])


def gather(value, axis):
    return [value] + [shift(value, axis, k) for k in (1, 2, 3)]


def total_of(got):
    return ((got[0] + got[1]) + got[2]) + got[3]


def scatter_term(pieces):
    got = [pieces[0]] + [shift(pieces[k], "y", k) for k in (1, 2, 3)]
    mine = total_of(got)
    return mine, lax.ppermute(mine, "zh", SWAP)


def scatter_doc(own, other):
    got = lax.ppermute(other, "c", SWAP)
    pieces = [own[9 * k : 9 * k + 9] + got[9 * k : 9 * k + 9] for k in range(4)]
    got = [pieces[0]] + [shift(pieces[k], "x", k) for k in (1, 2, 3)]
    return gather(total_of(got), "zl")


def gather_doc(value):
    mine = gather(value, "x")
    return mine + [lax.ppermute(m, "c", SWAP) for m in mine]


def local(blocks, block_rows, block_cols, counts, start):
    docs = float(BR * BLK * 32)
    terms = float(BR * BLK * 8)
    index = (block_rows, block_cols, counts)

    *pieces, held, turned = call(
        first_forward,
        (*index, start, blocks),
        (panel(17),) * 4 + (TILE, TILE),
        [
            SMEM((1, NB), jnp.int32), SMEM((1, NB), jnp.int32), SMEM((1, 1), jnp.int32),
            VMEM((K, BR * BLK), F32), SPLIT, held_panel(68),
            pltpu.SemaphoreType.DMA((NB // GROUP,)), pltpu.SemaphoreType.DMA((4,)),
        ],
        spaces=[pltpu.HBM] * 5,
        limit=30,
    )
    left_chunk, mr0 = call(left_first, scatter_term(pieces), (panel(17), SMALL), terms=terms)
    left1 = gather(left_chunk, "y")
    back_scratch = [SPLIT, held_panel(72), held_panel(4)]
    own, other = call(backward, (*index, *left1, held), (panel(36), panel(36)), back_scratch, limit=20)
    right_chunk, ml1, right0 = call(
        right_first, (*scatter_doc(own, other), start, mr0), (panel(9), SMALL, panel(8)),
        [VMEM((4, 9, K, BLK), F32)], docs=docs,
    )
    right1 = gather_doc(right_chunk)
    pieces = call(
        forward, (*index, *right1, turned), (panel(17),) * 4, [SPLIT, held_panel(68), held_panel(8)], limit=20
    )
    left2_chunk, mr1, h1 = call(
        left_second, (*scatter_term(pieces), left_chunk, ml1), (panel(17), SMALL, SMALL), terms=terms
    )
    left2 = gather(left2_chunk, "y")
    own, other = call(backward, (*index, *left2, held), (panel(36), panel(36)), back_scratch, limit=20)
    prior = call(
        right_prior, (*right1, start, mr0, mr1, h1), jax.ShapeDtypeStruct((BR, 48, BLK), BF), [held_panel(BR)]
    )
    right2_chunk, ext, ml2, h2 = call(
        right_second, (*scatter_doc(own, other), right_chunk, prior),
        (panel(8), jax.ShapeDtypeStruct((SHARERS, 8, BLK), F32), SMALL, SMALL),
        [VMEM((4, 9, K, BLK), F32)], docs=docs,
    )
    mine = gather(right2_chunk, "x")
    ext, theirs = lax.optimization_barrier((ext, lax.ppermute(right2_chunk, "c", SWAP)))
    ext = lax.all_to_all(ext, ("c", "x", "y", "zh"), 0, 0)
    right2 = mine + [theirs] + [lax.ppermute(m, "c", SWAP) for m in mine[1:]]
    left_out = call(left_result, (*left1, *left2, ml1, ml2, h2), WIDE)
    right_out = call(right_result, (ext, *right2, prior), WIDE, terms=terms)
    return left_out, right_out


def solution(mesh):
    fine = Mesh(np.asarray(mesh.devices).reshape(4, 4, 2, 4, 2), (*DOC, *TERM))
    return jax.shard_map(
        local,
        mesh=fine,
        in_specs=(P(DOC, TERM, None, None), P(DOC, TERM), P(DOC, TERM), P(DOC, TERM), P(None, TERM)),
        out_specs=(P(None, DOC), P(None, TERM)),
        check_vma=False,
    )
```

profile of v0, /device:TPU:1, one launch (start us, length us, event | category | flops | bytes accessed | tf_op | source)
XLA Modules:
  0.0 174.1 jit_solution(497141977435257989)
XLA Ops:
  1.3 1.0 copy-done
  3.7 6.8 %first_forward.1 = (f32[17,16,128]{2,1,0:T(8,128)S(1)}, f32[17,16,128]{2,1,0:T(8,128)S(1)}, f32[17,16,128]{2,1,0:T(8,128)S(1)}, f32[17,16,128]{2,1,0:T(8,128)S(1...) custom-call(s32[1,320]{1,0:T(1,128)S(1)} %copy-done.2, s32[1,320]{1,0:T(1,128)S(1)} %copy-done.3, ...), custom_call_target="tpu_custom_call" | custom-call | flops 2000000000 | bytes 2000000 | tf_op jit(solution)/shard_map/first_forward/pallas_call | solution.py:423
  10.5 2.2 %collective-permute-start = (f32[17,16,128]{2,1,0:T(8,128)S(1)}, f32[17,16,128]{2,1,0:T(8,128)S(1)}, u32[]{:S(2)}, u32[]{:S(2)}) collective-permute-start(f32[17,16,128]{2,1,0:T(8,128)S(1)} %get-tuple-element.30), channel_id=1, source_target_pairs={{0,2},{2,4},{4,6},{6,0},{1,3},{3,5},{5,7},{7,1},{8,10},{10,12},{12... | collective-permute-start | bytes 417800 | tf_op jit(solution)/shard_map/ppermute | solution.py:441
  12.7 2.6 %collective-permute-start.1 = (f32[17,16,128]{2,1,0:T(8,128)S(1)}, f32[17,16,128]{2,1,0:T(8,128)S(1)}, u32[]{:S(2)}, u32[]{:S(2)}) collective-permute-start(f32[17,16,128]{2,1,0:T(8,128)S(1)} %get-tuple-element.31), channel_id=1, source_target_pairs={{0,4},{2,6},{4,0},{6,2},{1,5},{3,7},{5,1},{7,3},{8,12},{10,14},{12... | collective-permute-start | bytes 417800 | tf_op jit(solution)/shard_map/ppermute | solution.py:441
  15.4 2.7 %collective-permute-done = f32[17,16,128]{2,1,0:T(8,128)S(1)} collective-permute-done((f32[17,16,128]{2,1,0:T(8,128)S(1)}, f32[17,16,128]{2,1,0:T(8,128)S(1)}, u32[]{:S(2)}, u32[]{:S(2)}) %collective-permute-start) | collective-permute-done | bytes 139296 | tf_op jit(solution)/shard_map/ppermute | solution.py:441
  18.1 4.2 %collective-permute-done.1 = f32[17,16,128]{2,1,0:T(8,128)S(1)} collective-permute-done((f32[17,16,128]{2,1,0:T(8,128)S(1)}, f32[17,16,128]{2,1,0:T(8,128)S(1)}, u32[]{:S(2)}, u32[]{:S(2)}) %collective-permute-start.1) | collective-permute-done | bytes 139296 | tf_op jit(solution)/shard_map/ppermute | solution.py:441
  22.3 5.5 %collective-permute-start.3 = (f32[17,16,128]{2,1,0:T(8,128)S(1)}, f32[17,16,128]{2,1,0:T(8,128)S(1)}, u32[]{:S(2)}, u32[]{:S(2)}) collective-permute-start(f32[17,16,128]{2,1,0:T(8,128)S(1)} %add_add_fusion.1.mine), channel_id=1, source_target_pairs={{0,1},{1,0},{2,3},{3,2},{4,5},{5,4},{6,7},{7,6},{8,9},{9,8},{10,11... | collective-permute-start | bytes 417800 | tf_op jit(solution)/shard_map/ppermute | solution.py:455
  27.8 2.8 %collective-permute-done.3.theirs = f32[17,16,128]{2,1,0:T(8,128)S(1)} collective-permute-done((f32[17,16,128]{2,1,0:T(8,128)S(1)}, f32[17,16,128]{2,1,0:T(8,128)S(1)}, u32[]{:S(2)}, u32[]{:S(2)}) %collective-permute-start.3) | collective-permute-done | bytes 139296 | tf_op jit(solution)/shard_map/ppermute | solution.py:455
  31.4 2.1 %collective-permute-start.6 = (f32[17,16,128]{2,1,0:T(8,128)S(1)}, f32[17,16,128]{2,1,0:T(8,128)S(1)}, u32[]{:S(2)}, u32[]{:S(2)}) collective-permute-start(f32[17,16,128]{2,1,0:T(8,128)S(1)} %get-tuple-element.33.p0.left_raw.a0), channel_id=1, source_target_pairs={{0,6},{2,0},{4,2},{6,4},{1,7},{3,1},{5,3},{7,5},{8,14},{10,8},{12,... | collective-permute-start | bytes 417800 | tf_op jit(solution)/shard_map/ppermute | solution.py:441
  34.8 2.2 %collective-permute-done.6.p3.a3 = f32[17,16,128]{2,1,0:T(8,128)S(1)} collective-permute-done((f32[17,16,128]{2,1,0:T(8,128)S(1)}, f32[17,16,128]{2,1,0:T(8,128)S(1)}, u32[]{:S(2)}, u32[]{:S(2)}) %collective-permute-start.6) | collective-permute-done | bytes 139296 | tf_op jit(solution)/shard_map/ppermute | solution.py:441
  37.0 2.0 %collective-permute-done.5.p2.a2 = f32[17,16,128]{2,1,0:T(8,128)S(1)} collective-permute-done((f32[17,16,128]{2,1,0:T(8,128)S(1)}, f32[17,16,128]{2,1,0:T(8,128)S(1)}, u32[]{:S(2)}, u32[]{:S(2)}) %collective-permute-start.5) | collective-permute-done | bytes 139296 | tf_op jit(solution)/shard_map/ppermute | solution.py:441
  39.0 1.4 collective-permute-done.4.p1.a1
  40.4 5.1 %backward.2 = (f32[36,16,128]{2,1,0:T(8,128)S(1)}, f32[36,16,128]{2,1,0:T(8,128)S(1)}) custom-call(s32[1,320]{1,0:T(1,128)S(1)} %copy-done.2, s32[1,320]{1,0:T(1,128)S(1)} %copy-done.3, s32[1,1]{1,0:T(1,128)S(6)} %copy.7.counts_any.counts, f32[17,16,128]{2,1,0:T(8,128)S(1)} %get-tuple-element.33.p0.left_raw.a0, ...), custom_call_target="tpu_custom_call" | custom-call | flops 2000000000 | bytes 2000000 | tf_op jit(solution)/shard_map/backward/pallas_call | solution.py:423
  45.5 4.0 %collective-permute-start.7 = (f32[36,16,128]{2,1,0:T(8,128)S(1)}, f32[36,16,128]{2,1,0:T(8,128)S(1)}, u32[]{:S(2)}, u32[]{:S(2)}) collective-permute-start(f32[36,16,128]{2,1,0:T(8,128)S(1)} %get-tuple-element.36), channel_id=1, source_target_pairs={{0,8},{8,0},{1,9},{9,1},{2,10},{10,2},{3,11},{11,3},{4,12},{12,4},... | collective-permute-start | bytes 884744 | tf_op jit(solution)/shard_map/ppermute | solution.py:459
  49.5 1.2 collective-permute-done.7
  51.2 2.3 %collective-permute-start.10 = (f32[9,16,128]{2,1,0:T(8,128)S(1)}, f32[9,16,128]{2,1,0:T(8,128)S(1)}, u32[]{:S(2)}, u32[]{:S(2)}) collective-permute-start(f32[9,16,128]{2,1,0:T(8,128)S(1)} %get-tuple-element.60), channel_id=1, source_target_pairs={{0,48},{16,0},{32,16},{48,32},{1,49},{17,1},{33,17},{49,33},{2,50}... | collective-permute-start | bytes 221192 | tf_op jit(solution)/shard_map/ppermute | solution.py:441
  53.6 1.6 collective-permute-done.8
  55.2 3.0 %collective-permute-done.9 = f32[9,16,128]{2,1,0:T(8,128)S(1)} collective-permute-done((f32[9,16,128]{2,1,0:T(8,128)S(1)}, f32[9,16,128]{2,1,0:T(8,128)S(1)}, u32[]{:S(2)}, u32[]{:S(2)}) %collective-permute-start.9) | collective-permute-done | bytes 73760 | tf_op jit(solution)/shard_map/ppermute | solution.py:441
  58.2 4.6 %collective-permute-start.13 = (f32[9,16,128]{2,1,0:T(8,128)S(1)}, f32[9,16,128]{2,1,0:T(8,128)S(1)}, u32[]{:S(2)}, u32[]{:S(2)}) collective-permute-start(f32[9,16,128]{2,1,0:T(8,128)S(1)} %fusion.5.t0), channel_id=1, source_target_pairs={{0,192},{64,0},{128,64},{192,128},{1,193},{65,1},{129,65},{193,129... | collective-permute-start | bytes 221192 | tf_op jit(solution)/shard_map/ppermute | solution.py:441
  62.8 1.8 %collective-permute-start.12 = (f32[9,16,128]{2,1,0:T(8,128)S(1)}, f32[9,16,128]{2,1,0:T(8,128)S(1)}, u32[]{:S(2)}, u32[]{:S(2)}) collective-permute-start(f32[9,16,128]{2,1,0:T(8,128)S(1)} %fusion.5.t0), channel_id=1, source_target_pairs={{0,128},{64,192},{128,0},{192,64},{1,129},{65,193},{129,1},{193,65... | collective-permute-start | bytes 221192 | tf_op jit(solution)/shard_map/ppermute | solution.py:441
  64.6 1.4 collective-permute-start.11
  66.0 1.1 collective-permute-done.12.t2
  67.0 3.1 %collective-permute-done.11.t1 = f32[9,16,128]{2,1,0:T(8,128)S(1)} collective-permute-done((f32[9,16,128]{2,1,0:T(8,128)S(1)}, f32[9,16,128]{2,1,0:T(8,128)S(1)}, u32[]{:S(2)}, u32[]{:S(2)}) %collective-permute-start.11) | collective-permute-done | bytes 73760 | tf_op jit(solution)/shard_map/ppermute | solution.py:441
  70.1 1.1 right_first.1
  71.2 0.9 collective-permute-start.16
  72.2 1.4 collective-permute-start.15
  73.6 3.6 %collective-permute-start.17 = (f32[9,16,128]{2,1,0:T(8,128)S(1)}, f32[9,16,128]{2,1,0:T(8,128)S(1)}, u32[]{:S(2)}, u32[]{:S(2)}) collective-permute-start(f32[9,16,128]{2,1,0:T(8,128)S(1)} %get-tuple-element.38.r0.right_raw), channel_id=1, source_target_pairs={{0,8},{8,0},{1,9},{9,1},{2,10},{10,2},{3,11},{11,3},{4,12},{12,4},... | collective-permute-start | bytes 221192 | tf_op jit(solution)/shard_map/ppermute | solution.py:467
  77.2 1.3 collective-permute-start.20
  78.6 3.1 %collective-permute-start.19 = (f32[9,16,128]{2,1,0:T(8,128)S(1)}, f32[9,16,128]{2,1,0:T(8,128)S(1)}, u32[]{:S(2)}, u32[]{:S(2)}) collective-permute-start(f32[9,16,128]{2,1,0:T(8,128)S(1)} %collective-permute-done.15.r2), channel_id=1, source_target_pairs={{0,8},{8,0},{1,9},{9,1},{2,10},{10,2},{3,11},{11,3},{4,12},{12,4},... | collective-permute-start | bytes 221192 | tf_op jit(solution)/shard_map/ppermute | solution.py:467
  83.3 5.1 %forward.1 = (f32[17,16,128]{2,1,0:T(8,128)S(1)}, f32[17,16,128]{2,1,0:T(8,128)S(1)}, f32[17,16,128]{2,1,0:T(8,128)S(1)}, f32[17,16,128]{2,1,0:T(8,128)S(1)}) custom-call(s32[1,320]{1,0:T(1,128)S(1)} %copy-done.2, s32[1,320]{1,0:T(1,128)S(1)} %copy-done.3, s32[1,1]{1,0:T(1,128)S(6)} %copy.7.counts_any.counts, ...), custom_call_target="tpu_custom_call" | custom-call | flops 2000000000 | bytes 2000000 | tf_op jit(solution)/shard_map/forward/pallas_call | solution.py:423
  88.4 1.1 collective-permute-start.22
  89.5 1.6 collective-permute-start.23
  91.1 5.6 %collective-permute-done.21 = f32[17,16,128]{2,1,0:T(8,128)S(1)} collective-permute-done((f32[17,16,128]{2,1,0:T(8,128)S(1)}, f32[17,16,128]{2,1,0:T(8,128)S(1)}, u32[]{:S(2)}, u32[]{:S(2)}) %collective-permute-start.21) | collective-permute-done | bytes 139296 | tf_op jit(solution)/shard_map/ppermute | solution.py:441
  97.6 3.8 %collective-permute-start.24 = (f32[17,16,128]{2,1,0:T(8,128)S(1)}, f32[17,16,128]{2,1,0:T(8,128)S(1)}, u32[]{:S(2)}, u32[]{:S(2)}) collective-permute-start(f32[17,16,128]{2,1,0:T(8,128)S(1)} %add_add_fusion.mine), channel_id=1, source_target_pairs={{0,1},{1,0},{2,3},{3,2},{4,5},{5,4},{6,7},{7,6},{8,9},{9,8},{10,11... | collective-permute-start | bytes 417800 | tf_op jit(solution)/shard_map/ppermute | solution.py:455
  101.3 8.1 %collective-permute-done.24.theirs = f32[17,16,128]{2,1,0:T(8,128)S(1)} collective-permute-done((f32[17,16,128]{2,1,0:T(8,128)S(1)}, f32[17,16,128]{2,1,0:T(8,128)S(1)}, u32[]{:S(2)}, u32[]{:S(2)}) %collective-permute-start.24) | collective-permute-done | bytes 139296 | tf_op jit(solution)/shard_map/ppermute | solution.py:455
  109.4 1.3 left_second.1
  110.7 2.9 %collective-permute-start.26 = (f32[17,16,128]{2,1,0:T(8,128)S(1)}, f32[17,16,128]{2,1,0:T(8,128)S(1)}, u32[]{:S(2)}, u32[]{:S(2)}) collective-permute-start(f32[17,16,128]{2,1,0:T(8,128)S(1)} %get-tuple-element.45.p0.b0), channel_id=1, source_target_pairs={{0,4},{2,6},{4,0},{6,2},{1,5},{3,7},{5,1},{7,3},{8,12},{10,14},{12... | collective-permute-start | bytes 417800 | tf_op jit(solution)/shard_map/ppermute | solution.py:441
  113.6 1.7 collective-permute-done.27.p3.b3
  115.3 0.9 collective-permute-done.26.p2.b2
  116.2 2.8 %collective-permute-done.25.p1.b1 = f32[17,16,128]{2,1,0:T(8,128)S(1)} collective-permute-done((f32[17,16,128]{2,1,0:T(8,128)S(1)}, f32[17,16,128]{2,1,0:T(8,128)S(1)}, u32[]{:S(2)}, u32[]{:S(2)}) %collective-permute-start.25) | collective-permute-done | bytes 139296 | tf_op jit(solution)/shard_map/ppermute | solution.py:441
  119.1 5.1 %backward.3 = (f32[36,16,128]{2,1,0:T(8,128)S(1)}, f32[36,16,128]{2,1,0:T(8,128)S(1)}) custom-call(s32[1,320]{1,0:T(1,128)S(1)} %copy-done.2, s32[1,320]{1,0:T(1,128)S(1)} %copy-done.3, s32[1,1]{1,0:T(1,128)S(6)} %copy.7.counts_any.counts, f32[17,16,128]{2,1,0:T(8,128)S(1)} %get-tuple-element.45.p0.b0, f32[17,16,128]{2,1,0:T(8,128)S(1)} %collective-permute-done.25.p1.b1, ...), custom_call_target="tpu_custom_call" | custom-call | flops 2000000000 | bytes 2000000 | tf_op jit(solution)/shard_map/backward/pallas_call | solution.py:423
  124.2 1.3 collective-permute-start.28
  125.5 1.2 collective-permute-done.28
  126.8 2.7 %collective-permute-start.31 = (f32[9,16,128]{2,1,0:T(8,128)S(1)}, f32[9,16,128]{2,1,0:T(8,128)S(1)}, u32[]{:S(2)}, u32[]{:S(2)}) collective-permute-start(f32[9,16,128]{2,1,0:T(8,128)S(1)} %get-tuple-element.57), channel_id=1, source_target_pairs={{0,48},{16,0},{32,16},{48,32},{1,49},{17,1},{33,17},{49,33},{2,50}... | collective-permute-start | bytes 221192 | tf_op jit(solution)/shard_map/ppermute | solution.py:441
  130.1 1.1 collective-permute-done.29
  131.2 1.3 collective-permute-done.31
  132.5 1.7 collective-permute-done.30
  134.2 0.9 collective-permute-start.34
  135.1 1.0 collective-permute-start.33
  136.1 1.4 collective-permute-start.32
  137.5 2.7 %right_prior.1.prior.right1 = bf16[64,48,128]{2,1,0:T(8,128)(2,1)S(1)} custom-call(f32[9,16,128]{2,1,0:T(8,128)S(1)} %get-tuple-element.38.r0.right_raw, f32[9,16,128]{2,1,0:T(8,128)S(1)} %collective-permute-done.14.r1, f32[9,16,128]{2,1,0:T(8,128)S(1)} %collective-permute-done.15.r2, f32[9,16,128]{2,1,0:T(8,128)S(1)} %collective-permute-done.16.r3, ...), custom_call_target="tpu_custom_call" | custom-call | flops 2000000000 | bytes 2000000 | tf_op jit(solution)/shard_map/right_prior/pallas_call | solution.py:423
  140.2 1.4 collective-permute-done.32.t1
  141.7 1.9 %right_second.1 = (f32[8,16,128]{2,1,0:T(8,128)S(1)}, f32[64,8,128]{2,1,0:T(8,128)}, f32[16,128]{1,0:T(8,128)S(1)}, f32[16,128]{1,0:T(8,128)S(1)}) custom-call(f32[9,16,128]{2,1,0:T(8,128)S(1)} %fusion.2.t0, f32[9,16,128]{2,1,0:T(8,128)S(1)} %collective-permute-done.32.t1, f32[9,16,128]{2,1,0:T(8,128)S(1)} %collective-permute-done.33.t2, ...), custom_call_target="tpu_custom_call" | custom-call | flops 2000000000 | bytes 2000000 | tf_op jit(solution)/shard_map/right_second/pallas_call | solution.py:423
  143.5 3.0 %collective-permute-start.35 = (f32[8,16,128]{2,1,0:T(8,128)S(1)}, f32[8,16,128]{2,1,0:T(8,128)S(1)}, u32[]{:S(2)}, u32[]{:S(2)}) collective-permute-start(f32[8,16,128]{2,1,0:T(8,128)S(1)} %get-tuple-element.53.r0), channel_id=1, source_target_pairs={{0,8},{8,0},{1,9},{9,1},{2,10},{10,2},{3,11},{11,3},{4,12},{12,4},... | collective-permute-start | bytes 196616 | tf_op jit(solution)/shard_map/ppermute | solution.py:513
  146.6 0.9 collective-permute-done.35.w0
  147.5 10.2 %all-to-all-start = ((f32[64,8,128]{2,1,0:T(8,128)}), f32[64,8,128]{2,1,0:T(8,128)S(1)}, u32[]{:S(2)}, u32[]{:S(2)}) async-start(f32[64,8,128]{2,1,0:T(8,128)} %get-tuple-element.54), calls=%async_computation | async-start | bytes 524288 | tf_op jit(solution)/shard_map/all_to_all | solution.py:514
  157.6 2.8 %collective-permute-start.38 = (f32[8,16,128]{2,1,0:T(8,128)S(1)}, f32[8,16,128]{2,1,0:T(8,128)S(1)}, u32[]{:S(2)}, u32[]{:S(2)}) collective-permute-start(f32[8,16,128]{2,1,0:T(8,128)S(1)} %get-tuple-element.53.r0), channel_id=1, source_target_pairs={{0,48},{16,0},{32,16},{48,32},{1,49},{17,1},{33,17},{49,33},{2,50}... | collective-permute-start | bytes 196616 | tf_op jit(solution)/shard_map/ppermute | solution.py:441
  161.5 1.1 collective-permute-done.38.r3
  162.6 1.7 collective-permute-start.41
  164.3 1.0 collective-permute-done.37.r2
  165.4 2.1 %collective-permute-start.40 = (f32[8,16,128]{2,1,0:T(8,128)S(1)}, f32[8,16,128]{2,1,0:T(8,128)S(1)}, u32[]{:S(2)}, u32[]{:S(2)}) collective-permute-start(f32[8,16,128]{2,1,0:T(8,128)S(1)} %collective-permute-done.37.r2), channel_id=1, source_target_pairs={{0,8},{8,0},{1,9},{9,1},{2,10},{10,2},{3,11},{11,3},{4,12},{12,4},... | collective-permute-start | bytes 196616 | tf_op jit(solution)/shard_map/ppermute | solution.py:515
  167.6 1.3 collective-permute-start.39
  168.9 2.8 %left_result.1 = f32[16,8192]{1,0:T(8,128)} custom-call(f32[17,16,128]{2,1,0:T(8,128)S(1)} %get-tuple-element.33.p0.left_raw.a0, f32[17,16,128]{2,1,0:T(8,128)S(1)} %collective-permute-done.4.p1.a1, f32[17,16,128]{2,1,0:T(8,128)S(1)} %collective-permute-done.5.p2.a2, f32[17,16,128]{2,1,0:T(8,128)S(1)} %collective-permute-done.6.p3.a3, ...), custom_call_target="tpu_custom_call" | custom-call | flops 2000000000 | bytes 2000000 | tf_op jit(solution)/shard_map/left_result/pallas_call | solution.py:423
  171.7 2.4 %right_result.1 = f32[16,8192]{1,0:T(8,128)} custom-call(f32[64,8,128]{2,1,0:T(8,128)S(1)} %all-to-all-done.ext, f32[8,16,128]{2,1,0:T(8,128)S(1)} %get-tuple-element.53.r0, f32[8,16,128]{2,1,0:T(8,128)S(1)} %collective-permute-done.36.r1, f32[8,16,128]{2,1,0:T(8,128)S(1)} %collective-permute-done.37.r2, f32[8,16,128]{2,1,0:T(8,128)S(1)} %collective-permute-done.38.r3, ...), custom_call_target="tpu_custom_call" | custom-call | flops 2000000000 | bytes 2000000 | tf_op jit(solution)/shard_map/right_result/pallas_call | solution.py:423
  (47 shorter events, 8.8 us)
Async XLA Ops:
  1.3 1.0 copy-start
  2.3 0.7 copy-start.2
  3.0 0.7 copy-start.3
  10.5 59.6 %copy-start.1 = (f32[16,8192]{1,0:T(8,128)S(1)}, f32[16,8192]{1,0:T(8,128)}, u32[]{:S(2)}) copy-start(f32[16,8192]{1,0:T(8,128)} %start.3) | copy-start | bytes 1572868
  10.5 7.5 %collective-permute-start = (f32[17,16,128]{2,1,0:T(8,128)S(1)}, f32[17,16,128]{2,1,0:T(8,128)S(1)}, u32[]{:S(2)}, u32[]{:S(2)}) collective-permute-start(f32[17,16,128]{2,1,0:T(8,128)S(1)} %get-tuple-element.30), channel_id=1, source_target_pairs={{0,2},{2,4},{4,6},{6,0},{1,3},{3,5},{5,7},{7,1},{8,10},{10,12},{12... | collective-permute-start | bytes 417800 | tf_op jit(solution)/shard_map/ppermute | solution.py:441
  12.7 9.5 %collective-permute-start.1 = (f32[17,16,128]{2,1,0:T(8,128)S(1)}, f32[17,16,128]{2,1,0:T(8,128)S(1)}, u32[]{:S(2)}, u32[]{:S(2)}) collective-permute-start(f32[17,16,128]{2,1,0:T(8,128)S(1)} %get-tuple-element.31), channel_id=1, source_target_pairs={{0,4},{2,6},{4,0},{6,2},{1,5},{3,7},{5,1},{7,3},{8,12},{10,14},{12... | collective-permute-start | bytes 417800 | tf_op jit(solution)/shard_map/ppermute | solution.py:441
  15.4 6.9 %collective-permute-start.2 = (f32[17,16,128]{2,1,0:T(8,128)S(1)}, f32[17,16,128]{2,1,0:T(8,128)S(1)}, u32[]{:S(2)}, u32[]{:S(2)}) collective-permute-start(f32[17,16,128]{2,1,0:T(8,128)S(1)} %get-tuple-element.32), channel_id=1, source_target_pairs={{0,6},{2,0},{4,2},{6,4},{1,7},{3,1},{5,3},{7,5},{8,14},{10,8},{12,... | collective-permute-start | bytes 417800 | tf_op jit(solution)/shard_map/ppermute | solution.py:441
  22.3 8.3 %collective-permute-start.3 = (f32[17,16,128]{2,1,0:T(8,128)S(1)}, f32[17,16,128]{2,1,0:T(8,128)S(1)}, u32[]{:S(2)}, u32[]{:S(2)}) collective-permute-start(f32[17,16,128]{2,1,0:T(8,128)S(1)} %add_add_fusion.1.mine), channel_id=1, source_target_pairs={{0,1},{1,0},{2,3},{3,2},{4,5},{5,4},{6,7},{7,6},{8,9},{9,8},{10,11... | collective-permute-start | bytes 417800 | tf_op jit(solution)/shard_map/ppermute | solution.py:455
  31.4 5.6 %collective-permute-start.6 = (f32[17,16,128]{2,1,0:T(8,128)S(1)}, f32[17,16,128]{2,1,0:T(8,128)S(1)}, u32[]{:S(2)}, u32[]{:S(2)}) collective-permute-start(f32[17,16,128]{2,1,0:T(8,128)S(1)} %get-tuple-element.33.p0.left_raw.a0), channel_id=1, source_target_pairs={{0,6},{2,0},{4,2},{6,4},{1,7},{3,1},{5,3},{7,5},{8,14},{10,8},{12,... | collective-permute-start | bytes 417800 | tf_op jit(solution)/shard_map/ppermute | solution.py:441
  33.5 5.5 %collective-permute-start.5 = (f32[17,16,128]{2,1,0:T(8,128)S(1)}, f32[17,16,128]{2,1,0:T(8,128)S(1)}, u32[]{:S(2)}, u32[]{:S(2)}) collective-permute-start(f32[17,16,128]{2,1,0:T(8,128)S(1)} %get-tuple-element.33.p0.left_raw.a0), channel_id=1, source_target_pairs={{0,4},{2,6},{4,0},{6,2},{1,5},{3,7},{5,1},{7,3},{8,12},{10,14},{12... | collective-permute-start | bytes 417800 | tf_op jit(solution)/shard_map/ppermute | solution.py:441
  34.0 6.4 %collective-permute-start.4 = (f32[17,16,128]{2,1,0:T(8,128)S(1)}, f32[17,16,128]{2,1,0:T(8,128)S(1)}, u32[]{:S(2)}, u32[]{:S(2)}) collective-permute-start(f32[17,16,128]{2,1,0:T(8,128)S(1)} %get-tuple-element.33.p0.left_raw.a0), channel_id=1, source_target_pairs={{0,2},{2,4},{4,6},{6,0},{1,3},{3,5},{5,7},{7,1},{8,10},{10,12},{12... | collective-permute-start | bytes 417800 | tf_op jit(solution)/shard_map/ppermute | solution.py:441
  45.5 5.2 %collective-permute-start.7 = (f32[36,16,128]{2,1,0:T(8,128)S(1)}, f32[36,16,128]{2,1,0:T(8,128)S(1)}, u32[]{:S(2)}, u32[]{:S(2)}) collective-permute-start(f32[36,16,128]{2,1,0:T(8,128)S(1)} %get-tuple-element.36), channel_id=1, source_target_pairs={{0,8},{8,0},{1,9},{9,1},{2,10},{10,2},{3,11},{11,3},{4,12},{12,4},... | collective-permute-start | bytes 884744 | tf_op jit(solution)/shard_map/ppermute | solution.py:459
  50.8 4.5 %collective-permute-start.8 = (f32[9,16,128]{2,1,0:T(8,128)S(1)}, f32[9,16,128]{2,1,0:T(8,128)S(1)}, u32[]{:S(2)}, u32[]{:S(2)}) collective-permute-start(f32[9,16,128]{2,1,0:T(8,128)S(1)} %get-tuple-element.59), channel_id=1, source_target_pairs={{0,16},{16,32},{32,48},{48,0},{1,17},{17,33},{33,49},{49,1},{2,18}... | collective-permute-start | bytes 221192 | tf_op jit(solution)/shard_map/ppermute | solution.py:441
  51.2 4.0 %collective-permute-start.10 = (f32[9,16,128]{2,1,0:T(8,128)S(1)}, f32[9,16,128]{2,1,0:T(8,128)S(1)}, u32[]{:S(2)}, u32[]{:S(2)}) collective-permute-start(f32[9,16,128]{2,1,0:T(8,128)S(1)} %get-tuple-element.60), channel_id=1, source_target_pairs={{0,48},{16,0},{32,16},{48,32},{1,49},{17,1},{33,17},{49,33},{2,50}... | collective-permute-start | bytes 221192 | tf_op jit(solution)/shard_map/ppermute | solution.py:441
  53.5 4.7 %collective-permute-start.9 = (f32[9,16,128]{2,1,0:T(8,128)S(1)}, f32[9,16,128]{2,1,0:T(8,128)S(1)}, u32[]{:S(2)}, u32[]{:S(2)}) collective-permute-start(f32[9,16,128]{2,1,0:T(8,128)S(1)} %get-tuple-element.61), channel_id=1, source_target_pairs={{0,32},{16,48},{32,0},{48,16},{1,33},{17,49},{33,1},{49,17},{2,34}... | collective-permute-start | bytes 221192 | tf_op jit(solution)/shard_map/ppermute | solution.py:441
  58.2 7.7 %collective-permute-start.13 = (f32[9,16,128]{2,1,0:T(8,128)S(1)}, f32[9,16,128]{2,1,0:T(8,128)S(1)}, u32[]{:S(2)}, u32[]{:S(2)}) collective-permute-start(f32[9,16,128]{2,1,0:T(8,128)S(1)} %fusion.5.t0), channel_id=1, source_target_pairs={{0,192},{64,0},{128,64},{192,128},{1,193},{65,1},{129,65},{193,129... | collective-permute-start | bytes 221192 | tf_op jit(solution)/shard_map/ppermute | solution.py:441
  62.8 4.2 %collective-permute-start.12 = (f32[9,16,128]{2,1,0:T(8,128)S(1)}, f32[9,16,128]{2,1,0:T(8,128)S(1)}, u32[]{:S(2)}, u32[]{:S(2)}) collective-permute-start(f32[9,16,128]{2,1,0:T(8,128)S(1)} %fusion.5.t0), channel_id=1, source_target_pairs={{0,128},{64,192},{128,0},{192,64},{1,129},{65,193},{129,1},{193,65... | collective-permute-start | bytes 221192 | tf_op jit(solution)/shard_map/ppermute | solution.py:441
  64.6 5.5 %collective-permute-start.11 = (f32[9,16,128]{2,1,0:T(8,128)S(1)}, f32[9,16,128]{2,1,0:T(8,128)S(1)}, u32[]{:S(2)}, u32[]{:S(2)}) collective-permute-start(f32[9,16,128]{2,1,0:T(8,128)S(1)} %fusion.5.t0), channel_id=1, source_target_pairs={{0,64},{64,128},{128,192},{192,0},{1,65},{65,129},{129,193},{193,1... | collective-permute-start | bytes 221192 | tf_op jit(solution)/shard_map/ppermute | solution.py:441
  71.2 6.0 %collective-permute-start.16 = (f32[9,16,128]{2,1,0:T(8,128)S(1)}, f32[9,16,128]{2,1,0:T(8,128)S(1)}, u32[]{:S(2)}, u32[]{:S(2)}) collective-permute-start(f32[9,16,128]{2,1,0:T(8,128)S(1)} %get-tuple-element.38.r0.right_raw), channel_id=1, source_target_pairs={{0,48},{16,0},{32,16},{48,32},{1,49},{17,1},{33,17},{49,33},{2,50}... | collective-permute-start | bytes 221192 | tf_op jit(solution)/shard_map/ppermute | solution.py:441
  72.2 6.4 %collective-permute-start.15 = (f32[9,16,128]{2,1,0:T(8,128)S(1)}, f32[9,16,128]{2,1,0:T(8,128)S(1)}, u32[]{:S(2)}, u32[]{:S(2)}) collective-permute-start(f32[9,16,128]{2,1,0:T(8,128)S(1)} %get-tuple-element.38.r0.right_raw), channel_id=1, source_target_pairs={{0,32},{16,48},{32,0},{48,16},{1,33},{17,49},{33,1},{49,17},{2,34}... | collective-permute-start | bytes 221192 | tf_op jit(solution)/shard_map/ppermute | solution.py:441
  73.6 8.1 %collective-permute-start.14 = (f32[9,16,128]{2,1,0:T(8,128)S(1)}, f32[9,16,128]{2,1,0:T(8,128)S(1)}, u32[]{:S(2)}, u32[]{:S(2)}) collective-permute-start(f32[9,16,128]{2,1,0:T(8,128)S(1)} %get-tuple-element.38.r0.right_raw), channel_id=1, source_target_pairs={{0,16},{16,32},{32,48},{48,0},{1,17},{17,33},{33,49},{49,1},{2,18}... | collective-permute-start | bytes 221192 | tf_op jit(solution)/shard_map/ppermute | solution.py:441
  73.6 8.8 %collective-permute-start.17 = (f32[9,16,128]{2,1,0:T(8,128)S(1)}, f32[9,16,128]{2,1,0:T(8,128)S(1)}, u32[]{:S(2)}, u32[]{:S(2)}) collective-permute-start(f32[9,16,128]{2,1,0:T(8,128)S(1)} %get-tuple-element.38.r0.right_raw), channel_id=1, source_target_pairs={{0,8},{8,0},{1,9},{9,1},{2,10},{10,2},{3,11},{11,3},{4,12},{12,4},... | collective-permute-start | bytes 221192 | tf_op jit(solution)/shard_map/ppermute | solution.py:467
  77.2 5.2 %collective-permute-start.20 = (f32[9,16,128]{2,1,0:T(8,128)S(1)}, f32[9,16,128]{2,1,0:T(8,128)S(1)}, u32[]{:S(2)}, u32[]{:S(2)}) collective-permute-start(f32[9,16,128]{2,1,0:T(8,128)S(1)} %collective-permute-done.16.r3), channel_id=1, source_target_pairs={{0,8},{8,0},{1,9},{9,1},{2,10},{10,2},{3,11},{11,3},{4,12},{12,4},... | collective-permute-start | bytes 221192 | tf_op jit(solution)/shard_map/ppermute | solution.py:467
  78.6 4.0 %collective-permute-start.19 = (f32[9,16,128]{2,1,0:T(8,128)S(1)}, f32[9,16,128]{2,1,0:T(8,128)S(1)}, u32[]{:S(2)}, u32[]{:S(2)}) collective-permute-start(f32[9,16,128]{2,1,0:T(8,128)S(1)} %collective-permute-done.15.r2), channel_id=1, source_target_pairs={{0,8},{8,0},{1,9},{9,1},{2,10},{10,2},{3,11},{11,3},{4,12},{12,4},... | collective-permute-start | bytes 221192 | tf_op jit(solution)/shard_map/ppermute | solution.py:467
  81.6 1.6 collective-permute-start.18
  88.3 8.4 %collective-permute-start.21 = (f32[17,16,128]{2,1,0:T(8,128)S(1)}, f32[17,16,128]{2,1,0:T(8,128)S(1)}, u32[]{:S(2)}, u32[]{:S(2)}) collective-permute-start(f32[17,16,128]{2,1,0:T(8,128)S(1)} %get-tuple-element.41), channel_id=1, source_target_pairs={{0,2},{2,4},{4,6},{6,0},{1,3},{3,5},{5,7},{7,1},{8,10},{10,12},{12... | collective-permute-start | bytes 417800 | tf_op jit(solution)/shard_map/ppermute | solution.py:441
  88.4 8.3 %collective-permute-start.22 = (f32[17,16,128]{2,1,0:T(8,128)S(1)}, f32[17,16,128]{2,1,0:T(8,128)S(1)}, u32[]{:S(2)}, u32[]{:S(2)}) collective-permute-start(f32[17,16,128]{2,1,0:T(8,128)S(1)} %get-tuple-element.42), channel_id=1, source_target_pairs={{0,4},{2,6},{4,0},{6,2},{1,5},{3,7},{5,1},{7,3},{8,12},{10,14},{12... | collective-permute-start | bytes 417800 | tf_op jit(solution)/shard_map/ppermute | solution.py:441
  89.5 8.0 %collective-permute-start.23 = (f32[17,16,128]{2,1,0:T(8,128)S(1)}, f32[17,16,128]{2,1,0:T(8,128)S(1)}, u32[]{:S(2)}, u32[]{:S(2)}) collective-permute-start(f32[17,16,128]{2,1,0:T(8,128)S(1)} %get-tuple-element.43), channel_id=1, source_target_pairs={{0,6},{2,0},{4,2},{6,4},{1,7},{3,1},{5,3},{7,5},{8,14},{10,8},{12,... | collective-permute-start | bytes 417800 | tf_op jit(solution)/shard_map/ppermute | solution.py:441
  97.6 11.8 %collective-permute-start.24 = (f32[17,16,128]{2,1,0:T(8,128)S(1)}, f32[17,16,128]{2,1,0:T(8,128)S(1)}, u32[]{:S(2)}, u32[]{:S(2)}) collective-permute-start(f32[17,16,128]{2,1,0:T(8,128)S(1)} %add_add_fusion.mine), channel_id=1, source_target_pairs={{0,1},{1,0},{2,3},{3,2},{4,5},{5,4},{6,7},{7,6},{8,9},{9,8},{10,11... | collective-permute-start | bytes 417800 | tf_op jit(solution)/shard_map/ppermute | solution.py:455
  110.7 4.7 %collective-permute-start.27 = (f32[17,16,128]{2,1,0:T(8,128)S(1)}, f32[17,16,128]{2,1,0:T(8,128)S(1)}, u32[]{:S(2)}, u32[]{:S(2)}) collective-permute-start(f32[17,16,128]{2,1,0:T(8,128)S(1)} %get-tuple-element.45.p0.b0), channel_id=1, source_target_pairs={{0,6},{2,0},{4,2},{6,4},{1,7},{3,1},{5,3},{7,5},{8,14},{10,8},{12,... | collective-permute-start | bytes 417800 | tf_op jit(solution)/shard_map/ppermute | solution.py:441
  110.7 5.5 %collective-permute-start.26 = (f32[17,16,128]{2,1,0:T(8,128)S(1)}, f32[17,16,128]{2,1,0:T(8,128)S(1)}, u32[]{:S(2)}, u32[]{:S(2)}) collective-permute-start(f32[17,16,128]{2,1,0:T(8,128)S(1)} %get-tuple-element.45.p0.b0), channel_id=1, source_target_pairs={{0,4},{2,6},{4,0},{6,2},{1,5},{3,7},{5,1},{7,3},{8,12},{10,14},{12... | collective-permute-start | bytes 417800 | tf_op jit(solution)/shard_map/ppermute | solution.py:441
  113.6 5.4 %collective-permute-start.25 = (f32[17,16,128]{2,1,0:T(8,128)S(1)}, f32[17,16,128]{2,1,0:T(8,128)S(1)}, u32[]{:S(2)}, u32[]{:S(2)}) collective-permute-start(f32[17,16,128]{2,1,0:T(8,128)S(1)} %get-tuple-element.45.p0.b0), channel_id=1, source_target_pairs={{0,2},{2,4},{4,6},{6,0},{1,3},{3,5},{5,7},{7,1},{8,10},{10,12},{12... | collective-permute-start | bytes 417800 | tf_op jit(solution)/shard_map/ppermute | solution.py:441
  124.2 2.5 %collective-permute-start.28 = (f32[36,16,128]{2,1,0:T(8,128)S(1)}, f32[36,16,128]{2,1,0:T(8,128)S(1)}, u32[]{:S(2)}, u32[]{:S(2)}) collective-permute-start(f32[36,16,128]{2,1,0:T(8,128)S(1)} %get-tuple-element.47), channel_id=1, source_target_pairs={{0,8},{8,0},{1,9},{9,1},{2,10},{10,2},{3,11},{11,3},{4,12},{12,4},... | collective-permute-start | bytes 884744 | tf_op jit(solution)/shard_map/ppermute | solution.py:459
  126.7 4.5 %collective-permute-start.29 = (f32[9,16,128]{2,1,0:T(8,128)S(1)}, f32[9,16,128]{2,1,0:T(8,128)S(1)}, u32[]{:S(2)}, u32[]{:S(2)}) collective-permute-start(f32[9,16,128]{2,1,0:T(8,128)S(1)} %get-tuple-element.56), channel_id=1, source_target_pairs={{0,16},{16,32},{32,48},{48,0},{1,17},{17,33},{33,49},{49,1},{2,18}... | collective-permute-start | bytes 221192 | tf_op jit(solution)/shard_map/ppermute | solution.py:441
  126.8 5.7 %collective-permute-start.31 = (f32[9,16,128]{2,1,0:T(8,128)S(1)}, f32[9,16,128]{2,1,0:T(8,128)S(1)}, u32[]{:S(2)}, u32[]{:S(2)}) collective-permute-start(f32[9,16,128]{2,1,0:T(8,128)S(1)} %get-tuple-element.57), channel_id=1, source_target_pairs={{0,48},{16,0},{32,16},{48,32},{1,49},{17,1},{33,17},{49,33},{2,50}... | collective-permute-start | bytes 221192 | tf_op jit(solution)/shard_map/ppermute | solution.py:441
  129.5 4.7 %collective-permute-start.30 = (f32[9,16,128]{2,1,0:T(8,128)S(1)}, f32[9,16,128]{2,1,0:T(8,128)S(1)}, u32[]{:S(2)}, u32[]{:S(2)}) collective-permute-start(f32[9,16,128]{2,1,0:T(8,128)S(1)} %get-tuple-element.58), channel_id=1, source_target_pairs={{0,32},{16,48},{32,0},{48,16},{1,33},{17,49},{33,1},{49,17},{2,34}... | collective-permute-start | bytes 221192 | tf_op jit(solution)/shard_map/ppermute | solution.py:441
  134.2 6.0 %collective-permute-start.34 = (f32[9,16,128]{2,1,0:T(8,128)S(1)}, f32[9,16,128]{2,1,0:T(8,128)S(1)}, u32[]{:S(2)}, u32[]{:S(2)}) collective-permute-start(f32[9,16,128]{2,1,0:T(8,128)S(1)} %fusion.2.t0), channel_id=1, source_target_pairs={{0,192},{64,0},{128,64},{192,128},{1,193},{65,1},{129,65},{193,129... | collective-permute-start | bytes 221192 | tf_op jit(solution)/shard_map/ppermute | solution.py:441
  135.1 5.1 %collective-permute-start.33 = (f32[9,16,128]{2,1,0:T(8,128)S(1)}, f32[9,16,128]{2,1,0:T(8,128)S(1)}, u32[]{:S(2)}, u32[]{:S(2)}) collective-permute-start(f32[9,16,128]{2,1,0:T(8,128)S(1)} %fusion.2.t0), channel_id=1, source_target_pairs={{0,128},{64,192},{128,0},{192,64},{1,129},{65,193},{129,1},{193,65... | collective-permute-start | bytes 221192 | tf_op jit(solution)/shard_map/ppermute | solution.py:441
  136.1 5.5 %collective-permute-start.32 = (f32[9,16,128]{2,1,0:T(8,128)S(1)}, f32[9,16,128]{2,1,0:T(8,128)S(1)}, u32[]{:S(2)}, u32[]{:S(2)}) collective-permute-start(f32[9,16,128]{2,1,0:T(8,128)S(1)} %fusion.2.t0), channel_id=1, source_target_pairs={{0,64},{64,128},{128,192},{192,0},{1,65},{65,129},{129,193},{193,1... | collective-permute-start | bytes 221192 | tf_op jit(solution)/shard_map/ppermute | solution.py:441
  143.5 3.9 %collective-permute-start.35 = (f32[8,16,128]{2,1,0:T(8,128)S(1)}, f32[8,16,128]{2,1,0:T(8,128)S(1)}, u32[]{:S(2)}, u32[]{:S(2)}) collective-permute-start(f32[8,16,128]{2,1,0:T(8,128)S(1)} %get-tuple-element.53.r0), channel_id=1, source_target_pairs={{0,8},{8,0},{1,9},{9,1},{2,10},{10,2},{3,11},{11,3},{4,12},{12,4},... | collective-permute-start | bytes 196616 | tf_op jit(solution)/shard_map/ppermute | solution.py:513
  147.5 24.3 %all-to-all-start = ((f32[64,8,128]{2,1,0:T(8,128)}), f32[64,8,128]{2,1,0:T(8,128)S(1)}, u32[]{:S(2)}, u32[]{:S(2)}) async-start(f32[64,8,128]{2,1,0:T(8,128)} %get-tuple-element.54), calls=%async_computation | async-start | bytes 524288 | tf_op jit(solution)/shard_map/all_to_all | solution.py:514
  157.6 5.0 %collective-permute-start.38 = (f32[8,16,128]{2,1,0:T(8,128)S(1)}, f32[8,16,128]{2,1,0:T(8,128)S(1)}, u32[]{:S(2)}, u32[]{:S(2)}) collective-permute-start(f32[8,16,128]{2,1,0:T(8,128)S(1)} %get-tuple-element.53.r0), channel_id=1, source_target_pairs={{0,48},{16,0},{32,16},{48,32},{1,49},{17,1},{33,17},{49,33},{2,50}... | collective-permute-start | bytes 196616 | tf_op jit(solution)/shard_map/ppermute | solution.py:441
  160.4 4.9 %collective-permute-start.37 = (f32[8,16,128]{2,1,0:T(8,128)S(1)}, f32[8,16,128]{2,1,0:T(8,128)S(1)}, u32[]{:S(2)}, u32[]{:S(2)}) collective-permute-start(f32[8,16,128]{2,1,0:T(8,128)S(1)} %get-tuple-element.53.r0), channel_id=1, source_target_pairs={{0,32},{16,48},{32,0},{48,16},{1,33},{17,49},{33,1},{49,17},{2,34}... | collective-permute-start | bytes 196616 | tf_op jit(solution)/shard_map/ppermute | solution.py:441
  160.9 6.7 %collective-permute-start.36 = (f32[8,16,128]{2,1,0:T(8,128)S(1)}, f32[8,16,128]{2,1,0:T(8,128)S(1)}, u32[]{:S(2)}, u32[]{:S(2)}) collective-permute-start(f32[8,16,128]{2,1,0:T(8,128)S(1)} %get-tuple-element.53.r0), channel_id=1, source_target_pairs={{0,16},{16,32},{32,48},{48,0},{1,17},{17,33},{33,49},{49,1},{2,18}... | collective-permute-start | bytes 196616 | tf_op jit(solution)/shard_map/ppermute | solution.py:441
  162.6 9.1 %collective-permute-start.41 = (f32[8,16,128]{2,1,0:T(8,128)S(1)}, f32[8,16,128]{2,1,0:T(8,128)S(1)}, u32[]{:S(2)}, u32[]{:S(2)}) collective-permute-start(f32[8,16,128]{2,1,0:T(8,128)S(1)} %collective-permute-done.38.r3), channel_id=1, source_target_pairs={{0,8},{8,0},{1,9},{9,1},{2,10},{10,2},{3,11},{11,3},{4,12},{12,4},... | collective-permute-start | bytes 196616 | tf_op jit(solution)/shard_map/ppermute | solution.py:515
  165.4 6.4 %collective-permute-start.40 = (f32[8,16,128]{2,1,0:T(8,128)S(1)}, f32[8,16,128]{2,1,0:T(8,128)S(1)}, u32[]{:S(2)}, u32[]{:S(2)}) collective-permute-start(f32[8,16,128]{2,1,0:T(8,128)S(1)} %collective-permute-done.37.r2), channel_id=1, source_target_pairs={{0,8},{8,0},{1,9},{9,1},{2,10},{10,2},{3,11},{11,3},{4,12},{12,4},... | collective-permute-start | bytes 196616 | tf_op jit(solution)/shard_map/ppermute | solution.py:515
  167.6 4.2 %collective-permute-start.39 = (f32[8,16,128]{2,1,0:T(8,128)S(1)}, f32[8,16,128]{2,1,0:T(8,128)S(1)}, u32[]{:S(2)}, u32[]{:S(2)}) collective-permute-start(f32[8,16,128]{2,1,0:T(8,128)S(1)} %collective-permute-done.36.r1), channel_id=1, source_target_pairs={{0,8},{8,0},{1,9},{9,1},{2,10},{10,2},{3,11},{11,3},{4,12},{12,4},... | collective-permute-start | bytes 196616 | tf_op jit(solution)/shard_map/ppermute | solution.py:515
where the time goes:
time: 175 us; the launch traced here: 174 us
  starting transfers between devices  79 us (45%)
  waiting for transfers between devices  55.9 us (32%)
  Pallas kernels  35.1 us (20%)
  local copies, waits for them, and re-layouts  2.4 us (1%)
    ppermute x30, waiting for transfers between devices, shift(): return lax.ppermute(value, axis, [(i, (i + k) % 4) for i in range(4)])  40.8 us
    ppermute x30, starting transfers between devices, shift(): return lax.ppermute(value, axis, [(i, (i + k) % 4) for i in range(4)])  37.4 us
    pallas_call x11, Pallas kernels, call(): pl.pallas_call(functools.partial(body, **constants) if constants else bod...  35.1 us
    ppermute x2, waiting for transfers between devices, scatter_term(): return (mine, lax.ppermute(mine, 'zh', SWAP))  10.9 us
    all_to_all x1, starting transfers between devices, local(): ext = lax.all_to_all(ext, ('c', 'x', 'y', 'zh'), 0, 0)  10.2 us
    ppermute x2, starting transfers between devices, scatter_term(): return (mine, lax.ppermute(mine, 'zh', SWAP))  9.27 us
    ppermute x4, starting transfers between devices, gather_doc(): return mine + [lax.ppermute(m, 'c', SWAP) for m in mine]  8.77 us
    ppermute x2, starting transfers between devices, scatter_doc(): got = lax.ppermute(other, 'c', SWAP)  5.29 us
  transfers between devices with their start and end apart: 43, of which 29 were waited for; matrix products, arithmetic and copies ran while one was open for 0% of the time, Pallas kernels for 3%

commit v1 on v0

--- a/solution.py
+++ b/solution.py
@@ -14,7 +14,7 @@
 BR = 64
 NB = 320
 GROUP = 32
-SHARERS = 64
+SHARERS = 8
 DOC = ("zl", "x", "c")
 TERM = ("y", "zh")
 F32 = jnp.float32
@@ -306,7 +306,7 @@
     out[16] = pad_lanes(fold(gram), fold(mixed))
 
 
-def right_second(t0, t1, t2, t3, right_raw, prior, out, ext_out, ml2, h2, order, *, docs):
+def right_second(t0, t1, t2, t3, right_raw, prior, out, ml2, h2, order, *, docs):
     total = zl_total(t0, t1, t2, t3, order)
     first = lax.axis_index("c") * 32 + lax.axis_index("x") * 8
     proj, inverse = projected(total(8), docs)
@@ -324,10 +324,18 @@
         wide = stacked(value)
         gram = gram + cross(wide, wide)
         mixed = mixed + cross(wide, prior[first + i])
-    both = jnp.concatenate([fold(gram), fold(mixed)], axis=1)
-    ext_out[...] = jnp.broadcast_to(
-        jnp.concatenate([both[0:8], both[8:16], jnp.zeros((8, 64), F32)], axis=1)[None], (SHARERS, 8, BLK)
-    )
+    out[8] = pad_lanes(fold(gram), fold(mixed))
+
+
+def gram_copies(r0, r1, r2, r3, w0, w1, w2, w3, ext_out, grams):
+    for base, piece in by_side((r0, r1, r2, r3, w0, w1, w2, w3)):
+        grams[lax.shift_right_logical(base, 3)] = piece[8]
+    total = grams[0]
+    for i in range(1, 8):
+        total = total + grams[i]
+    packed = jnp.concatenate([total[0:8, 0 : 2 * K], total[8:16, 0 : 2 * K], jnp.zeros((8, BLK - 4 * K), F32)], axis=1)
+    for i in range(SHARERS):
+        ext_out[i] = packed
 
 
 def lanes(index):
@@ -504,16 +512,16 @@
     prior = call(
         right_prior, (*right1, start, mr0, mr1, h1), jax.ShapeDtypeStruct((BR, 48, BLK), BF), [held_panel(BR)]
     )
-    right2_chunk, ext, ml2, h2 = call(
-        right_second, (*scatter_doc(own, other), right_chunk, prior),
-        (panel(8), jax.ShapeDtypeStruct((SHARERS, 8, BLK), F32), SMALL, SMALL),
+    right2_chunk, ml2, h2 = call(
+        right_second, (*scatter_doc(own, other), right_chunk, prior), (panel(9), SMALL, SMALL),
         [VMEM((4, 9, K, BLK), F32)], docs=docs,
     )
+    left_out = call(left_result, (*left1, *left2, ml1, ml2, h2), WIDE)
     mine = gather(right2_chunk, "x")
-    ext, theirs = lax.optimization_barrier((ext, lax.ppermute(right2_chunk, "c", SWAP)))
-    ext = lax.all_to_all(ext, ("c", "x", "y", "zh"), 0, 0)
-    right2 = mine + [theirs] + [lax.ppermute(m, "c", SWAP) for m in mine[1:]]
-    left_out = call(left_result, (*left1, *left2, ml1, ml2, h2), WIDE)
+    mine[3], left_out = lax.optimization_barrier((mine[3], left_out))
+    right2 = mine + [lax.ppermute(m, "c", SWAP) for m in mine]
+    ext = call(gram_copies, right2, jax.ShapeDtypeStruct((SHARERS, 8, BLK), F32), [held_panel(8)])
+    ext = lax.all_to_all(ext, TERM, 0, 0)
     right_out = call(right_result, (ext, *right2, prior), WIDE, terms=terms)
     return left_out, right_out
 

time: 175 us -> 173 us (0.989)
  blocking collectives: 0 us -> 12.5 us
  Pallas kernels: 35.1 us -> 22.7 us
    all_to_all x0 -> x1, blocking collectives: none -> 12.5 us  [local(): ext = lax.all_to_all(ext, TERM, 0, 0)]
    pallas_call x11 -> x12, Pallas kernels: 35.1 us -> 22.7 us  [call(): pl.pallas_call(functools.partial(body, **constants) if constants else bod...]
    all_to_all x1 -> x0, starting transfers between devices: 10.2 us -> none  [local(): ext = lax.all_to_all(ext, ('c', 'x', 'y', 'zh'), 0, 0)]
    ppermute x2, starting transfers between devices: 9.27 us -> 18.3 us  [scatter_term(): return (mine, lax.ppermute(mine, 'zh', SWAP))]
    ppermute x2, starting transfers between devices: 5.29 us -> 11.3 us  [scatter_doc(): got = lax.ppermute(other, 'c', SWAP)]
    ppermute x4, starting transfers between devices: 8.15 us -> 5.36 us  [local(): right2 = mine + [lax.ppermute(m, 'c', SWAP) for m in mine]]
    ppermute x30, starting transfers between devices: 37.4 us -> 35.5 us  [shift(): return lax.ppermute(value, axis, [(i, (i + k) % 4) for i in range(4)])]
  transfers between devices with their start and end apart: 43 -> 42, of which waited for: 29 -> 30; matrix products, arithmetic and copies ran while one was open for 0% -> 0% of each run, Pallas kernels for 3% -> 3%
where the time goes in v1:
time: 173 us
  starting transfers between devices  79.5 us (46%)
  waiting for transfers between devices  54.5 us (32%)
  Pallas kernels  22.7 us (13%)
  blocking collectives  12.5 us (7%)
  local copies, waits for them, and re-layouts  2.4 us (1%)
    ppermute x30, waiting for transfers between devices, shift(): return lax.ppermute(value, axis, [(i, (i + k) % 4) for i in range(4)])  39.8 us
    ppermute x30, starting transfers between devices, shift(): return lax.ppermute(value, axis, [(i, (i + k) % 4) for i in range(4)])  35.5 us
    pallas_call x12, Pallas kernels, call(): pl.pallas_call(functools.partial(body, **constants) if constants else bod...  22.7 us
    ppermute x2, starting transfers between devices, scatter_term(): return (mine, lax.ppermute(mine, 'zh', SWAP))  18.3 us
    all_to_all x1, blocking collectives, local(): ext = lax.all_to_all(ext, TERM, 0, 0)  12.5 us
    ppermute x2, starting transfers between devices, scatter_doc(): got = lax.ppermute(other, 'c', SWAP)  11.3 us
    ppermute x2, waiting for transfers between devices, scatter_term(): return (mine, lax.ppermute(mine, 'zh', SWAP))  10.2 us
    ppermute x4, starting transfers between devices, gather_doc(): return mine + [lax.ppermute(m, 'c', SWAP) for m in mine]  8.95 us
  transfers between devices with their start and end apart: 42, of which 30 were waited for; matrix products, arithmetic and copies ran while one was open for 0% of the time, Pallas kernels for 3%

profile of v1, /device:TPU:1, one launch (start us, length us, event | category | flops | bytes accessed | tf_op | source)
XLA Modules:
  0.0 173.3 jit_solution(6075155652903035012)
XLA Ops:
  1.3 1.0 copy-done
  2.3 0.7 copy-done.2
  3.0 0.7 copy-done.3
  3.7 4.2 %first_forward.1 = (f32[17,16,128]{2,1,0:T(8,128)S(1)}, f32[17,16,128]{2,1,0:T(8,128)S(1)}, f32[17,16,128]{2,1,0:T(8,128)S(1)}, f32[17,16,128]{2,1,0:T(8,128)S(1...) custom-call(s32[1,320]{1,0:T(1,128)S(1)} %copy-done.2, s32[1,320]{1,0:T(1,128)S(1)} %copy-done.3, ...), custom_call_target="tpu_custom_call" | custom-call | flops 2000000000 | bytes 2000000 | tf_op jit(solution)/shard_map/first_forward/pallas_call | solution.py:431
  7.9 2.2 %collective-permute-start = (f32[17,16,128]{2,1,0:T(8,128)S(1)}, f32[17,16,128]{2,1,0:T(8,128)S(1)}, u32[]{:S(2)}, u32[]{:S(2)}) collective-permute-start(f32[17,16,128]{2,1,0:T(8,128)S(1)} %get-tuple-element.29), channel_id=1, source_target_pairs={{0,2},{2,4},{4,6},{6,0},{1,3},{3,5},{5,7},{7,1},{8,10},{10,12},{12... | collective-permute-start | bytes 417800 | tf_op jit(solution)/shard_map/ppermute | solution.py:449
  10.1 5.3 %collective-permute-start.1 = (f32[17,16,128]{2,1,0:T(8,128)S(1)}, f32[17,16,128]{2,1,0:T(8,128)S(1)}, u32[]{:S(2)}, u32[]{:S(2)}) collective-permute-start(f32[17,16,128]{2,1,0:T(8,128)S(1)} %get-tuple-element.30), channel_id=1, source_target_pairs={{0,4},{2,6},{4,0},{6,2},{1,5},{3,7},{5,1},{7,3},{8,12},{10,14},{12... | collective-permute-start | bytes 417800 | tf_op jit(solution)/shard_map/ppermute | solution.py:449
  15.4 1.3 collective-permute-done
  16.6 3.9 %collective-permute-done.1 = f32[17,16,128]{2,1,0:T(8,128)S(1)} collective-permute-done((f32[17,16,128]{2,1,0:T(8,128)S(1)}, f32[17,16,128]{2,1,0:T(8,128)S(1)}, u32[]{:S(2)}, u32[]{:S(2)}) %collective-permute-start.1) | collective-permute-done | bytes 139296 | tf_op jit(solution)/shard_map/ppermute | solution.py:449
  20.6 8.0 %collective-permute-start.3 = (f32[17,16,128]{2,1,0:T(8,128)S(1)}, f32[17,16,128]{2,1,0:T(8,128)S(1)}, u32[]{:S(2)}, u32[]{:S(2)}) collective-permute-start(f32[17,16,128]{2,1,0:T(8,128)S(1)} %add_add_fusion.1.mine), channel_id=1, source_target_pairs={{0,1},{1,0},{2,3},{3,2},{4,5},{5,4},{6,7},{7,6},{8,9},{9,8},{10,11... | collective-permute-start | bytes 417800 | tf_op jit(solution)/shard_map/ppermute | solution.py:463
  28.5 3.3 %collective-permute-done.3.theirs = f32[17,16,128]{2,1,0:T(8,128)S(1)} collective-permute-done((f32[17,16,128]{2,1,0:T(8,128)S(1)}, f32[17,16,128]{2,1,0:T(8,128)S(1)}, u32[]{:S(2)}, u32[]{:S(2)}) %collective-permute-start.3) | collective-permute-done | bytes 139296 | tf_op jit(solution)/shard_map/ppermute | solution.py:463
  31.8 0.8 left_first.1
  32.6 1.6 collective-permute-start.6
  34.2 0.8 collective-permute-start.5
  35.1 2.3 %collective-permute-done.6.p3.a3 = f32[17,16,128]{2,1,0:T(8,128)S(1)} collective-permute-done((f32[17,16,128]{2,1,0:T(8,128)S(1)}, f32[17,16,128]{2,1,0:T(8,128)S(1)}, u32[]{:S(2)}, u32[]{:S(2)}) %collective-permute-start.6) | collective-permute-done | bytes 139296 | tf_op jit(solution)/shard_map/ppermute | solution.py:449
  37.4 2.3 %collective-permute-done.5.p2.a2 = f32[17,16,128]{2,1,0:T(8,128)S(1)} collective-permute-done((f32[17,16,128]{2,1,0:T(8,128)S(1)}, f32[17,16,128]{2,1,0:T(8,128)S(1)}, u32[]{:S(2)}, u32[]{:S(2)}) %collective-permute-start.5) | collective-permute-done | bytes 139296 | tf_op jit(solution)/shard_map/ppermute | solution.py:449
  39.7 1.4 collective-permute-done.4.p1.a1
  41.1 2.1 %backward.2 = (f32[36,16,128]{2,1,0:T(8,128)S(1)}, f32[36,16,128]{2,1,0:T(8,128)S(1)}) custom-call(s32[1,320]{1,0:T(1,128)S(1)} %copy-done.2, s32[1,320]{1,0:T(1,128)S(1)} %copy-done.3, s32[1,1]{1,0:T(1,128)S(6)} %copy.7.counts_any.counts, f32[17,16,128]{2,1,0:T(8,128)S(1)} %get-tuple-element.32.p0.left_raw.a0, ...), custom_call_target="tpu_custom_call" | custom-call | flops 2000000000 | bytes 2000000 | tf_op jit(solution)/shard_map/backward/pallas_call | solution.py:431
  43.2 7.3 %collective-permute-start.7 = (f32[36,16,128]{2,1,0:T(8,128)S(1)}, f32[36,16,128]{2,1,0:T(8,128)S(1)}, u32[]{:S(2)}, u32[]{:S(2)}) collective-permute-start(f32[36,16,128]{2,1,0:T(8,128)S(1)} %get-tuple-element.35), channel_id=1, source_target_pairs={{0,8},{8,0},{1,9},{9,1},{2,10},{10,2},{3,11},{11,3},{4,12},{12,4},... | collective-permute-start | bytes 884744 | tf_op jit(solution)/shard_map/ppermute | solution.py:467
  50.5 1.2 collective-permute-done.7
  51.8 2.7 %collective-permute-start.10 = (f32[9,16,128]{2,1,0:T(8,128)S(1)}, f32[9,16,128]{2,1,0:T(8,128)S(1)}, u32[]{:S(2)}, u32[]{:S(2)}) collective-permute-start(f32[9,16,128]{2,1,0:T(8,128)S(1)} %get-tuple-element.58), channel_id=1, source_target_pairs={{0,48},{16,0},{32,16},{48,32},{1,49},{17,1},{33,17},{49,33},{2,50}... | collective-permute-start | bytes 221192 | tf_op jit(solution)/shard_map/ppermute | solution.py:449
  54.5 1.1 collective-permute-start.9
  55.5 0.7 collective-permute-done.8
  56.2 3.0 %collective-permute-done.9 = f32[9,16,128]{2,1,0:T(8,128)S(1)} collective-permute-done((f32[9,16,128]{2,1,0:T(8,128)S(1)}, f32[9,16,128]{2,1,0:T(8,128)S(1)}, u32[]{:S(2)}, u32[]{:S(2)}) %collective-permute-start.9) | collective-permute-done | bytes 73760 | tf_op jit(solution)/shard_map/ppermute | solution.py:449
  59.2 2.3 %collective-permute-start.13 = (f32[9,16,128]{2,1,0:T(8,128)S(1)}, f32[9,16,128]{2,1,0:T(8,128)S(1)}, u32[]{:S(2)}, u32[]{:S(2)}) collective-permute-start(f32[9,16,128]{2,1,0:T(8,128)S(1)} %fusion.5.t0), channel_id=1, source_target_pairs={{0,192},{64,0},{128,64},{192,128},{1,193},{65,1},{129,65},{193,129... | collective-permute-start | bytes 221192 | tf_op jit(solution)/shard_map/ppermute | solution.py:449
  61.6 3.9 %collective-permute-start.12 = (f32[9,16,128]{2,1,0:T(8,128)S(1)}, f32[9,16,128]{2,1,0:T(8,128)S(1)}, u32[]{:S(2)}, u32[]{:S(2)}) collective-permute-start(f32[9,16,128]{2,1,0:T(8,128)S(1)} %fusion.5.t0), channel_id=1, source_target_pairs={{0,128},{64,192},{128,0},{192,64},{1,129},{65,193},{129,1},{193,65... | collective-permute-start | bytes 221192 | tf_op jit(solution)/shard_map/ppermute | solution.py:449
  66.0 2.8 %collective-permute-done.12.t2 = f32[9,16,128]{2,1,0:T(8,128)S(1)} collective-permute-done((f32[9,16,128]{2,1,0:T(8,128)S(1)}, f32[9,16,128]{2,1,0:T(8,128)S(1)}, u32[]{:S(2)}, u32[]{:S(2)}) %collective-permute-start.12) | collective-permute-done | bytes 73760 | tf_op jit(solution)/shard_map/ppermute | solution.py:449
  68.8 2.3 %collective-permute-done.11.t1 = f32[9,16,128]{2,1,0:T(8,128)S(1)} collective-permute-done((f32[9,16,128]{2,1,0:T(8,128)S(1)}, f32[9,16,128]{2,1,0:T(8,128)S(1)}, u32[]{:S(2)}, u32[]{:S(2)}) %collective-permute-start.11) | collective-permute-done | bytes 73760 | tf_op jit(solution)/shard_map/ppermute | solution.py:449
  71.1 1.1 right_first.1
  72.2 1.2 collective-permute-start.16
  74.0 3.4 %collective-permute-start.17 = (f32[9,16,128]{2,1,0:T(8,128)S(1)}, f32[9,16,128]{2,1,0:T(8,128)S(1)}, u32[]{:S(2)}, u32[]{:S(2)}) collective-permute-start(f32[9,16,128]{2,1,0:T(8,128)S(1)} %get-tuple-element.37.r0.right_raw), channel_id=1, source_target_pairs={{0,8},{8,0},{1,9},{9,1},{2,10},{10,2},{3,11},{11,3},{4,12},{12,4},... | collective-permute-start | bytes 221192 | tf_op jit(solution)/shard_map/ppermute | solution.py:475
  77.4 2.3 %collective-permute-start.20 = (f32[9,16,128]{2,1,0:T(8,128)S(1)}, f32[9,16,128]{2,1,0:T(8,128)S(1)}, u32[]{:S(2)}, u32[]{:S(2)}) collective-permute-start(f32[9,16,128]{2,1,0:T(8,128)S(1)} %collective-permute-done.16.r3), channel_id=1, source_target_pairs={{0,8},{8,0},{1,9},{9,1},{2,10},{10,2},{3,11},{11,3},{4,12},{12,4},... | collective-permute-start | bytes 221192 | tf_op jit(solution)/shard_map/ppermute | solution.py:475
  79.7 2.5 %collective-permute-start.19 = (f32[9,16,128]{2,1,0:T(8,128)S(1)}, f32[9,16,128]{2,1,0:T(8,128)S(1)}, u32[]{:S(2)}, u32[]{:S(2)}) collective-permute-start(f32[9,16,128]{2,1,0:T(8,128)S(1)} %collective-permute-done.15.r2), channel_id=1, source_target_pairs={{0,8},{8,0},{1,9},{9,1},{2,10},{10,2},{3,11},{11,3},{4,12},{12,4},... | collective-permute-start | bytes 221192 | tf_op jit(solution)/shard_map/ppermute | solution.py:475
  82.3 0.7 collective-permute-start.18
  83.2 0.7 collective-permute-done.18.w1
  83.9 2.0 %forward.1 = (f32[17,16,128]{2,1,0:T(8,128)S(1)}, f32[17,16,128]{2,1,0:T(8,128)S(1)}, f32[17,16,128]{2,1,0:T(8,128)S(1)}, f32[17,16,128]{2,1,0:T(8,128)S(1)}) custom-call(s32[1,320]{1,0:T(1,128)S(1)} %copy-done.2, s32[1,320]{1,0:T(1,128)S(1)} %copy-done.3, s32[1,1]{1,0:T(1,128)S(6)} %copy.7.counts_any.counts, ...), custom_call_target="tpu_custom_call" | custom-call | flops 2000000000 | bytes 2000000 | tf_op jit(solution)/shard_map/forward/pallas_call | solution.py:431
  86.0 3.4 %collective-permute-start.22 = (f32[17,16,128]{2,1,0:T(8,128)S(1)}, f32[17,16,128]{2,1,0:T(8,128)S(1)}, u32[]{:S(2)}, u32[]{:S(2)}) collective-permute-start(f32[17,16,128]{2,1,0:T(8,128)S(1)} %get-tuple-element.41), channel_id=1, source_target_pairs={{0,4},{2,6},{4,0},{6,2},{1,5},{3,7},{5,1},{7,3},{8,12},{10,14},{12... | collective-permute-start | bytes 417800 | tf_op jit(solution)/shard_map/ppermute | solution.py:449
  89.9 1.3 collective-permute-done.21
  91.1 2.2 %collective-permute-done.22 = f32[17,16,128]{2,1,0:T(8,128)S(1)} collective-permute-done((f32[17,16,128]{2,1,0:T(8,128)S(1)}, f32[17,16,128]{2,1,0:T(8,128)S(1)}, u32[]{:S(2)}, u32[]{:S(2)}) %collective-permute-start.22) | collective-permute-done | bytes 139296 | tf_op jit(solution)/shard_map/ppermute | solution.py:449
  93.4 10.3 %collective-permute-start.24 = (f32[17,16,128]{2,1,0:T(8,128)S(1)}, f32[17,16,128]{2,1,0:T(8,128)S(1)}, u32[]{:S(2)}, u32[]{:S(2)}) collective-permute-start(f32[17,16,128]{2,1,0:T(8,128)S(1)} %add_add_fusion.mine), channel_id=1, source_target_pairs={{0,1},{1,0},{2,3},{3,2},{4,5},{5,4},{6,7},{7,6},{8,9},{9,8},{10,11... | collective-permute-start | bytes 417800 | tf_op jit(solution)/shard_map/ppermute | solution.py:463
  103.8 7.0 %collective-permute-done.24.theirs = f32[17,16,128]{2,1,0:T(8,128)S(1)} collective-permute-done((f32[17,16,128]{2,1,0:T(8,128)S(1)}, f32[17,16,128]{2,1,0:T(8,128)S(1)}, u32[]{:S(2)}, u32[]{:S(2)}) %collective-permute-start.24) | collective-permute-done | bytes 139296 | tf_op jit(solution)/shard_map/ppermute | solution.py:463
  110.8 1.3 left_second.1
  112.1 2.2 %collective-permute-start.27 = (f32[17,16,128]{2,1,0:T(8,128)S(1)}, f32[17,16,128]{2,1,0:T(8,128)S(1)}, u32[]{:S(2)}, u32[]{:S(2)}) collective-permute-start(f32[17,16,128]{2,1,0:T(8,128)S(1)} %get-tuple-element.44.p0.b0), channel_id=1, source_target_pairs={{0,6},{2,0},{4,2},{6,4},{1,7},{3,1},{5,3},{7,5},{8,14},{10,8},{12,... | collective-permute-start | bytes 417800 | tf_op jit(solution)/shard_map/ppermute | solution.py:449
  114.3 0.6 collective-permute-start.26
  115.0 1.8 %collective-permute-done.27.p3.b3 = f32[17,16,128]{2,1,0:T(8,128)S(1)} collective-permute-done((f32[17,16,128]{2,1,0:T(8,128)S(1)}, f32[17,16,128]{2,1,0:T(8,128)S(1)}, u32[]{:S(2)}, u32[]{:S(2)}) %collective-permute-start.27) | collective-permute-done | bytes 139296 | tf_op jit(solution)/shard_map/ppermute | solution.py:449
  116.8 3.0 %collective-permute-done.26.p2.b2 = f32[17,16,128]{2,1,0:T(8,128)S(1)} collective-permute-done((f32[17,16,128]{2,1,0:T(8,128)S(1)}, f32[17,16,128]{2,1,0:T(8,128)S(1)}, u32[]{:S(2)}, u32[]{:S(2)}) %collective-permute-start.26) | collective-permute-done | bytes 139296 | tf_op jit(solution)/shard_map/ppermute | solution.py:449
  119.8 4.1 %collective-permute-done.25.p1.b1 = f32[17,16,128]{2,1,0:T(8,128)S(1)} collective-permute-done((f32[17,16,128]{2,1,0:T(8,128)S(1)}, f32[17,16,128]{2,1,0:T(8,128)S(1)}, u32[]{:S(2)}, u32[]{:S(2)}) %collective-permute-start.25) | collective-permute-done | bytes 139296 | tf_op jit(solution)/shard_map/ppermute | solution.py:449
  123.8 2.1 %backward.3 = (f32[36,16,128]{2,1,0:T(8,128)S(1)}, f32[36,16,128]{2,1,0:T(8,128)S(1)}) custom-call(s32[1,320]{1,0:T(1,128)S(1)} %copy-done.2, s32[1,320]{1,0:T(1,128)S(1)} %copy-done.3, s32[1,1]{1,0:T(1,128)S(6)} %copy.7.counts_any.counts, f32[17,16,128]{2,1,0:T(8,128)S(1)} %get-tuple-element.44.p0.b0, f32[17,16,128]{2,1,0:T(8,128)S(1)} %collective-permute-done.25.p1.b1, ...), custom_call_target="tpu_custom_call" | custom-call | flops 2000000000 | bytes 2000000 | tf_op jit(solution)/shard_map/backward/pallas_call | solution.py:431
  126.0 4.1 %collective-permute-start.28 = (f32[36,16,128]{2,1,0:T(8,128)S(1)}, f32[36,16,128]{2,1,0:T(8,128)S(1)}, u32[]{:S(2)}, u32[]{:S(2)}) collective-permute-start(f32[36,16,128]{2,1,0:T(8,128)S(1)} %get-tuple-element.46), channel_id=1, source_target_pairs={{0,8},{8,0},{1,9},{9,1},{2,10},{10,2},{3,11},{11,3},{4,12},{12,4},... | collective-permute-start | bytes 884744 | tf_op jit(solution)/shard_map/ppermute | solution.py:467
  130.1 1.2 collective-permute-done.28
  131.4 2.7 %collective-permute-start.31 = (f32[9,16,128]{2,1,0:T(8,128)S(1)}, f32[9,16,128]{2,1,0:T(8,128)S(1)}, u32[]{:S(2)}, u32[]{:S(2)}) collective-permute-start(f32[9,16,128]{2,1,0:T(8,128)S(1)} %get-tuple-element.55), channel_id=1, source_target_pairs={{0,48},{16,0},{32,16},{48,32},{1,49},{17,1},{33,17},{49,33},{2,50}... | collective-permute-start | bytes 221192 | tf_op jit(solution)/shard_map/ppermute | solution.py:449
  134.1 1.7 %collective-permute-done.29 = f32[9,16,128]{2,1,0:T(8,128)S(1)} collective-permute-done((f32[9,16,128]{2,1,0:T(8,128)S(1)}, f32[9,16,128]{2,1,0:T(8,128)S(1)}, u32[]{:S(2)}, u32[]{:S(2)}) %collective-permute-start.29) | collective-permute-done | bytes 73760 | tf_op jit(solution)/shard_map/ppermute | solution.py:449
  135.8 1.3 collective-permute-done.31
  137.1 1.7 collective-permute-done.30
  139.0 1.4 collective-permute-start.32
  140.3 2.7 %right_prior.1.prior.right1 = bf16[64,48,128]{2,1,0:T(8,128)(2,1)S(1)} custom-call(f32[9,16,128]{2,1,0:T(8,128)S(1)} %get-tuple-element.37.r0.right_raw, f32[9,16,128]{2,1,0:T(8,128)S(1)} %collective-permute-done.14.r1, f32[9,16,128]{2,1,0:T(8,128)S(1)} %collective-permute-done.15.r2, f32[9,16,128]{2,1,0:T(8,128)S(1)} %collective-permute-done.16.r3, ...), custom_call_target="tpu_custom_call" | custom-call | flops 2000000000 | bytes 2000000 | tf_op jit(solution)/shard_map/right_prior/pallas_call | solution.py:431
  143.1 2.0 %collective-permute-done.32.t1 = f32[9,16,128]{2,1,0:T(8,128)S(1)} collective-permute-done((f32[9,16,128]{2,1,0:T(8,128)S(1)}, f32[9,16,128]{2,1,0:T(8,128)S(1)}, u32[]{:S(2)}, u32[]{:S(2)}) %collective-permute-start.32) | collective-permute-done | bytes 73760 | tf_op jit(solution)/shard_map/ppermute | solution.py:449
  145.0 1.1 right_second.1
  146.1 3.5 %collective-permute-start.38 = (f32[9,16,128]{2,1,0:T(8,128)S(1)}, f32[9,16,128]{2,1,0:T(8,128)S(1)}, u32[]{:S(2)}, u32[]{:S(2)}) collective-permute-start(f32[9,16,128]{2,1,0:T(8,128)S(1)} %get-tuple-element.49.r0), channel_id=1, source_target_pairs={{0,8},{8,0},{1,9},{9,1},{2,10},{10,2},{3,11},{11,3},{4,12},{12,4},... | collective-permute-start | bytes 221192 | tf_op jit(solution)/shard_map/ppermute | solution.py:522
  149.6 2.0 %collective-permute-start.36 = (f32[9,16,128]{2,1,0:T(8,128)S(1)}, f32[9,16,128]{2,1,0:T(8,128)S(1)}, u32[]{:S(2)}, u32[]{:S(2)}) collective-permute-start(f32[9,16,128]{2,1,0:T(8,128)S(1)} %get-tuple-element.49.r0), channel_id=1, source_target_pairs={{0,16},{16,32},{32,48},{48,0},{1,17},{17,33},{33,49},{49,1},{2,18}... | collective-permute-start | bytes 221192 | tf_op jit(solution)/shard_map/ppermute | solution.py:449
  151.6 0.7 collective-permute-start.35
  152.3 2.9 %left_result.1 = f32[16,8192]{1,0:T(8,128)} custom-call(f32[17,16,128]{2,1,0:T(8,128)S(1)} %get-tuple-element.32.p0.left_raw.a0, f32[17,16,128]{2,1,0:T(8,128)S(1)} %collective-permute-done.4.p1.a1, f32[17,16,128]{2,1,0:T(8,128)S(1)} %collective-permute-done.5.p2.a2, f32[17,16,128]{2,1,0:T(8,128)S(1)} %collective-permute-done.6.p3.a3, ...), custom_call_target="tpu_custom_call" | custom-call | flops 2000000000 | bytes 2000000 | tf_op jit(solution)/shard_map/left_result/pallas_call | solution.py:431
  155.2 1.4 collective-permute-start.40
  158.4 12.5 %all_to_all.5.ext = f32[8,8,128]{2,1,0:T(8,128)S(1)} all-to-all(f32[8,8,128]{2,1,0:T(8,128)S(1)} %gram_copies.1), channel_id=1, replica_groups=mesh['zl'=4,'x'=4,'c'=2,'y'=4,'zh'=2] {'y','zh'}, dimensions={0} | all-to-all | bytes 65536 | tf_op jit(solution)/shard_map/all_to_all | solution.py:524
  171.0 2.3 %right_result.1 = f32[16,8192]{1,0:T(8,128)} custom-call(f32[8,8,128]{2,1,0:T(8,128)S(1)} %all_to_all.5.ext, f32[9,16,128]{2,1,0:T(8,128)S(1)} %get-tuple-element.49.r0, f32[9,16,128]{2,1,0:T(8,128)S(1)} %collective-permute-done.36.r1, f32[9,16,128]{2,1,0:T(8,128)S(1)} %collective-permute-done.37.r2, f32[9,16,128]{2,1,0:T(8,128)S(1)} %collective-permute-done.35.r3, ...), custom_call_target="tpu_custom_call" | custom-call | flops 2000000000 | bytes 2000000 | tf_op jit(solution)/shard_map/right_result/pallas_call | solution.py:431
  (47 shorter events, 4.5 us)
Async XLA Ops:
  1.3 1.0 copy-start
  2.3 0.7 copy-start.2
  3.0 0.7 copy-start.3
  7.9 63.2 %copy-start.1 = (f32[16,8192]{1,0:T(8,128)S(1)}, f32[16,8192]{1,0:T(8,128)}, u32[]{:S(2)}) copy-start(f32[16,8192]{1,0:T(8,128)} %start.3) | copy-start | bytes 1572868
  7.9 8.7 %collective-permute-start = (f32[17,16,128]{2,1,0:T(8,128)S(1)}, f32[17,16,128]{2,1,0:T(8,128)S(1)}, u32[]{:S(2)}, u32[]{:S(2)}) collective-permute-start(f32[17,16,128]{2,1,0:T(8,128)S(1)} %get-tuple-element.29), channel_id=1, source_target_pairs={{0,2},{2,4},{4,6},{6,0},{1,3},{3,5},{5,7},{7,1},{8,10},{10,12},{12... | collective-permute-start | bytes 417800 | tf_op jit(solution)/shard_map/ppermute | solution.py:449
  10.1 10.4 %collective-permute-start.1 = (f32[17,16,128]{2,1,0:T(8,128)S(1)}, f32[17,16,128]{2,1,0:T(8,128)S(1)}, u32[]{:S(2)}, u32[]{:S(2)}) collective-permute-start(f32[17,16,128]{2,1,0:T(8,128)S(1)} %get-tuple-element.30), channel_id=1, source_target_pairs={{0,4},{2,6},{4,0},{6,2},{1,5},{3,7},{5,1},{7,3},{8,12},{10,14},{12... | collective-permute-start | bytes 417800 | tf_op jit(solution)/shard_map/ppermute | solution.py:449
  15.4 5.2 %collective-permute-start.2 = (f32[17,16,128]{2,1,0:T(8,128)S(1)}, f32[17,16,128]{2,1,0:T(8,128)S(1)}, u32[]{:S(2)}, u32[]{:S(2)}) collective-permute-start(f32[17,16,128]{2,1,0:T(8,128)S(1)} %get-tuple-element.31), channel_id=1, source_target_pairs={{0,6},{2,0},{4,2},{6,4},{1,7},{3,1},{5,3},{7,5},{8,14},{10,8},{12,... | collective-permute-start | bytes 417800 | tf_op jit(solution)/shard_map/ppermute | solution.py:449
  20.6 11.2 %collective-permute-start.3 = (f32[17,16,128]{2,1,0:T(8,128)S(1)}, f32[17,16,128]{2,1,0:T(8,128)S(1)}, u32[]{:S(2)}, u32[]{:S(2)}) collective-permute-start(f32[17,16,128]{2,1,0:T(8,128)S(1)} %add_add_fusion.1.mine), channel_id=1, source_target_pairs={{0,1},{1,0},{2,3},{3,2},{4,5},{5,4},{6,7},{7,6},{8,9},{9,8},{10,11... | collective-permute-start | bytes 417800 | tf_op jit(solution)/shard_map/ppermute | solution.py:463
  32.6 4.8 %collective-permute-start.6 = (f32[17,16,128]{2,1,0:T(8,128)S(1)}, f32[17,16,128]{2,1,0:T(8,128)S(1)}, u32[]{:S(2)}, u32[]{:S(2)}) collective-permute-start(f32[17,16,128]{2,1,0:T(8,128)S(1)} %get-tuple-element.32.p0.left_raw.a0), channel_id=1, source_target_pairs={{0,6},{2,0},{4,2},{6,4},{1,7},{3,1},{5,3},{7,5},{8,14},{10,8},{12,... | collective-permute-start | bytes 417800 | tf_op jit(solution)/shard_map/ppermute | solution.py:449
  34.2 5.5 %collective-permute-start.5 = (f32[17,16,128]{2,1,0:T(8,128)S(1)}, f32[17,16,128]{2,1,0:T(8,128)S(1)}, u32[]{:S(2)}, u32[]{:S(2)}) collective-permute-start(f32[17,16,128]{2,1,0:T(8,128)S(1)} %get-tuple-element.32.p0.left_raw.a0), channel_id=1, source_target_pairs={{0,4},{2,6},{4,0},{6,2},{1,5},{3,7},{5,1},{7,3},{8,12},{10,14},{12... | collective-permute-start | bytes 417800 | tf_op jit(solution)/shard_map/ppermute | solution.py:449
  35.0 6.1 %collective-permute-start.4 = (f32[17,16,128]{2,1,0:T(8,128)S(1)}, f32[17,16,128]{2,1,0:T(8,128)S(1)}, u32[]{:S(2)}, u32[]{:S(2)}) collective-permute-start(f32[17,16,128]{2,1,0:T(8,128)S(1)} %get-tuple-element.32.p0.left_raw.a0), channel_id=1, source_target_pairs={{0,2},{2,4},{4,6},{6,0},{1,3},{3,5},{5,7},{7,1},{8,10},{10,12},{12... | collective-permute-start | bytes 417800 | tf_op jit(solution)/shard_map/ppermute | solution.py:449
  43.2 8.5 %collective-permute-start.7 = (f32[36,16,128]{2,1,0:T(8,128)S(1)}, f32[36,16,128]{2,1,0:T(8,128)S(1)}, u32[]{:S(2)}, u32[]{:S(2)}) collective-permute-start(f32[36,16,128]{2,1,0:T(8,128)S(1)} %get-tuple-element.35), channel_id=1, source_target_pairs={{0,8},{8,0},{1,9},{9,1},{2,10},{10,2},{3,11},{11,3},{4,12},{12,4},... | collective-permute-start | bytes 884744 | tf_op jit(solution)/shard_map/ppermute | solution.py:467
  51.7 4.5 %collective-permute-start.8 = (f32[9,16,128]{2,1,0:T(8,128)S(1)}, f32[9,16,128]{2,1,0:T(8,128)S(1)}, u32[]{:S(2)}, u32[]{:S(2)}) collective-permute-start(f32[9,16,128]{2,1,0:T(8,128)S(1)} %get-tuple-element.57), channel_id=1, source_target_pairs={{0,16},{16,32},{32,48},{48,0},{1,17},{17,33},{33,49},{49,1},{2,18}... | collective-permute-start | bytes 221192 | tf_op jit(solution)/shard_map/ppermute | solution.py:449
  51.8 4.4 %collective-permute-start.10 = (f32[9,16,128]{2,1,0:T(8,128)S(1)}, f32[9,16,128]{2,1,0:T(8,128)S(1)}, u32[]{:S(2)}, u32[]{:S(2)}) collective-permute-start(f32[9,16,128]{2,1,0:T(8,128)S(1)} %get-tuple-element.58), channel_id=1, source_target_pairs={{0,48},{16,0},{32,16},{48,32},{1,49},{17,1},{33,17},{49,33},{2,50}... | collective-permute-start | bytes 221192 | tf_op jit(solution)/shard_map/ppermute | solution.py:449
  54.5 4.7 %collective-permute-start.9 = (f32[9,16,128]{2,1,0:T(8,128)S(1)}, f32[9,16,128]{2,1,0:T(8,128)S(1)}, u32[]{:S(2)}, u32[]{:S(2)}) collective-permute-start(f32[9,16,128]{2,1,0:T(8,128)S(1)} %get-tuple-element.59), channel_id=1, source_target_pairs={{0,32},{16,48},{32,0},{48,16},{1,33},{17,49},{33,1},{49,17},{2,34}... | collective-permute-start | bytes 221192 | tf_op jit(solution)/shard_map/ppermute | solution.py:449
  59.2 6.8 %collective-permute-start.13 = (f32[9,16,128]{2,1,0:T(8,128)S(1)}, f32[9,16,128]{2,1,0:T(8,128)S(1)}, u32[]{:S(2)}, u32[]{:S(2)}) collective-permute-start(f32[9,16,128]{2,1,0:T(8,128)S(1)} %fusion.5.t0), channel_id=1, source_target_pairs={{0,192},{64,0},{128,64},{192,128},{1,193},{65,1},{129,65},{193,129... | collective-permute-start | bytes 221192 | tf_op jit(solution)/shard_map/ppermute | solution.py:449
  61.6 7.2 %collective-permute-start.12 = (f32[9,16,128]{2,1,0:T(8,128)S(1)}, f32[9,16,128]{2,1,0:T(8,128)S(1)}, u32[]{:S(2)}, u32[]{:S(2)}) collective-permute-start(f32[9,16,128]{2,1,0:T(8,128)S(1)} %fusion.5.t0), channel_id=1, source_target_pairs={{0,128},{64,192},{128,0},{192,64},{1,129},{65,193},{129,1},{193,65... | collective-permute-start | bytes 221192 | tf_op jit(solution)/shard_map/ppermute | solution.py:449
  65.5 5.6 %collective-permute-start.11 = (f32[9,16,128]{2,1,0:T(8,128)S(1)}, f32[9,16,128]{2,1,0:T(8,128)S(1)}, u32[]{:S(2)}, u32[]{:S(2)}) collective-permute-start(f32[9,16,128]{2,1,0:T(8,128)S(1)} %fusion.5.t0), channel_id=1, source_target_pairs={{0,64},{64,128},{128,192},{192,0},{1,65},{65,129},{129,193},{193,1... | collective-permute-start | bytes 221192 | tf_op jit(solution)/shard_map/ppermute | solution.py:449
  72.2 5.2 %collective-permute-start.16 = (f32[9,16,128]{2,1,0:T(8,128)S(1)}, f32[9,16,128]{2,1,0:T(8,128)S(1)}, u32[]{:S(2)}, u32[]{:S(2)}) collective-permute-start(f32[9,16,128]{2,1,0:T(8,128)S(1)} %get-tuple-element.37.r0.right_raw), channel_id=1, source_target_pairs={{0,48},{16,0},{32,16},{48,32},{1,49},{17,1},{33,17},{49,33},{2,50}... | collective-permute-start | bytes 221192 | tf_op jit(solution)/shard_map/ppermute | solution.py:449
  73.4 6.4 %collective-permute-start.15 = (f32[9,16,128]{2,1,0:T(8,128)S(1)}, f32[9,16,128]{2,1,0:T(8,128)S(1)}, u32[]{:S(2)}, u32[]{:S(2)}) collective-permute-start(f32[9,16,128]{2,1,0:T(8,128)S(1)} %get-tuple-element.37.r0.right_raw), channel_id=1, source_target_pairs={{0,32},{16,48},{32,0},{48,16},{1,33},{17,49},{33,1},{49,17},{2,34}... | collective-permute-start | bytes 221192 | tf_op jit(solution)/shard_map/ppermute | solution.py:449
  73.6 8.7 %collective-permute-start.14 = (f32[9,16,128]{2,1,0:T(8,128)S(1)}, f32[9,16,128]{2,1,0:T(8,128)S(1)}, u32[]{:S(2)}, u32[]{:S(2)}) collective-permute-start(f32[9,16,128]{2,1,0:T(8,128)S(1)} %get-tuple-element.37.r0.right_raw), channel_id=1, source_target_pairs={{0,16},{16,32},{32,48},{48,0},{1,17},{17,33},{33,49},{49,1},{2,18}... | collective-permute-start | bytes 221192 | tf_op jit(solution)/shard_map/ppermute | solution.py:449
  74.0 9.0 %collective-permute-start.17 = (f32[9,16,128]{2,1,0:T(8,128)S(1)}, f32[9,16,128]{2,1,0:T(8,128)S(1)}, u32[]{:S(2)}, u32[]{:S(2)}) collective-permute-start(f32[9,16,128]{2,1,0:T(8,128)S(1)} %get-tuple-element.37.r0.right_raw), channel_id=1, source_target_pairs={{0,8},{8,0},{1,9},{9,1},{2,10},{10,2},{3,11},{11,3},{4,12},{12,4},... | collective-permute-start | bytes 221192 | tf_op jit(solution)/shard_map/ppermute | solution.py:475
  77.4 5.6 %collective-permute-start.20 = (f32[9,16,128]{2,1,0:T(8,128)S(1)}, f32[9,16,128]{2,1,0:T(8,128)S(1)}, u32[]{:S(2)}, u32[]{:S(2)}) collective-permute-start(f32[9,16,128]{2,1,0:T(8,128)S(1)} %collective-permute-done.16.r3), channel_id=1, source_target_pairs={{0,8},{8,0},{1,9},{9,1},{2,10},{10,2},{3,11},{11,3},{4,12},{12,4},... | collective-permute-start | bytes 221192 | tf_op jit(solution)/shard_map/ppermute | solution.py:475
  79.7 3.4 %collective-permute-start.19 = (f32[9,16,128]{2,1,0:T(8,128)S(1)}, f32[9,16,128]{2,1,0:T(8,128)S(1)}, u32[]{:S(2)}, u32[]{:S(2)}) collective-permute-start(f32[9,16,128]{2,1,0:T(8,128)S(1)} %collective-permute-done.15.r2), channel_id=1, source_target_pairs={{0,8},{8,0},{1,9},{9,1},{2,10},{10,2},{3,11},{11,3},{4,12},{12,4},... | collective-permute-start | bytes 221192 | tf_op jit(solution)/shard_map/ppermute | solution.py:475
  82.3 1.6 collective-permute-start.18
  86.0 5.2 %collective-permute-start.21 = (f32[17,16,128]{2,1,0:T(8,128)S(1)}, f32[17,16,128]{2,1,0:T(8,128)S(1)}, u32[]{:S(2)}, u32[]{:S(2)}) collective-permute-start(f32[17,16,128]{2,1,0:T(8,128)S(1)} %get-tuple-element.40), channel_id=1, source_target_pairs={{0,2},{2,4},{4,6},{6,0},{1,3},{3,5},{5,7},{7,1},{8,10},{10,12},{12... | collective-permute-start | bytes 417800 | tf_op jit(solution)/shard_map/ppermute | solution.py:449
  86.0 7.3 %collective-permute-start.22 = (f32[17,16,128]{2,1,0:T(8,128)S(1)}, f32[17,16,128]{2,1,0:T(8,128)S(1)}, u32[]{:S(2)}, u32[]{:S(2)}) collective-permute-start(f32[17,16,128]{2,1,0:T(8,128)S(1)} %get-tuple-element.41), channel_id=1, source_target_pairs={{0,4},{2,6},{4,0},{6,2},{1,5},{3,7},{5,1},{7,3},{8,12},{10,14},{12... | collective-permute-start | bytes 417800 | tf_op jit(solution)/shard_map/ppermute | solution.py:449
  89.5 3.9 %collective-permute-start.23 = (f32[17,16,128]{2,1,0:T(8,128)S(1)}, f32[17,16,128]{2,1,0:T(8,128)S(1)}, u32[]{:S(2)}, u32[]{:S(2)}) collective-permute-start(f32[17,16,128]{2,1,0:T(8,128)S(1)} %get-tuple-element.42), channel_id=1, source_target_pairs={{0,6},{2,0},{4,2},{6,4},{1,7},{3,1},{5,3},{7,5},{8,14},{10,8},{12,... | collective-permute-start | bytes 417800 | tf_op jit(solution)/shard_map/ppermute | solution.py:449
  93.4 17.3 %collective-permute-start.24 = (f32[17,16,128]{2,1,0:T(8,128)S(1)}, f32[17,16,128]{2,1,0:T(8,128)S(1)}, u32[]{:S(2)}, u32[]{:S(2)}) collective-permute-start(f32[17,16,128]{2,1,0:T(8,128)S(1)} %add_add_fusion.mine), channel_id=1, source_target_pairs={{0,1},{1,0},{2,3},{3,2},{4,5},{5,4},{6,7},{7,6},{8,9},{9,8},{10,11... | collective-permute-start | bytes 417800 | tf_op jit(solution)/shard_map/ppermute | solution.py:463
  112.1 4.7 %collective-permute-start.27 = (f32[17,16,128]{2,1,0:T(8,128)S(1)}, f32[17,16,128]{2,1,0:T(8,128)S(1)}, u32[]{:S(2)}, u32[]{:S(2)}) collective-permute-start(f32[17,16,128]{2,1,0:T(8,128)S(1)} %get-tuple-element.44.p0.b0), channel_id=1, source_target_pairs={{0,6},{2,0},{4,2},{6,4},{1,7},{3,1},{5,3},{7,5},{8,14},{10,8},{12,... | collective-permute-start | bytes 417800 | tf_op jit(solution)/shard_map/ppermute | solution.py:449
  114.3 5.5 %collective-permute-start.26 = (f32[17,16,128]{2,1,0:T(8,128)S(1)}, f32[17,16,128]{2,1,0:T(8,128)S(1)}, u32[]{:S(2)}, u32[]{:S(2)}) collective-permute-start(f32[17,16,128]{2,1,0:T(8,128)S(1)} %get-tuple-element.44.p0.b0), channel_id=1, source_target_pairs={{0,4},{2,6},{4,0},{6,2},{1,5},{3,7},{5,1},{7,3},{8,12},{10,14},{12... | collective-permute-start | bytes 417800 | tf_op jit(solution)/shard_map/ppermute | solution.py:449
  114.9 9.0 %collective-permute-start.25 = (f32[17,16,128]{2,1,0:T(8,128)S(1)}, f32[17,16,128]{2,1,0:T(8,128)S(1)}, u32[]{:S(2)}, u32[]{:S(2)}) collective-permute-start(f32[17,16,128]{2,1,0:T(8,128)S(1)} %get-tuple-element.44.p0.b0), channel_id=1, source_target_pairs={{0,2},{2,4},{4,6},{6,0},{1,3},{3,5},{5,7},{7,1},{8,10},{10,12},{12... | collective-permute-start | bytes 417800 | tf_op jit(solution)/shard_map/ppermute | solution.py:449
  126.0 5.3 %collective-permute-start.28 = (f32[36,16,128]{2,1,0:T(8,128)S(1)}, f32[36,16,128]{2,1,0:T(8,128)S(1)}, u32[]{:S(2)}, u32[]{:S(2)}) collective-permute-start(f32[36,16,128]{2,1,0:T(8,128)S(1)} %get-tuple-element.46), channel_id=1, source_target_pairs={{0,8},{8,0},{1,9},{9,1},{2,10},{10,2},{3,11},{11,3},{4,12},{12,4},... | collective-permute-start | bytes 884744 | tf_op jit(solution)/shard_map/ppermute | solution.py:467
  131.3 4.5 %collective-permute-start.29 = (f32[9,16,128]{2,1,0:T(8,128)S(1)}, f32[9,16,128]{2,1,0:T(8,128)S(1)}, u32[]{:S(2)}, u32[]{:S(2)}) collective-permute-start(f32[9,16,128]{2,1,0:T(8,128)S(1)} %get-tuple-element.54), channel_id=1, source_target_pairs={{0,16},{16,32},{32,48},{48,0},{1,17},{17,33},{33,49},{49,1},{2,18}... | collective-permute-start | bytes 221192 | tf_op jit(solution)/shard_map/ppermute | solution.py:449
  131.4 5.7 %collective-permute-start.31 = (f32[9,16,128]{2,1,0:T(8,128)S(1)}, f32[9,16,128]{2,1,0:T(8,128)S(1)}, u32[]{:S(2)}, u32[]{:S(2)}) collective-permute-start(f32[9,16,128]{2,1,0:T(8,128)S(1)} %get-tuple-element.55), channel_id=1, source_target_pairs={{0,48},{16,0},{32,16},{48,32},{1,49},{17,1},{33,17},{49,33},{2,50}... | collective-permute-start | bytes 221192 | tf_op jit(solution)/shard_map/ppermute | solution.py:449
  134.0 4.7 %collective-permute-start.30 = (f32[9,16,128]{2,1,0:T(8,128)S(1)}, f32[9,16,128]{2,1,0:T(8,128)S(1)}, u32[]{:S(2)}, u32[]{:S(2)}) collective-permute-start(f32[9,16,128]{2,1,0:T(8,128)S(1)} %get-tuple-element.56), channel_id=1, source_target_pairs={{0,32},{16,48},{32,0},{48,16},{1,33},{17,49},{33,1},{49,17},{2,34}... | collective-permute-start | bytes 221192 | tf_op jit(solution)/shard_map/ppermute | solution.py:449
  138.8 4.2 %collective-permute-start.34 = (f32[9,16,128]{2,1,0:T(8,128)S(1)}, f32[9,16,128]{2,1,0:T(8,128)S(1)}, u32[]{:S(2)}, u32[]{:S(2)}) collective-permute-start(f32[9,16,128]{2,1,0:T(8,128)S(1)} %fusion.2.t0), channel_id=1, source_target_pairs={{0,192},{64,0},{128,64},{192,128},{1,193},{65,1},{129,65},{193,129... | collective-permute-start | bytes 221192 | tf_op jit(solution)/shard_map/ppermute | solution.py:449
  138.9 4.2 %collective-permute-start.33 = (f32[9,16,128]{2,1,0:T(8,128)S(1)}, f32[9,16,128]{2,1,0:T(8,128)S(1)}, u32[]{:S(2)}, u32[]{:S(2)}) collective-permute-start(f32[9,16,128]{2,1,0:T(8,128)S(1)} %fusion.2.t0), channel_id=1, source_target_pairs={{0,128},{64,192},{128,0},{192,64},{1,129},{65,193},{129,1},{193,65... | collective-permute-start | bytes 221192 | tf_op jit(solution)/shard_map/ppermute | solution.py:449
  139.0 6.1 %collective-permute-start.32 = (f32[9,16,128]{2,1,0:T(8,128)S(1)}, f32[9,16,128]{2,1,0:T(8,128)S(1)}, u32[]{:S(2)}, u32[]{:S(2)}) collective-permute-start(f32[9,16,128]{2,1,0:T(8,128)S(1)} %fusion.2.t0), channel_id=1, source_target_pairs={{0,64},{64,128},{128,192},{192,0},{1,65},{65,129},{129,193},{193,1... | collective-permute-start | bytes 221192 | tf_op jit(solution)/shard_map/ppermute | solution.py:449
  146.1 11.0 %collective-permute-start.38 = (f32[9,16,128]{2,1,0:T(8,128)S(1)}, f32[9,16,128]{2,1,0:T(8,128)S(1)}, u32[]{:S(2)}, u32[]{:S(2)}) collective-permute-start(f32[9,16,128]{2,1,0:T(8,128)S(1)} %get-tuple-element.49.r0), channel_id=1, source_target_pairs={{0,8},{8,0},{1,9},{9,1},{2,10},{10,2},{3,11},{11,3},{4,12},{12,4},... | collective-permute-start | bytes 221192 | tf_op jit(solution)/shard_map/ppermute | solution.py:522
  149.6 5.6 %collective-permute-start.37 = (f32[9,16,128]{2,1,0:T(8,128)S(1)}, f32[9,16,128]{2,1,0:T(8,128)S(1)}, u32[]{:S(2)}, u32[]{:S(2)}) collective-permute-start(f32[9,16,128]{2,1,0:T(8,128)S(1)} %get-tuple-element.49.r0), channel_id=1, source_target_pairs={{0,32},{16,48},{32,0},{48,16},{1,33},{17,49},{33,1},{49,17},{2,34}... | collective-permute-start | bytes 221192 | tf_op jit(solution)/shard_map/ppermute | solution.py:449
  149.6 7.0 %collective-permute-start.36 = (f32[9,16,128]{2,1,0:T(8,128)S(1)}, f32[9,16,128]{2,1,0:T(8,128)S(1)}, u32[]{:S(2)}, u32[]{:S(2)}) collective-permute-start(f32[9,16,128]{2,1,0:T(8,128)S(1)} %get-tuple-element.49.r0), channel_id=1, source_target_pairs={{0,16},{16,32},{32,48},{48,0},{1,17},{17,33},{33,49},{49,1},{2,18}... | collective-permute-start | bytes 221192 | tf_op jit(solution)/shard_map/ppermute | solution.py:449
  151.6 3.6 %collective-permute-start.35 = (f32[9,16,128]{2,1,0:T(8,128)S(1)}, f32[9,16,128]{2,1,0:T(8,128)S(1)}, u32[]{:S(2)}, u32[]{:S(2)}) collective-permute-start(f32[9,16,128]{2,1,0:T(8,128)S(1)} %get-tuple-element.49.r0), channel_id=1, source_target_pairs={{0,48},{16,0},{32,16},{48,32},{1,49},{17,1},{33,17},{49,33},{2,50}... | collective-permute-start | bytes 221192 | tf_op jit(solution)/shard_map/ppermute | solution.py:449
  155.2 2.3 %collective-permute-start.40 = (f32[9,16,128]{2,1,0:T(8,128)S(1)}, f32[9,16,128]{2,1,0:T(8,128)S(1)}, u32[]{:S(2)}, u32[]{:S(2)}) collective-permute-start(f32[9,16,128]{2,1,0:T(8,128)S(1)} %collective-permute-done.37.r2), channel_id=1, source_target_pairs={{0,8},{8,0},{1,9},{9,1},{2,10},{10,2},{3,11},{11,3},{4,12},{12,4},... | collective-permute-start | bytes 221192 | tf_op jit(solution)/shard_map/ppermute | solution.py:522
  156.6 1.4 collective-permute-start.39
  157.1 1.3 collective-permute-start.41

commit v2 on v0

--- a/solution.py
+++ b/solution.py
@@ -344,17 +344,14 @@
     return (wide[32:48, :] + wide[16:32, :]) + wide[0:16, :]
 
 
-def left_result(a0, a1, a2, a3, b0, b1, b2, b3, ml1, ml2, h2, out):
-    y = lax.axis_index("y")
+def left_result(first, second, ml1, ml2, h2, out):
     inverse = ml2[:, 0:K]
     factors = factor_parts(inverse, -mm(mm(inverse, h2[:, 0:K]), ml1[:, 0:K]))
-    for k, (first, second) in enumerate(zip((a0, a1, a2, a3), (b0, b1, b2, b3))):
-        base = spin(y, k) * 16
-
-        def result(i, base=base, first=first, second=second):
-            out[:, lanes(base + i)] = mix(factors, stacked(second[i]), stacked(first[i]))
-
-        each(16, result, 8)
+
+    def result(i):
+        out[:, lanes(i)] = mix(factors, second[i], first[i])
+
+    each(BR, result, 8)
 
 
 def by_side(pieces):
@@ -408,6 +405,7 @@
 SMALL = jax.ShapeDtypeStruct((K, BLK), F32)
 WIDE = jax.ShapeDtypeStruct((K, BR * BLK), F32)
 TILE = jax.ShapeDtypeStruct((NB, BLK, BLK), BF)
+PARTS = jax.ShapeDtypeStruct((BR, 48, BLK), BF)
 SPLIT = VMEM((BR, 48, BLK), BF)
 
 
@@ -486,8 +484,9 @@
     )
     left_chunk, mr0 = call(left_first, scatter_term(pieces), (panel(17), SMALL), terms=terms)
     left1 = gather(left_chunk, "y")
-    back_scratch = [SPLIT, held_panel(72), held_panel(4)]
-    own, other = call(backward, (*index, *left1, held), (panel(36), panel(36)), back_scratch, limit=20)
+    back_scratch = [held_panel(72), held_panel(4)]
+    back_outs = (panel(36), panel(36), PARTS)
+    own, other, left1_parts = call(backward, (*index, *left1, held), back_outs, back_scratch, limit=20)
     right_chunk, ml1, right0 = call(
         right_first, (*scatter_doc(own, other), start, mr0), (panel(9), SMALL, panel(8)),
         [VMEM((4, 9, K, BLK), F32)], docs=docs,
@@ -500,9 +499,9 @@
         left_second, (*scatter_term(pieces), left_chunk, ml1), (panel(17), SMALL, SMALL), terms=terms
     )
     left2 = gather(left2_chunk, "y")
-    own, other = call(backward, (*index, *left2, held), (panel(36), panel(36)), back_scratch, limit=20)
+    own, other, left2_parts = call(backward, (*index, *left2, held), back_outs, back_scratch, limit=20)
     prior = call(
-        right_prior, (*right1, start, mr0, mr1, h1), jax.ShapeDtypeStruct((BR, 48, BLK), BF), [held_panel(BR)]
+        right_prior, (*right1, start, mr0, mr1, h1), PARTS, [held_panel(BR)]
     )
     right2_chunk, ext, ml2, h2 = call(
         right_second, (*scatter_doc(own, other), right_chunk, prior),
@@ -510,10 +509,10 @@
         [VMEM((4, 9, K, BLK), F32)], docs=docs,
     )
     mine = gather(right2_chunk, "x")
-    ext, theirs = lax.optimization_barrier((ext, lax.ppermute(right2_chunk, "c", SWAP)))
+    left_out = call(left_result, (left1_parts, left2_parts, ml1, ml2, h2), WIDE)
+    ext, left_out, *mine = lax.optimization_barrier((ext, left_out, *mine))
     ext = lax.all_to_all(ext, ("c", "x", "y", "zh"), 0, 0)
-    right2 = mine + [theirs] + [lax.ppermute(m, "c", SWAP) for m in mine[1:]]
-    left_out = call(left_result, (*left1, *left2, ml1, ml2, h2), WIDE)
+    right2 = mine + [lax.ppermute(m, "c", SWAP) for m in mine]
     right_out = call(right_result, (ext, *right2, prior), WIDE, terms=terms)
     return left_out, right_out
 

time: 175 us -> 179 us (1.023)
  Pallas kernels: 35.1 us -> 26.3 us
  starting transfers between devices: 79 us -> 86.6 us
  waiting for transfers between devices: 55.9 us -> 60.1 us
    ppermute x2, starting transfers between devices: 5.29 us -> 17.2 us  [scatter_doc(): got = lax.ppermute(other, 'c', SWAP)]
    all_to_all x1, waiting for transfers between devices: 0.01 us -> 11.2 us  [local(): ext = lax.all_to_all(ext, ('c', 'x', 'y', 'zh'), 0, 0)]
    pallas_call x11, Pallas kernels: 35.1 us -> 26.3 us  [call(): pl.pallas_call(functools.partial(body, **constants) if constants else bod...]
    ppermute x4, starting transfers between devices: 8.15 us -> 1.11 us  [local(): right2 = mine + [lax.ppermute(m, 'c', SWAP) for m in mine]]
    ppermute x2, starting transfers between devices: 9.27 us -> 15.2 us  [scatter_term(): return (mine, lax.ppermute(mine, 'zh', SWAP))]
    ppermute x30, waiting for transfers between devices: 40.8 us -> 36.9 us  [shift(): return lax.ppermute(value, axis, [(i, (i + k) % 4) for i in range(4)])]
    ppermute x2, waiting for transfers between devices: 10.9 us -> 7.61 us  [scatter_term(): return (mine, lax.ppermute(mine, 'zh', SWAP))]
    ppermute x4, starting transfers between devices: 8.77 us -> 5.76 us  [gather_doc(): return mine + [lax.ppermute(m, 'c', SWAP) for m in mine]]
  transfers between devices with their start and end apart: 43 -> 43, of which waited for: 29 -> 33; matrix products, arithmetic and copies ran while one was open for 0% -> 0% of each run, Pallas kernels for 3% -> 3%
where the time goes in v2:
time: 179 us; the launch traced here: 177 us
  starting transfers between devices  86.6 us (48%)
  waiting for transfers between devices  60.1 us (34%)
  Pallas kernels  26.3 us (15%)
  local copies, waits for them, and re-layouts  2.4 us (1%)
    ppermute x30, starting transfers between devices, shift(): return lax.ppermute(value, axis, [(i, (i + k) % 4) for i in range(4)])  37.5 us
    ppermute x30, waiting for transfers between devices, shift(): return lax.ppermute(value, axis, [(i, (i + k) % 4) for i in range(4)])  36.9 us
    pallas_call x11, Pallas kernels, call(): pl.pallas_call(functools.partial(body, **constants) if constants else bod...  26.3 us
    ppermute x2, starting transfers between devices, scatter_doc(): got = lax.ppermute(other, 'c', SWAP)  17.2 us
    ppermute x2, starting transfers between devices, scatter_term(): return (mine, lax.ppermute(mine, 'zh', SWAP))  15.2 us
    all_to_all x1, waiting for transfers between devices, local(): ext = lax.all_to_all(ext, ('c', 'x', 'y', 'zh'), 0, 0)  11.2 us
    all_to_all x1, starting transfers between devices, local(): ext = lax.all_to_all(ext, ('c', 'x', 'y', 'zh'), 0, 0)  9.77 us
    ppermute x2, waiting for transfers between devices, scatter_term(): return (mine, lax.ppermute(mine, 'zh', SWAP))  7.61 us
  transfers between devices with their start and end apart: 43, of which 33 were waited for; matrix products, arithmetic and copies ran while one was open for 0% of the time, Pallas kernels for 3%

profile of v2, /device:TPU:1, one launch (start us, length us, event | category | flops | bytes accessed | tf_op | source)
XLA Modules:
  0.0 177.0 jit_solution(16932255588987205580)
XLA Ops:
  1.3 1.0 copy-done
  2.3 0.7 copy-done.2
  3.0 0.7 copy-done.3
  3.7 4.4 %first_forward.1 = (f32[17,16,128]{2,1,0:T(8,128)S(1)}, f32[17,16,128]{2,1,0:T(8,128)S(1)}, f32[17,16,128]{2,1,0:T(8,128)S(1)}, f32[17,16,128]{2,1,0:T(8,128)S(1...) custom-call(s32[1,320]{1,0:T(1,128)S(1)} %copy-done.2, s32[1,320]{1,0:T(1,128)S(1)} %copy-done.3, ...), custom_call_target="tpu_custom_call" | custom-call | flops 2000000000 | bytes 2000000 | tf_op jit(solution)/shard_map/first_forward/pallas_call | solution.py:421
  8.2 4.6 %collective-permute-start = (f32[17,16,128]{2,1,0:T(8,128)S(1)}, f32[17,16,128]{2,1,0:T(8,128)S(1)}, u32[]{:S(2)}, u32[]{:S(2)}) collective-permute-start(f32[17,16,128]{2,1,0:T(8,128)S(1)} %get-tuple-element.36), channel_id=1, source_target_pairs={{0,2},{2,4},{4,6},{6,0},{1,3},{3,5},{5,7},{7,1},{8,10},{10,12},{12... | collective-permute-start | bytes 417800 | tf_op jit(solution)/shard_map/ppermute | solution.py:439
  12.8 2.5 %collective-permute-start.2 = (f32[17,16,128]{2,1,0:T(8,128)S(1)}, f32[17,16,128]{2,1,0:T(8,128)S(1)}, u32[]{:S(2)}, u32[]{:S(2)}) collective-permute-start(f32[17,16,128]{2,1,0:T(8,128)S(1)} %get-tuple-element.38), channel_id=1, source_target_pairs={{0,6},{2,0},{4,2},{6,4},{1,7},{3,1},{5,3},{7,5},{8,14},{10,8},{12,... | collective-permute-start | bytes 417800 | tf_op jit(solution)/shard_map/ppermute | solution.py:439
  15.2 2.9 %collective-permute-done.1 = f32[17,16,128]{2,1,0:T(8,128)S(1)} collective-permute-done((f32[17,16,128]{2,1,0:T(8,128)S(1)}, f32[17,16,128]{2,1,0:T(8,128)S(1)}, u32[]{:S(2)}, u32[]{:S(2)}) %collective-permute-start.1) | collective-permute-done | bytes 139296 | tf_op jit(solution)/shard_map/ppermute | solution.py:439
  18.2 11.1 %collective-permute-start.3 = (f32[17,16,128]{2,1,0:T(8,128)S(1)}, f32[17,16,128]{2,1,0:T(8,128)S(1)}, u32[]{:S(2)}, u32[]{:S(2)}) collective-permute-start(f32[17,16,128]{2,1,0:T(8,128)S(1)} %add_add_fusion.1.mine), channel_id=1, source_target_pairs={{0,1},{1,0},{2,3},{3,2},{4,5},{5,4},{6,7},{7,6},{8,9},{9,8},{10,11... | collective-permute-start | bytes 417800 | tf_op jit(solution)/shard_map/ppermute | solution.py:453
  29.3 3.7 %collective-permute-done.3.theirs = f32[17,16,128]{2,1,0:T(8,128)S(1)} collective-permute-done((f32[17,16,128]{2,1,0:T(8,128)S(1)}, f32[17,16,128]{2,1,0:T(8,128)S(1)}, u32[]{:S(2)}, u32[]{:S(2)}) %collective-permute-start.3) | collective-permute-done | bytes 139296 | tf_op jit(solution)/shard_map/ppermute | solution.py:453
  33.0 0.8 left_first.1
  33.9 0.9 collective-permute-start.6
  35.4 2.4 %collective-permute-done.6.p3 = f32[17,16,128]{2,1,0:T(8,128)S(1)} collective-permute-done((f32[17,16,128]{2,1,0:T(8,128)S(1)}, f32[17,16,128]{2,1,0:T(8,128)S(1)}, u32[]{:S(2)}, u32[]{:S(2)}) %collective-permute-start.6) | collective-permute-done | bytes 139296 | tf_op jit(solution)/shard_map/ppermute | solution.py:439
  37.8 2.5 %collective-permute-done.5.p2 = f32[17,16,128]{2,1,0:T(8,128)S(1)} collective-permute-done((f32[17,16,128]{2,1,0:T(8,128)S(1)}, f32[17,16,128]{2,1,0:T(8,128)S(1)}, u32[]{:S(2)}, u32[]{:S(2)}) %collective-permute-start.5) | collective-permute-done | bytes 139296 | tf_op jit(solution)/shard_map/ppermute | solution.py:439
  40.3 1.4 collective-permute-done.4.p1
  41.6 3.0 %backward.2 = (f32[36,16,128]{2,1,0:T(8,128)S(1)}, f32[36,16,128]{2,1,0:T(8,128)S(1)}, bf16[64,48,128]{2,1,0:T(8,128)(2,1)S(1)}) custom-call(s32[1,320]{1,0:T(1,128)S(1)} %copy-done.2, s32[1,320]{1,0:T(1,128)S(1)} %copy-done.3, s32[1,1]{1,0:T(1,128)S(6)} %copy.7.counts_any.counts, f32[17,16,128]{2,1,0:T(8,128)S(1)} %get-tuple-element.39.p0.left_raw, ...), custom_call_target="tpu_custom_call" | custom-call | flops 2000000000 | bytes 2000000 | tf_op jit(solution)/shard_map/backward/pallas_call | solution.py:421
  44.6 6.0 %collective-permute-start.7 = (f32[36,16,128]{2,1,0:T(8,128)S(1)}, f32[36,16,128]{2,1,0:T(8,128)S(1)}, u32[]{:S(2)}, u32[]{:S(2)}) collective-permute-start(f32[36,16,128]{2,1,0:T(8,128)S(1)} %get-tuple-element.42), channel_id=1, source_target_pairs={{0,8},{8,0},{1,9},{9,1},{2,10},{10,2},{3,11},{11,3},{4,12},{12,4},... | collective-permute-start | bytes 884744 | tf_op jit(solution)/shard_map/ppermute | solution.py:457
  50.7 1.2 collective-permute-done.7
  51.9 3.6 %collective-permute-start.8 = (f32[9,16,128]{2,1,0:T(8,128)S(1)}, f32[9,16,128]{2,1,0:T(8,128)S(1)}, u32[]{:S(2)}, u32[]{:S(2)}) collective-permute-start(f32[9,16,128]{2,1,0:T(8,128)S(1)} %get-tuple-element.71), channel_id=1, source_target_pairs={{0,16},{16,32},{32,48},{48,0},{1,17},{17,33},{33,49},{49,1},{2,18}... | collective-permute-start | bytes 221192 | tf_op jit(solution)/shard_map/ppermute | solution.py:439
  55.5 1.9 %collective-permute-start.9 = (f32[9,16,128]{2,1,0:T(8,128)S(1)}, f32[9,16,128]{2,1,0:T(8,128)S(1)}, u32[]{:S(2)}, u32[]{:S(2)}) collective-permute-start(f32[9,16,128]{2,1,0:T(8,128)S(1)} %get-tuple-element.73), channel_id=1, source_target_pairs={{0,32},{16,48},{32,0},{48,16},{1,33},{17,49},{33,1},{49,17},{2,34}... | collective-permute-start | bytes 221192 | tf_op jit(solution)/shard_map/ppermute | solution.py:439
  57.4 1.3 collective-permute-done.10
  58.7 1.5 collective-permute-done.9
  60.2 4.4 %collective-permute-start.13 = (f32[9,16,128]{2,1,0:T(8,128)S(1)}, f32[9,16,128]{2,1,0:T(8,128)S(1)}, u32[]{:S(2)}, u32[]{:S(2)}) collective-permute-start(f32[9,16,128]{2,1,0:T(8,128)S(1)} %fusion.5.t0), channel_id=1, source_target_pairs={{0,192},{64,0},{128,64},{192,128},{1,193},{65,1},{129,65},{193,129... | collective-permute-start | bytes 221192 | tf_op jit(solution)/shard_map/ppermute | solution.py:439
  65.1 1.0 collective-permute-done.13.t3
  66.1 2.7 %collective-permute-done.12.t2 = f32[9,16,128]{2,1,0:T(8,128)S(1)} collective-permute-done((f32[9,16,128]{2,1,0:T(8,128)S(1)}, f32[9,16,128]{2,1,0:T(8,128)S(1)}, u32[]{:S(2)}, u32[]{:S(2)}) %collective-permute-start.12) | collective-permute-done | bytes 73760 | tf_op jit(solution)/shard_map/ppermute | solution.py:439
  68.8 1.6 collective-permute-done.11.t1
  70.4 1.1 right_first.1
  71.5 3.7 %collective-permute-start.16 = (f32[9,16,128]{2,1,0:T(8,128)S(1)}, f32[9,16,128]{2,1,0:T(8,128)S(1)}, u32[]{:S(2)}, u32[]{:S(2)}) collective-permute-start(f32[9,16,128]{2,1,0:T(8,128)S(1)} %get-tuple-element.44.r0.right_raw), channel_id=1, source_target_pairs={{0,48},{16,0},{32,16},{48,32},{1,49},{17,1},{33,17},{49,33},{2,50}... | collective-permute-start | bytes 221192 | tf_op jit(solution)/shard_map/ppermute | solution.py:439
  75.8 1.1 collective-permute-start.17
  77.3 2.0 %collective-permute-start.20 = (f32[9,16,128]{2,1,0:T(8,128)S(1)}, f32[9,16,128]{2,1,0:T(8,128)S(1)}, u32[]{:S(2)}, u32[]{:S(2)}) collective-permute-start(f32[9,16,128]{2,1,0:T(8,128)S(1)} %collective-permute-done.16.r3), channel_id=1, source_target_pairs={{0,8},{8,0},{1,9},{9,1},{2,10},{10,2},{3,11},{11,3},{4,12},{12,4},... | collective-permute-start | bytes 221192 | tf_op jit(solution)/shard_map/ppermute | solution.py:465
  79.3 0.7 collective-permute-done.15.r2
  80.0 2.2 %collective-permute-start.19 = (f32[9,16,128]{2,1,0:T(8,128)S(1)}, f32[9,16,128]{2,1,0:T(8,128)S(1)}, u32[]{:S(2)}, u32[]{:S(2)}) collective-permute-start(f32[9,16,128]{2,1,0:T(8,128)S(1)} %collective-permute-done.15.r2), channel_id=1, source_target_pairs={{0,8},{8,0},{1,9},{9,1},{2,10},{10,2},{3,11},{11,3},{4,12},{12,4},... | collective-permute-start | bytes 221192 | tf_op jit(solution)/shard_map/ppermute | solution.py:465
  83.6 2.9 %forward.1 = (f32[17,16,128]{2,1,0:T(8,128)S(1)}, f32[17,16,128]{2,1,0:T(8,128)S(1)}, f32[17,16,128]{2,1,0:T(8,128)S(1)}, f32[17,16,128]{2,1,0:T(8,128)S(1)}) custom-call(s32[1,320]{1,0:T(1,128)S(1)} %copy-done.2, s32[1,320]{1,0:T(1,128)S(1)} %copy-done.3, s32[1,1]{1,0:T(1,128)S(6)} %copy.7.counts_any.counts, ...), custom_call_target="tpu_custom_call" | custom-call | flops 2000000000 | bytes 2000000 | tf_op jit(solution)/shard_map/forward/pallas_call | solution.py:421
  86.5 0.8 collective-permute-start.21
  87.3 2.5 %collective-permute-start.23 = (f32[17,16,128]{2,1,0:T(8,128)S(1)}, f32[17,16,128]{2,1,0:T(8,128)S(1)}, u32[]{:S(2)}, u32[]{:S(2)}) collective-permute-start(f32[17,16,128]{2,1,0:T(8,128)S(1)} %get-tuple-element.49), channel_id=1, source_target_pairs={{0,6},{2,0},{4,2},{6,4},{1,7},{3,1},{5,3},{7,5},{8,14},{10,8},{12,... | collective-permute-start | bytes 417800 | tf_op jit(solution)/shard_map/ppermute | solution.py:439
  89.8 3.4 %collective-permute-done.21 = f32[17,16,128]{2,1,0:T(8,128)S(1)} collective-permute-done((f32[17,16,128]{2,1,0:T(8,128)S(1)}, f32[17,16,128]{2,1,0:T(8,128)S(1)}, u32[]{:S(2)}, u32[]{:S(2)}) %collective-permute-start.21) | collective-permute-done | bytes 139296 | tf_op jit(solution)/shard_map/ppermute | solution.py:439
  93.2 0.9 collective-permute-done.23
  94.1 4.1 %collective-permute-start.24 = (f32[17,16,128]{2,1,0:T(8,128)S(1)}, f32[17,16,128]{2,1,0:T(8,128)S(1)}, u32[]{:S(2)}, u32[]{:S(2)}) collective-permute-start(f32[17,16,128]{2,1,0:T(8,128)S(1)} %add_add_fusion.mine), channel_id=1, source_target_pairs={{0,1},{1,0},{2,3},{3,2},{4,5},{5,4},{6,7},{7,6},{8,9},{9,8},{10,11... | collective-permute-start | bytes 417800 | tf_op jit(solution)/shard_map/ppermute | solution.py:453
  98.2 3.9 %collective-permute-done.24.theirs = f32[17,16,128]{2,1,0:T(8,128)S(1)} collective-permute-done((f32[17,16,128]{2,1,0:T(8,128)S(1)}, f32[17,16,128]{2,1,0:T(8,128)S(1)}, u32[]{:S(2)}, u32[]{:S(2)}) %collective-permute-start.24) | collective-permute-done | bytes 139296 | tf_op jit(solution)/shard_map/ppermute | solution.py:453
  102.1 1.3 left_second.1
  103.4 2.1 %collective-permute-start.27 = (f32[17,16,128]{2,1,0:T(8,128)S(1)}, f32[17,16,128]{2,1,0:T(8,128)S(1)}, u32[]{:S(2)}, u32[]{:S(2)}) collective-permute-start(f32[17,16,128]{2,1,0:T(8,128)S(1)} %get-tuple-element.51.p0), channel_id=1, source_target_pairs={{0,6},{2,0},{4,2},{6,4},{1,7},{3,1},{5,3},{7,5},{8,14},{10,8},{12,... | collective-permute-start | bytes 417800 | tf_op jit(solution)/shard_map/ppermute | solution.py:439
  105.4 0.8 collective-permute-start.26
  106.3 2.7 %collective-permute-done.27.p3 = f32[17,16,128]{2,1,0:T(8,128)S(1)} collective-permute-done((f32[17,16,128]{2,1,0:T(8,128)S(1)}, f32[17,16,128]{2,1,0:T(8,128)S(1)}, u32[]{:S(2)}, u32[]{:S(2)}) %collective-permute-start.27) | collective-permute-done | bytes 139296 | tf_op jit(solution)/shard_map/ppermute | solution.py:439
  108.9 2.0 %collective-permute-done.26.p2 = f32[17,16,128]{2,1,0:T(8,128)S(1)} collective-permute-done((f32[17,16,128]{2,1,0:T(8,128)S(1)}, f32[17,16,128]{2,1,0:T(8,128)S(1)}, u32[]{:S(2)}, u32[]{:S(2)}) %collective-permute-start.26) | collective-permute-done | bytes 139296 | tf_op jit(solution)/shard_map/ppermute | solution.py:439
  111.0 1.4 collective-permute-done.25.p1
  112.3 3.0 %backward.3 = (f32[36,16,128]{2,1,0:T(8,128)S(1)}, f32[36,16,128]{2,1,0:T(8,128)S(1)}, bf16[64,48,128]{2,1,0:T(8,128)(2,1)S(1)}) custom-call(s32[1,320]{1,0:T(1,128)S(1)} %copy-done.2, s32[1,320]{1,0:T(1,128)S(1)} %copy-done.3, s32[1,1]{1,0:T(1,128)S(6)} %copy.7.counts_any.counts, f32[17,16,128]{2,1,0:T(8,128)S(1)} %get-tuple-element.51.p0, ...), custom_call_target="tpu_custom_call" | custom-call | flops 2000000000 | bytes 2000000 | tf_op jit(solution)/shard_map/backward/pallas_call | solution.py:421
  115.3 11.2 %collective-permute-start.28 = (f32[36,16,128]{2,1,0:T(8,128)S(1)}, f32[36,16,128]{2,1,0:T(8,128)S(1)}, u32[]{:S(2)}, u32[]{:S(2)}) collective-permute-start(f32[36,16,128]{2,1,0:T(8,128)S(1)} %get-tuple-element.53), channel_id=1, source_target_pairs={{0,8},{8,0},{1,9},{9,1},{2,10},{10,2},{3,11},{11,3},{4,12},{12,4},... | collective-permute-start | bytes 884744 | tf_op jit(solution)/shard_map/ppermute | solution.py:457
  126.5 1.2 collective-permute-done.28
  127.8 2.7 %collective-permute-start.31 = (f32[9,16,128]{2,1,0:T(8,128)S(1)}, f32[9,16,128]{2,1,0:T(8,128)S(1)}, u32[]{:S(2)}, u32[]{:S(2)}) collective-permute-start(f32[9,16,128]{2,1,0:T(8,128)S(1)} %get-tuple-element.69), channel_id=1, source_target_pairs={{0,48},{16,0},{32,16},{48,32},{1,49},{17,1},{33,17},{49,33},{2,50}... | collective-permute-start | bytes 221192 | tf_op jit(solution)/shard_map/ppermute | solution.py:439
  130.5 1.7 collective-permute-done.29
  132.2 1.3 collective-permute-done.31
  133.5 1.7 collective-permute-done.30
  135.3 1.9 %collective-permute-start.33 = (f32[9,16,128]{2,1,0:T(8,128)S(1)}, f32[9,16,128]{2,1,0:T(8,128)S(1)}, u32[]{:S(2)}, u32[]{:S(2)}) collective-permute-start(f32[9,16,128]{2,1,0:T(8,128)S(1)} %fusion.2.t0), channel_id=1, source_target_pairs={{0,128},{64,192},{128,0},{192,64},{1,129},{65,193},{129,1},{193,65... | collective-permute-start | bytes 221192 | tf_op jit(solution)/shard_map/ppermute | solution.py:439
  137.2 1.4 collective-permute-start.32
  138.6 2.7 %right_prior.1.prior.right1 = bf16[64,48,128]{2,1,0:T(8,128)(2,1)S(1)} custom-call(f32[9,16,128]{2,1,0:T(8,128)S(1)} %get-tuple-element.44.r0.right_raw, f32[9,16,128]{2,1,0:T(8,128)S(1)} %collective-permute-done.14.r1, f32[9,16,128]{2,1,0:T(8,128)S(1)} %collective-permute-done.15.r2, f32[9,16,128]{2,1,0:T(8,128)S(1)} %collective-permute-done.16.r3, ...), custom_call_target="tpu_custom_call" | custom-call | flops 2000000000 | bytes 2000000 | tf_op jit(solution)/shard_map/right_prior/pallas_call | solution.py:421
  141.3 1.8 %collective-permute-done.32.t1 = f32[9,16,128]{2,1,0:T(8,128)S(1)} collective-permute-done((f32[9,16,128]{2,1,0:T(8,128)S(1)}, f32[9,16,128]{2,1,0:T(8,128)S(1)}, u32[]{:S(2)}, u32[]{:S(2)}) %collective-permute-start.32) | collective-permute-done | bytes 73760 | tf_op jit(solution)/shard_map/ppermute | solution.py:439
  143.1 1.9 %right_second.1 = (f32[8,16,128]{2,1,0:T(8,128)S(1)}, f32[64,8,128]{2,1,0:T(8,128)}, f32[16,128]{1,0:T(8,128)S(1)}, f32[16,128]{1,0:T(8,128)S(1)}) custom-call(f32[9,16,128]{2,1,0:T(8,128)S(1)} %fusion.2.t0, f32[9,16,128]{2,1,0:T(8,128)S(1)} %collective-permute-done.32.t1, f32[9,16,128]{2,1,0:T(8,128)S(1)} %collective-permute-done.33.t2, ...), custom_call_target="tpu_custom_call" | custom-call | flops 2000000000 | bytes 2000000 | tf_op jit(solution)/shard_map/right_second/pallas_call | solution.py:421
  145.0 1.1 collective-permute-start.37
  146.1 0.9 collective-permute-start.36
  147.0 2.9 %left_result.1 = f32[16,8192]{1,0:T(8,128)} custom-call(bf16[64,48,128]{2,1,0:T(8,128)(2,1)S(1)} %get-tuple-element.57.first, bf16[64,48,128]{2,1,0:T(8,128)(2,1)S(1)} %get-tuple-element.58.second, f32[16,128]{1,0:T(8,128)S(1)} %get-tuple-element.50.ml1, f32[16,128]{1,0:T(8,128)S(1)} %get-tuple-element.59.ml2, f32[16,128]{1,0:T(8,128)S(1)} %get-tuple-element.60.h2), custom_call_target="tpu_custom_call" | custom-call | flops 2000000000 | bytes 2000000 | tf_op jit(solution)/shard_map/left_result/pallas_call | solution.py:421
  149.9 0.8 collective-permute-done.36.r2
  150.8 0.7 collective-permute-done.35.r1
  151.5 9.8 %all-to-all-start = ((f32[64,8,128]{2,1,0:T(8,128)}), f32[64,8,128]{2,1,0:T(8,128)S(1)}, u32[]{:S(2)}, u32[]{:S(2)}) async-start(f32[64,8,128]{2,1,0:T(8,128)} %get-tuple-element.63), calls=%async_computation | async-start | bytes 524288 | tf_op jit(solution)/shard_map/all_to_all | solution.py:514
  163.4 11.2 %all-to-all-done.ext = f32[64,8,128]{2,1,0:T(8,128)S(1)} async-done(((f32[64,8,128]{2,1,0:T(8,128)}), f32[64,8,128]{2,1,0:T(8,128)S(1)}, u32[]{:S(2)}, u32[]{:S(2)}) %all-to-all-start) | async-done | bytes 262176 | tf_op jit(solution)/shard_map/all_to_all | solution.py:514
  174.7 2.4 %right_result.1 = f32[16,8192]{1,0:T(8,128)} custom-call(f32[64,8,128]{2,1,0:T(8,128)S(1)} %all-to-all-done.ext, f32[8,16,128]{2,1,0:T(8,128)S(1)} %get-tuple-element.64.r0, f32[8,16,128]{2,1,0:T(8,128)S(1)} %collective-permute-done.35.r1, f32[8,16,128]{2,1,0:T(8,128)S(1)} %collective-permute-done.36.r2, f32[8,16,128]{2,1,0:T(8,128)S(1)} %collective-permute-done.37.r3, ...), custom_call_target="tpu_custom_call" | custom-call | flops 2000000000 | bytes 2000000 | tf_op jit(solution)/shard_map/right_result/pallas_call | solution.py:421
  (47 shorter events, 6.0 us)
Async XLA Ops:
  1.3 1.0 copy-start
  2.3 0.7 copy-start.2
  3.0 0.7 copy-start.3
  8.1 62.2 %copy-start.1 = (f32[16,8192]{1,0:T(8,128)S(1)}, f32[16,8192]{1,0:T(8,128)}, u32[]{:S(2)}) copy-start(f32[16,8192]{1,0:T(8,128)} %start.3) | copy-start | bytes 1572868
  8.2 7.1 %collective-permute-start = (f32[17,16,128]{2,1,0:T(8,128)S(1)}, f32[17,16,128]{2,1,0:T(8,128)S(1)}, u32[]{:S(2)}, u32[]{:S(2)}) collective-permute-start(f32[17,16,128]{2,1,0:T(8,128)S(1)} %get-tuple-element.36), channel_id=1, source_target_pairs={{0,2},{2,4},{4,6},{6,0},{1,3},{3,5},{5,7},{7,1},{8,10},{10,12},{12... | collective-permute-start | bytes 417800 | tf_op jit(solution)/shard_map/ppermute | solution.py:439
  12.8 5.4 %collective-permute-start.1 = (f32[17,16,128]{2,1,0:T(8,128)S(1)}, f32[17,16,128]{2,1,0:T(8,128)S(1)}, u32[]{:S(2)}, u32[]{:S(2)}) collective-permute-start(f32[17,16,128]{2,1,0:T(8,128)S(1)} %get-tuple-element.37), channel_id=1, source_target_pairs={{0,4},{2,6},{4,0},{6,2},{1,5},{3,7},{5,1},{7,3},{8,12},{10,14},{12... | collective-permute-start | bytes 417800 | tf_op jit(solution)/shard_map/ppermute | solution.py:439
  12.8 5.4 %collective-permute-start.2 = (f32[17,16,128]{2,1,0:T(8,128)S(1)}, f32[17,16,128]{2,1,0:T(8,128)S(1)}, u32[]{:S(2)}, u32[]{:S(2)}) collective-permute-start(f32[17,16,128]{2,1,0:T(8,128)S(1)} %get-tuple-element.38), channel_id=1, source_target_pairs={{0,6},{2,0},{4,2},{6,4},{1,7},{3,1},{5,3},{7,5},{8,14},{10,8},{12,... | collective-permute-start | bytes 417800 | tf_op jit(solution)/shard_map/ppermute | solution.py:439
  18.2 14.8 %collective-permute-start.3 = (f32[17,16,128]{2,1,0:T(8,128)S(1)}, f32[17,16,128]{2,1,0:T(8,128)S(1)}, u32[]{:S(2)}, u32[]{:S(2)}) collective-permute-start(f32[17,16,128]{2,1,0:T(8,128)S(1)} %add_add_fusion.1.mine), channel_id=1, source_target_pairs={{0,1},{1,0},{2,3},{3,2},{4,5},{5,4},{6,7},{7,6},{8,9},{9,8},{10,11... | collective-permute-start | bytes 417800 | tf_op jit(solution)/shard_map/ppermute | solution.py:453
  33.9 3.9 %collective-permute-start.6 = (f32[17,16,128]{2,1,0:T(8,128)S(1)}, f32[17,16,128]{2,1,0:T(8,128)S(1)}, u32[]{:S(2)}, u32[]{:S(2)}) collective-permute-start(f32[17,16,128]{2,1,0:T(8,128)S(1)} %get-tuple-element.39.p0.left_raw), channel_id=1, source_target_pairs={{0,6},{2,0},{4,2},{6,4},{1,7},{3,1},{5,3},{7,5},{8,14},{10,8},{12,... | collective-permute-start | bytes 417800 | tf_op jit(solution)/shard_map/ppermute | solution.py:439
  34.7 5.5 %collective-permute-start.5 = (f32[17,16,128]{2,1,0:T(8,128)S(1)}, f32[17,16,128]{2,1,0:T(8,128)S(1)}, u32[]{:S(2)}, u32[]{:S(2)}) collective-permute-start(f32[17,16,128]{2,1,0:T(8,128)S(1)} %get-tuple-element.39.p0.left_raw), channel_id=1, source_target_pairs={{0,4},{2,6},{4,0},{6,2},{1,5},{3,7},{5,1},{7,3},{8,12},{10,14},{12... | collective-permute-start | bytes 417800 | tf_op jit(solution)/shard_map/ppermute | solution.py:439
  34.7 6.9 %collective-permute-start.4 = (f32[17,16,128]{2,1,0:T(8,128)S(1)}, f32[17,16,128]{2,1,0:T(8,128)S(1)}, u32[]{:S(2)}, u32[]{:S(2)}) collective-permute-start(f32[17,16,128]{2,1,0:T(8,128)S(1)} %get-tuple-element.39.p0.left_raw), channel_id=1, source_target_pairs={{0,2},{2,4},{4,6},{6,0},{1,3},{3,5},{5,7},{7,1},{8,10},{10,12},{12... | collective-permute-start | bytes 417800 | tf_op jit(solution)/shard_map/ppermute | solution.py:439
  44.6 7.3 %collective-permute-start.7 = (f32[36,16,128]{2,1,0:T(8,128)S(1)}, f32[36,16,128]{2,1,0:T(8,128)S(1)}, u32[]{:S(2)}, u32[]{:S(2)}) collective-permute-start(f32[36,16,128]{2,1,0:T(8,128)S(1)} %get-tuple-element.42), channel_id=1, source_target_pairs={{0,8},{8,0},{1,9},{9,1},{2,10},{10,2},{3,11},{11,3},{4,12},{12,4},... | collective-permute-start | bytes 884744 | tf_op jit(solution)/shard_map/ppermute | solution.py:457
  51.9 5.5 %collective-permute-start.8 = (f32[9,16,128]{2,1,0:T(8,128)S(1)}, f32[9,16,128]{2,1,0:T(8,128)S(1)}, u32[]{:S(2)}, u32[]{:S(2)}) collective-permute-start(f32[9,16,128]{2,1,0:T(8,128)S(1)} %get-tuple-element.71), channel_id=1, source_target_pairs={{0,16},{16,32},{32,48},{48,0},{1,17},{17,33},{33,49},{49,1},{2,18}... | collective-permute-start | bytes 221192 | tf_op jit(solution)/shard_map/ppermute | solution.py:439
  55.5 3.2 %collective-permute-start.10 = (f32[9,16,128]{2,1,0:T(8,128)S(1)}, f32[9,16,128]{2,1,0:T(8,128)S(1)}, u32[]{:S(2)}, u32[]{:S(2)}) collective-permute-start(f32[9,16,128]{2,1,0:T(8,128)S(1)} %get-tuple-element.72), channel_id=1, source_target_pairs={{0,48},{16,0},{32,16},{48,32},{1,49},{17,1},{33,17},{49,33},{2,50}... | collective-permute-start | bytes 221192 | tf_op jit(solution)/shard_map/ppermute | solution.py:439
  55.5 4.7 %collective-permute-start.9 = (f32[9,16,128]{2,1,0:T(8,128)S(1)}, f32[9,16,128]{2,1,0:T(8,128)S(1)}, u32[]{:S(2)}, u32[]{:S(2)}) collective-permute-start(f32[9,16,128]{2,1,0:T(8,128)S(1)} %get-tuple-element.73), channel_id=1, source_target_pairs={{0,32},{16,48},{32,0},{48,16},{1,33},{17,49},{33,1},{49,17},{2,34}... | collective-permute-start | bytes 221192 | tf_op jit(solution)/shard_map/ppermute | solution.py:439
  60.2 5.8 %collective-permute-start.13 = (f32[9,16,128]{2,1,0:T(8,128)S(1)}, f32[9,16,128]{2,1,0:T(8,128)S(1)}, u32[]{:S(2)}, u32[]{:S(2)}) collective-permute-start(f32[9,16,128]{2,1,0:T(8,128)S(1)} %fusion.5.t0), channel_id=1, source_target_pairs={{0,192},{64,0},{128,64},{192,128},{1,193},{65,1},{129,65},{193,129... | collective-permute-start | bytes 221192 | tf_op jit(solution)/shard_map/ppermute | solution.py:439
  64.7 4.1 %collective-permute-start.12 = (f32[9,16,128]{2,1,0:T(8,128)S(1)}, f32[9,16,128]{2,1,0:T(8,128)S(1)}, u32[]{:S(2)}, u32[]{:S(2)}) collective-permute-start(f32[9,16,128]{2,1,0:T(8,128)S(1)} %fusion.5.t0), channel_id=1, source_target_pairs={{0,128},{64,192},{128,0},{192,64},{1,129},{65,193},{129,1},{193,65... | collective-permute-start | bytes 221192 | tf_op jit(solution)/shard_map/ppermute | solution.py:439
  64.7 5.7 %collective-permute-start.11 = (f32[9,16,128]{2,1,0:T(8,128)S(1)}, f32[9,16,128]{2,1,0:T(8,128)S(1)}, u32[]{:S(2)}, u32[]{:S(2)}) collective-permute-start(f32[9,16,128]{2,1,0:T(8,128)S(1)} %fusion.5.t0), channel_id=1, source_target_pairs={{0,64},{64,128},{128,192},{192,0},{1,65},{65,129},{129,193},{193,1... | collective-permute-start | bytes 221192 | tf_op jit(solution)/shard_map/ppermute | solution.py:439
  71.5 5.8 %collective-permute-start.16 = (f32[9,16,128]{2,1,0:T(8,128)S(1)}, f32[9,16,128]{2,1,0:T(8,128)S(1)}, u32[]{:S(2)}, u32[]{:S(2)}) collective-permute-start(f32[9,16,128]{2,1,0:T(8,128)S(1)} %get-tuple-element.44.r0.right_raw), channel_id=1, source_target_pairs={{0,48},{16,0},{32,16},{48,32},{1,49},{17,1},{33,17},{49,33},{2,50}... | collective-permute-start | bytes 221192 | tf_op jit(solution)/shard_map/ppermute | solution.py:439
  75.2 4.8 %collective-permute-start.15 = (f32[9,16,128]{2,1,0:T(8,128)S(1)}, f32[9,16,128]{2,1,0:T(8,128)S(1)}, u32[]{:S(2)}, u32[]{:S(2)}) collective-permute-start(f32[9,16,128]{2,1,0:T(8,128)S(1)} %get-tuple-element.44.r0.right_raw), channel_id=1, source_target_pairs={{0,32},{16,48},{32,0},{48,16},{1,33},{17,49},{33,1},{49,17},{2,34}... | collective-permute-start | bytes 221192 | tf_op jit(solution)/shard_map/ppermute | solution.py:439
  75.2 7.0 %collective-permute-start.14 = (f32[9,16,128]{2,1,0:T(8,128)S(1)}, f32[9,16,128]{2,1,0:T(8,128)S(1)}, u32[]{:S(2)}, u32[]{:S(2)}) collective-permute-start(f32[9,16,128]{2,1,0:T(8,128)S(1)} %get-tuple-element.44.r0.right_raw), channel_id=1, source_target_pairs={{0,16},{16,32},{32,48},{48,0},{1,17},{17,33},{33,49},{49,1},{2,18}... | collective-permute-start | bytes 221192 | tf_op jit(solution)/shard_map/ppermute | solution.py:439
  75.8 6.8 %collective-permute-start.17 = (f32[9,16,128]{2,1,0:T(8,128)S(1)}, f32[9,16,128]{2,1,0:T(8,128)S(1)}, u32[]{:S(2)}, u32[]{:S(2)}) collective-permute-start(f32[9,16,128]{2,1,0:T(8,128)S(1)} %get-tuple-element.44.r0.right_raw), channel_id=1, source_target_pairs={{0,8},{8,0},{1,9},{9,1},{2,10},{10,2},{3,11},{11,3},{4,12},{12,4},... | collective-permute-start | bytes 221192 | tf_op jit(solution)/shard_map/ppermute | solution.py:465
  77.3 5.4 %collective-permute-start.20 = (f32[9,16,128]{2,1,0:T(8,128)S(1)}, f32[9,16,128]{2,1,0:T(8,128)S(1)}, u32[]{:S(2)}, u32[]{:S(2)}) collective-permute-start(f32[9,16,128]{2,1,0:T(8,128)S(1)} %collective-permute-done.16.r3), channel_id=1, source_target_pairs={{0,8},{8,0},{1,9},{9,1},{2,10},{10,2},{3,11},{11,3},{4,12},{12,4},... | collective-permute-start | bytes 221192 | tf_op jit(solution)/shard_map/ppermute | solution.py:465
  80.0 3.1 %collective-permute-start.19 = (f32[9,16,128]{2,1,0:T(8,128)S(1)}, f32[9,16,128]{2,1,0:T(8,128)S(1)}, u32[]{:S(2)}, u32[]{:S(2)}) collective-permute-start(f32[9,16,128]{2,1,0:T(8,128)S(1)} %collective-permute-done.15.r2), channel_id=1, source_target_pairs={{0,8},{8,0},{1,9},{9,1},{2,10},{10,2},{3,11},{11,3},{4,12},{12,4},... | collective-permute-start | bytes 221192 | tf_op jit(solution)/shard_map/ppermute | solution.py:465
  82.2 1.4 collective-permute-start.18
  86.5 6.7 %collective-permute-start.21 = (f32[17,16,128]{2,1,0:T(8,128)S(1)}, f32[17,16,128]{2,1,0:T(8,128)S(1)}, u32[]{:S(2)}, u32[]{:S(2)}) collective-permute-start(f32[17,16,128]{2,1,0:T(8,128)S(1)} %get-tuple-element.47), channel_id=1, source_target_pairs={{0,2},{2,4},{4,6},{6,0},{1,3},{3,5},{5,7},{7,1},{8,10},{10,12},{12... | collective-permute-start | bytes 417800 | tf_op jit(solution)/shard_map/ppermute | solution.py:439
  87.3 5.9 %collective-permute-start.22 = (f32[17,16,128]{2,1,0:T(8,128)S(1)}, f32[17,16,128]{2,1,0:T(8,128)S(1)}, u32[]{:S(2)}, u32[]{:S(2)}) collective-permute-start(f32[17,16,128]{2,1,0:T(8,128)S(1)} %get-tuple-element.48), channel_id=1, source_target_pairs={{0,4},{2,6},{4,0},{6,2},{1,5},{3,7},{5,1},{7,3},{8,12},{10,14},{12... | collective-permute-start | bytes 417800 | tf_op jit(solution)/shard_map/ppermute | solution.py:439
  87.3 6.8 %collective-permute-start.23 = (f32[17,16,128]{2,1,0:T(8,128)S(1)}, f32[17,16,128]{2,1,0:T(8,128)S(1)}, u32[]{:S(2)}, u32[]{:S(2)}) collective-permute-start(f32[17,16,128]{2,1,0:T(8,128)S(1)} %get-tuple-element.49), channel_id=1, source_target_pairs={{0,6},{2,0},{4,2},{6,4},{1,7},{3,1},{5,3},{7,5},{8,14},{10,8},{12,... | collective-permute-start | bytes 417800 | tf_op jit(solution)/shard_map/ppermute | solution.py:439
  94.1 8.0 %collective-permute-start.24 = (f32[17,16,128]{2,1,0:T(8,128)S(1)}, f32[17,16,128]{2,1,0:T(8,128)S(1)}, u32[]{:S(2)}, u32[]{:S(2)}) collective-permute-start(f32[17,16,128]{2,1,0:T(8,128)S(1)} %add_add_fusion.mine), channel_id=1, source_target_pairs={{0,1},{1,0},{2,3},{3,2},{4,5},{5,4},{6,7},{7,6},{8,9},{9,8},{10,11... | collective-permute-start | bytes 417800 | tf_op jit(solution)/shard_map/ppermute | solution.py:453
  103.4 5.5 %collective-permute-start.27 = (f32[17,16,128]{2,1,0:T(8,128)S(1)}, f32[17,16,128]{2,1,0:T(8,128)S(1)}, u32[]{:S(2)}, u32[]{:S(2)}) collective-permute-start(f32[17,16,128]{2,1,0:T(8,128)S(1)} %get-tuple-element.51.p0), channel_id=1, source_target_pairs={{0,6},{2,0},{4,2},{6,4},{1,7},{3,1},{5,3},{7,5},{8,14},{10,8},{12,... | collective-permute-start | bytes 417800 | tf_op jit(solution)/shard_map/ppermute | solution.py:439
  105.4 5.5 %collective-permute-start.26 = (f32[17,16,128]{2,1,0:T(8,128)S(1)}, f32[17,16,128]{2,1,0:T(8,128)S(1)}, u32[]{:S(2)}, u32[]{:S(2)}) collective-permute-start(f32[17,16,128]{2,1,0:T(8,128)S(1)} %get-tuple-element.51.p0), channel_id=1, source_target_pairs={{0,4},{2,6},{4,0},{6,2},{1,5},{3,7},{5,1},{7,3},{8,12},{10,14},{12... | collective-permute-start | bytes 417800 | tf_op jit(solution)/shard_map/ppermute | solution.py:439
  106.2 6.1 %collective-permute-start.25 = (f32[17,16,128]{2,1,0:T(8,128)S(1)}, f32[17,16,128]{2,1,0:T(8,128)S(1)}, u32[]{:S(2)}, u32[]{:S(2)}) collective-permute-start(f32[17,16,128]{2,1,0:T(8,128)S(1)} %get-tuple-element.51.p0), channel_id=1, source_target_pairs={{0,2},{2,4},{4,6},{6,0},{1,3},{3,5},{5,7},{7,1},{8,10},{10,12},{12... | collective-permute-start | bytes 417800 | tf_op jit(solution)/shard_map/ppermute | solution.py:439
  115.3 12.4 %collective-permute-start.28 = (f32[36,16,128]{2,1,0:T(8,128)S(1)}, f32[36,16,128]{2,1,0:T(8,128)S(1)}, u32[]{:S(2)}, u32[]{:S(2)}) collective-permute-start(f32[36,16,128]{2,1,0:T(8,128)S(1)} %get-tuple-element.53), channel_id=1, source_target_pairs={{0,8},{8,0},{1,9},{9,1},{2,10},{10,2},{3,11},{11,3},{4,12},{12,4},... | collective-permute-start | bytes 884744 | tf_op jit(solution)/shard_map/ppermute | solution.py:457
  127.8 4.5 %collective-permute-start.29 = (f32[9,16,128]{2,1,0:T(8,128)S(1)}, f32[9,16,128]{2,1,0:T(8,128)S(1)}, u32[]{:S(2)}, u32[]{:S(2)}) collective-permute-start(f32[9,16,128]{2,1,0:T(8,128)S(1)} %get-tuple-element.68), channel_id=1, source_target_pairs={{0,16},{16,32},{32,48},{48,0},{1,17},{17,33},{33,49},{49,1},{2,18}... | collective-permute-start | bytes 221192 | tf_op jit(solution)/shard_map/ppermute | solution.py:439
  127.8 5.7 %collective-permute-start.31 = (f32[9,16,128]{2,1,0:T(8,128)S(1)}, f32[9,16,128]{2,1,0:T(8,128)S(1)}, u32[]{:S(2)}, u32[]{:S(2)}) collective-permute-start(f32[9,16,128]{2,1,0:T(8,128)S(1)} %get-tuple-element.69), channel_id=1, source_target_pairs={{0,48},{16,0},{32,16},{48,32},{1,49},{17,1},{33,17},{49,33},{2,50}... | collective-permute-start | bytes 221192 | tf_op jit(solution)/shard_map/ppermute | solution.py:439
  130.5 4.7 %collective-permute-start.30 = (f32[9,16,128]{2,1,0:T(8,128)S(1)}, f32[9,16,128]{2,1,0:T(8,128)S(1)}, u32[]{:S(2)}, u32[]{:S(2)}) collective-permute-start(f32[9,16,128]{2,1,0:T(8,128)S(1)} %get-tuple-element.70), channel_id=1, source_target_pairs={{0,32},{16,48},{32,0},{48,16},{1,33},{17,49},{33,1},{49,17},{2,34}... | collective-permute-start | bytes 221192 | tf_op jit(solution)/shard_map/ppermute | solution.py:439
  135.2 6.0 %collective-permute-start.34 = (f32[9,16,128]{2,1,0:T(8,128)S(1)}, f32[9,16,128]{2,1,0:T(8,128)S(1)}, u32[]{:S(2)}, u32[]{:S(2)}) collective-permute-start(f32[9,16,128]{2,1,0:T(8,128)S(1)} %fusion.2.t0), channel_id=1, source_target_pairs={{0,192},{64,0},{128,64},{192,128},{1,193},{65,1},{129,65},{193,129... | collective-permute-start | bytes 221192 | tf_op jit(solution)/shard_map/ppermute | solution.py:439
  135.3 5.9 %collective-permute-start.33 = (f32[9,16,128]{2,1,0:T(8,128)S(1)}, f32[9,16,128]{2,1,0:T(8,128)S(1)}, u32[]{:S(2)}, u32[]{:S(2)}) collective-permute-start(f32[9,16,128]{2,1,0:T(8,128)S(1)} %fusion.2.t0), channel_id=1, source_target_pairs={{0,128},{64,192},{128,0},{192,64},{1,129},{65,193},{129,1},{193,65... | collective-permute-start | bytes 221192 | tf_op jit(solution)/shard_map/ppermute | solution.py:439
  137.2 5.9 %collective-permute-start.32 = (f32[9,16,128]{2,1,0:T(8,128)S(1)}, f32[9,16,128]{2,1,0:T(8,128)S(1)}, u32[]{:S(2)}, u32[]{:S(2)}) collective-permute-start(f32[9,16,128]{2,1,0:T(8,128)S(1)} %fusion.2.t0), channel_id=1, source_target_pairs={{0,64},{64,128},{128,192},{192,0},{1,65},{65,129},{129,193},{193,1... | collective-permute-start | bytes 221192 | tf_op jit(solution)/shard_map/ppermute | solution.py:439
  145.0 4.9 %collective-permute-start.37 = (f32[8,16,128]{2,1,0:T(8,128)S(1)}, f32[8,16,128]{2,1,0:T(8,128)S(1)}, u32[]{:S(2)}, u32[]{:S(2)}) collective-permute-start(f32[8,16,128]{2,1,0:T(8,128)S(1)} %get-tuple-element.64.r0), channel_id=1, source_target_pairs={{0,48},{16,0},{32,16},{48,32},{1,49},{17,1},{33,17},{49,33},{2,50}... | collective-permute-start | bytes 196616 | tf_op jit(solution)/shard_map/ppermute | solution.py:439
  146.1 4.6 %collective-permute-start.36 = (f32[8,16,128]{2,1,0:T(8,128)S(1)}, f32[8,16,128]{2,1,0:T(8,128)S(1)}, u32[]{:S(2)}, u32[]{:S(2)}) collective-permute-start(f32[8,16,128]{2,1,0:T(8,128)S(1)} %get-tuple-element.64.r0), channel_id=1, source_target_pairs={{0,32},{16,48},{32,0},{48,16},{1,33},{17,49},{33,1},{49,17},{2,34}... | collective-permute-start | bytes 196616 | tf_op jit(solution)/shard_map/ppermute | solution.py:439
  147.0 4.4 %collective-permute-start.35 = (f32[8,16,128]{2,1,0:T(8,128)S(1)}, f32[8,16,128]{2,1,0:T(8,128)S(1)}, u32[]{:S(2)}, u32[]{:S(2)}) collective-permute-start(f32[8,16,128]{2,1,0:T(8,128)S(1)} %get-tuple-element.64.r0), channel_id=1, source_target_pairs={{0,16},{16,32},{32,48},{48,0},{1,17},{17,33},{33,49},{49,1},{2,18}... | collective-permute-start | bytes 196616 | tf_op jit(solution)/shard_map/ppermute | solution.py:439
  151.5 23.2 %all-to-all-start = ((f32[64,8,128]{2,1,0:T(8,128)}), f32[64,8,128]{2,1,0:T(8,128)S(1)}, u32[]{:S(2)}, u32[]{:S(2)}) async-start(f32[64,8,128]{2,1,0:T(8,128)} %get-tuple-element.63), calls=%async_computation | async-start | bytes 524288 | tf_op jit(solution)/shard_map/all_to_all | solution.py:514
  161.2 1.3 collective-permute-start.38
  161.7 1.3 collective-permute-start.39
  161.8 1.3 collective-permute-start.40
  162.2 1.3 collective-permute-start.41

commit v3 on v0

--- a/solution.py
+++ b/solution.py
@@ -401,6 +401,10 @@
         each(8, result, 8)
 
 
+def in_hbm(value):
+    return pltpu.with_memory_space_constraint(value, pltpu.HBM)
+
+
 def panel(n):
     return jax.ShapeDtypeStruct((n, K, BLK), F32)
 
@@ -474,7 +478,7 @@
 
     *pieces, held, turned = call(
         first_forward,
-        (*index, start, blocks),
+        (*(in_hbm(v) for v in index[:2]), counts, in_hbm(start), blocks),
         (panel(17),) * 4 + (TILE, TILE),
         [
             SMEM((1, NB), jnp.int32), SMEM((1, NB), jnp.int32), SMEM((1, 1), jnp.int32),
@@ -510,10 +514,10 @@
         [VMEM((4, 9, K, BLK), F32)], docs=docs,
     )
     mine = gather(right2_chunk, "x")
-    ext, theirs = lax.optimization_barrier((ext, lax.ppermute(right2_chunk, "c", SWAP)))
     ext = lax.all_to_all(ext, ("c", "x", "y", "zh"), 0, 0)
-    right2 = mine + [theirs] + [lax.ppermute(m, "c", SWAP) for m in mine[1:]]
     left_out = call(left_result, (*left1, *left2, ml1, ml2, h2), WIDE)
+    mine[3], left_out = lax.optimization_barrier((mine[3], left_out))
+    right2 = mine + [lax.ppermute(m, "c", SWAP) for m in mine]
     right_out = call(right_result, (ext, *right2, prior), WIDE, terms=terms)
     return left_out, right_out
 

time: 175 us -> 172 us (0.983)
  starting transfers between devices: 79 us -> 97.6 us
  waiting for transfers between devices: 55.9 us -> 46.1 us
  Pallas kernels: 35.1 us -> 26.8 us
  local copies, waits for them, and re-layouts: 2.4 us -> 0.01 us
    ppermute x30, starting transfers between devices: 37.4 us -> 58.6 us  [shift(): return lax.ppermute(value, axis, [(i, (i + k) % 4) for i in range(4)])]
    pallas_call x11, Pallas kernels: 35.1 us -> 26.8 us  [call(): pl.pallas_call(functools.partial(body, **constants) if constants else bod...]
    ppermute x30, waiting for transfers between devices: 40.8 us -> 34 us  [shift(): return lax.ppermute(value, axis, [(i, (i + k) % 4) for i in range(4)])]
    ppermute x4, starting transfers between devices: 8.15 us -> 2.12 us  [local(): right2 = mine + [lax.ppermute(m, 'c', SWAP) for m in mine]]
    ppermute x2, waiting for transfers between devices: 10.9 us -> 5.87 us  [scatter_term(): return (mine, lax.ppermute(mine, 'zh', SWAP))]
    unnamed x8 -> x6, local copies, waits for them, and re-layouts: 2.4 us -> 0.01 us
    all_to_all x1, waiting for transfers between devices: 0.01 us -> 2.07 us  [local(): ext = lax.all_to_all(ext, ('c', 'x', 'y', 'zh'), 0, 0)]
    all_to_all x1, starting transfers between devices: 10.2 us -> 12 us  [local(): ext = lax.all_to_all(ext, ('c', 'x', 'y', 'zh'), 0, 0)]
  transfers between devices with their start and end apart: 43 -> 43, of which waited for: 29 -> 25; matrix products, arithmetic and copies ran while one was open for 0% -> 0% of each run, Pallas kernels for 3% -> 3%
where the time goes in v3:
time: 172 us
  starting transfers between devices  97.6 us (57%)
  waiting for transfers between devices  46.1 us (27%)
  Pallas kernels  26.8 us (16%)
    ppermute x30, starting transfers between devices, shift(): return lax.ppermute(value, axis, [(i, (i + k) % 4) for i in range(4)])  58.6 us
    ppermute x30, waiting for transfers between devices, shift(): return lax.ppermute(value, axis, [(i, (i + k) % 4) for i in range(4)])  34 us
    pallas_call x11, Pallas kernels, call(): pl.pallas_call(functools.partial(body, **constants) if constants else bod...  26.8 us
    all_to_all x1, starting transfers between devices, local(): ext = lax.all_to_all(ext, ('c', 'x', 'y', 'zh'), 0, 0)  12 us
    ppermute x2, starting transfers between devices, scatter_term(): return (mine, lax.ppermute(mine, 'zh', SWAP))  11.1 us
    ppermute x4, starting transfers between devices, gather_doc(): return mine + [lax.ppermute(m, 'c', SWAP) for m in mine]  8.25 us
    ppermute x2, waiting for transfers between devices, scatter_term(): return (mine, lax.ppermute(mine, 'zh', SWAP))  5.87 us
    ppermute x2, starting transfers between devices, scatter_doc(): got = lax.ppermute(other, 'c', SWAP)  5.58 us
  transfers between devices with their start and end apart: 43, of which 25 were waited for; matrix products, arithmetic and copies ran while one was open for 0% of the time, Pallas kernels for 3%

profile of v3, /device:TPU:1, one launch (start us, length us, event | category | flops | bytes accessed | tf_op | source)
XLA Modules:
  0.0 172.3 jit_solution(10363687388040882990)
XLA Ops:
  1.3 6.3 %first_forward.1 = (f32[17,16,128]{2,1,0:T(8,128)S(1)}, f32[17,16,128]{2,1,0:T(8,128)S(1)}, f32[17,16,128]{2,1,0:T(8,128)S(1)}, f32[17,16,128]{2,1,0:T(8,128)S(1...) custom-call(s32[1,320]{1,0:T(1,128)} %rows.5, s32[1,320]{1,0:T(1,128)} %cols.5, ...), custom_call_target="tpu_custom_call" | custom-call | flops 2000000000 | bytes 2000000 | tf_op jit(solution)/shard_map/first_forward/pallas_call | solution.py:427
  7.7 2.7 %collective-permute-start = (f32[17,16,128]{2,1,0:T(8,128)S(1)}, f32[17,16,128]{2,1,0:T(8,128)S(1)}, u32[]{:S(2)}, u32[]{:S(2)}) collective-permute-start(f32[17,16,128]{2,1,0:T(8,128)S(1)} %get-tuple-element.30), channel_id=1, source_target_pairs={{0,2},{2,4},{4,6},{6,0},{1,3},{3,5},{5,7},{7,1},{8,10},{10,12},{12... | collective-permute-start | bytes 417800 | tf_op jit(solution)/shard_map/ppermute | solution.py:445
  10.3 4.1 %collective-permute-start.1 = (f32[17,16,128]{2,1,0:T(8,128)S(1)}, f32[17,16,128]{2,1,0:T(8,128)S(1)}, u32[]{:S(2)}, u32[]{:S(2)}) collective-permute-start(f32[17,16,128]{2,1,0:T(8,128)S(1)} %get-tuple-element.31), channel_id=1, source_target_pairs={{0,4},{2,6},{4,0},{6,2},{1,5},{3,7},{5,1},{7,3},{8,12},{10,14},{12... | collective-permute-start | bytes 417800 | tf_op jit(solution)/shard_map/ppermute | solution.py:445
  14.4 2.0 %collective-permute-start.2 = (f32[17,16,128]{2,1,0:T(8,128)S(1)}, f32[17,16,128]{2,1,0:T(8,128)S(1)}, u32[]{:S(2)}, u32[]{:S(2)}) collective-permute-start(f32[17,16,128]{2,1,0:T(8,128)S(1)} %get-tuple-element.32), channel_id=1, source_target_pairs={{0,6},{2,0},{4,2},{6,4},{1,7},{3,1},{5,3},{7,5},{8,14},{10,8},{12,... | collective-permute-start | bytes 417800 | tf_op jit(solution)/shard_map/ppermute | solution.py:445
  16.4 4.1 %collective-permute-done.1 = f32[17,16,128]{2,1,0:T(8,128)S(1)} collective-permute-done((f32[17,16,128]{2,1,0:T(8,128)S(1)}, f32[17,16,128]{2,1,0:T(8,128)S(1)}, u32[]{:S(2)}, u32[]{:S(2)}) %collective-permute-start.1) | collective-permute-done | bytes 139296 | tf_op jit(solution)/shard_map/ppermute | solution.py:445
  20.6 6.0 %collective-permute-start.3 = (f32[17,16,128]{2,1,0:T(8,128)S(1)}, f32[17,16,128]{2,1,0:T(8,128)S(1)}, u32[]{:S(2)}, u32[]{:S(2)}) collective-permute-start(f32[17,16,128]{2,1,0:T(8,128)S(1)} %add_add_fusion.1.mine), channel_id=1, source_target_pairs={{0,1},{1,0},{2,3},{3,2},{4,5},{5,4},{6,7},{7,6},{8,9},{9,8},{10,11... | collective-permute-start | bytes 417800 | tf_op jit(solution)/shard_map/ppermute | solution.py:459
  26.6 2.5 %collective-permute-done.3.theirs = f32[17,16,128]{2,1,0:T(8,128)S(1)} collective-permute-done((f32[17,16,128]{2,1,0:T(8,128)S(1)}, f32[17,16,128]{2,1,0:T(8,128)S(1)}, u32[]{:S(2)}, u32[]{:S(2)}) %collective-permute-start.3) | collective-permute-done | bytes 139296 | tf_op jit(solution)/shard_map/ppermute | solution.py:459
  29.1 0.8 left_first.1
  29.9 3.9 %collective-permute-start.6 = (f32[17,16,128]{2,1,0:T(8,128)S(1)}, f32[17,16,128]{2,1,0:T(8,128)S(1)}, u32[]{:S(2)}, u32[]{:S(2)}) collective-permute-start(f32[17,16,128]{2,1,0:T(8,128)S(1)} %get-tuple-element.33.p0.left_raw.a0), channel_id=1, source_target_pairs={{0,6},{2,0},{4,2},{6,4},{1,7},{3,1},{5,3},{7,5},{8,14},{10,8},{12,... | collective-permute-start | bytes 417800 | tf_op jit(solution)/shard_map/ppermute | solution.py:445
  33.8 1.4 collective-permute-start.5
  35.1 0.8 collective-permute-start.4
  36.0 3.3 %collective-permute-done.5.p2.a2 = f32[17,16,128]{2,1,0:T(8,128)S(1)} collective-permute-done((f32[17,16,128]{2,1,0:T(8,128)S(1)}, f32[17,16,128]{2,1,0:T(8,128)S(1)}, u32[]{:S(2)}, u32[]{:S(2)}) %collective-permute-start.5) | collective-permute-done | bytes 139296 | tf_op jit(solution)/shard_map/ppermute | solution.py:445
  39.2 2.1 %collective-permute-done.4.p1.a1 = f32[17,16,128]{2,1,0:T(8,128)S(1)} collective-permute-done((f32[17,16,128]{2,1,0:T(8,128)S(1)}, f32[17,16,128]{2,1,0:T(8,128)S(1)}, u32[]{:S(2)}, u32[]{:S(2)}) %collective-permute-start.4) | collective-permute-done | bytes 139296 | tf_op jit(solution)/shard_map/ppermute | solution.py:445
  41.4 2.6 %backward.2 = (f32[36,16,128]{2,1,0:T(8,128)S(1)}, f32[36,16,128]{2,1,0:T(8,128)S(1)}) custom-call(s32[1,320]{1,0:T(1,128)S(1)} %copy-done.1, s32[1,320]{1,0:T(1,128)S(1)} %copy-done.2, s32[1,1]{1,0:T(1,128)S(6)} %copy.7.counts_any.counts, f32[17,16,128]{2,1,0:T(8,128)S(1)} %get-tuple-element.33.p0.left_raw.a0, ...), custom_call_target="tpu_custom_call" | custom-call | flops 2000000000 | bytes 2000000 | tf_op jit(solution)/shard_map/backward/pallas_call | solution.py:427
  44.0 3.5 %collective-permute-start.7 = (f32[36,16,128]{2,1,0:T(8,128)S(1)}, f32[36,16,128]{2,1,0:T(8,128)S(1)}, u32[]{:S(2)}, u32[]{:S(2)}) collective-permute-start(f32[36,16,128]{2,1,0:T(8,128)S(1)} %get-tuple-element.36), channel_id=1, source_target_pairs={{0,8},{8,0},{1,9},{9,1},{2,10},{10,2},{3,11},{11,3},{4,12},{12,4},... | collective-permute-start | bytes 884744 | tf_op jit(solution)/shard_map/ppermute | solution.py:463
  47.4 1.2 collective-permute-done.7
  48.7 5.7 %collective-permute-start.8 = (f32[9,16,128]{2,1,0:T(8,128)S(1)}, f32[9,16,128]{2,1,0:T(8,128)S(1)}, u32[]{:S(2)}, u32[]{:S(2)}) collective-permute-start(f32[9,16,128]{2,1,0:T(8,128)S(1)} %get-tuple-element.59), channel_id=1, source_target_pairs={{0,16},{16,32},{32,48},{48,0},{1,17},{17,33},{33,49},{49,1},{2,18}... | collective-permute-start | bytes 221192 | tf_op jit(solution)/shard_map/ppermute | solution.py:445
  54.4 1.9 %collective-permute-start.9 = (f32[9,16,128]{2,1,0:T(8,128)S(1)}, f32[9,16,128]{2,1,0:T(8,128)S(1)}, u32[]{:S(2)}, u32[]{:S(2)}) collective-permute-start(f32[9,16,128]{2,1,0:T(8,128)S(1)} %get-tuple-element.61), channel_id=1, source_target_pairs={{0,32},{16,48},{32,0},{48,16},{1,33},{17,49},{33,1},{49,17},{2,34}... | collective-permute-start | bytes 221192 | tf_op jit(solution)/shard_map/ppermute | solution.py:445
  56.3 1.3 collective-permute-done.10
  57.6 1.5 collective-permute-done.9
  59.1 4.2 %collective-permute-start.13 = (f32[9,16,128]{2,1,0:T(8,128)S(1)}, f32[9,16,128]{2,1,0:T(8,128)S(1)}, u32[]{:S(2)}, u32[]{:S(2)}) collective-permute-start(f32[9,16,128]{2,1,0:T(8,128)S(1)} %fusion.5.t0), channel_id=1, source_target_pairs={{0,192},{64,0},{128,64},{192,128},{1,193},{65,1},{129,65},{193,129... | collective-permute-start | bytes 221192 | tf_op jit(solution)/shard_map/ppermute | solution.py:445
  63.3 1.2 collective-permute-start.12
  64.5 0.6 collective-permute-done.13.t3
  65.1 3.2 %collective-permute-done.12.t2 = f32[9,16,128]{2,1,0:T(8,128)S(1)} collective-permute-done((f32[9,16,128]{2,1,0:T(8,128)S(1)}, f32[9,16,128]{2,1,0:T(8,128)S(1)}, u32[]{:S(2)}, u32[]{:S(2)}) %collective-permute-start.12) | collective-permute-done | bytes 73760 | tf_op jit(solution)/shard_map/ppermute | solution.py:445
  68.3 2.1 %collective-permute-done.11.t1 = f32[9,16,128]{2,1,0:T(8,128)S(1)} collective-permute-done((f32[9,16,128]{2,1,0:T(8,128)S(1)}, f32[9,16,128]{2,1,0:T(8,128)S(1)}, u32[]{:S(2)}, u32[]{:S(2)}) %collective-permute-start.11) | collective-permute-done | bytes 73760 | tf_op jit(solution)/shard_map/ppermute | solution.py:445
  70.3 1.1 right_first.1
  71.4 2.0 %collective-permute-start.16 = (f32[9,16,128]{2,1,0:T(8,128)S(1)}, f32[9,16,128]{2,1,0:T(8,128)S(1)}, u32[]{:S(2)}, u32[]{:S(2)}) collective-permute-start(f32[9,16,128]{2,1,0:T(8,128)S(1)} %get-tuple-element.38.r0.right_raw), channel_id=1, source_target_pairs={{0,48},{16,0},{32,16},{48,32},{1,49},{17,1},{33,17},{49,33},{2,50}... | collective-permute-start | bytes 221192 | tf_op jit(solution)/shard_map/ppermute | solution.py:445
  73.4 0.6 collective-permute-start.14
  74.1 2.9 %collective-permute-start.17 = (f32[9,16,128]{2,1,0:T(8,128)S(1)}, f32[9,16,128]{2,1,0:T(8,128)S(1)}, u32[]{:S(2)}, u32[]{:S(2)}) collective-permute-start(f32[9,16,128]{2,1,0:T(8,128)S(1)} %get-tuple-element.38.r0.right_raw), channel_id=1, source_target_pairs={{0,8},{8,0},{1,9},{9,1},{2,10},{10,2},{3,11},{11,3},{4,12},{12,4},... | collective-permute-start | bytes 221192 | tf_op jit(solution)/shard_map/ppermute | solution.py:471
  77.0 1.7 collective-permute-start.20
  78.7 3.3 %collective-permute-start.19 = (f32[9,16,128]{2,1,0:T(8,128)S(1)}, f32[9,16,128]{2,1,0:T(8,128)S(1)}, u32[]{:S(2)}, u32[]{:S(2)}) collective-permute-start(f32[9,16,128]{2,1,0:T(8,128)S(1)} %collective-permute-done.15.r2), channel_id=1, source_target_pairs={{0,8},{8,0},{1,9},{9,1},{2,10},{10,2},{3,11},{11,3},{4,12},{12,4},... | collective-permute-start | bytes 221192 | tf_op jit(solution)/shard_map/ppermute | solution.py:471
  82.3 0.5 collective-permute-done.19.w2
  83.3 2.5 %forward.1 = (f32[17,16,128]{2,1,0:T(8,128)S(1)}, f32[17,16,128]{2,1,0:T(8,128)S(1)}, f32[17,16,128]{2,1,0:T(8,128)S(1)}, f32[17,16,128]{2,1,0:T(8,128)S(1)}) custom-call(s32[1,320]{1,0:T(1,128)S(1)} %copy-done.1, s32[1,320]{1,0:T(1,128)S(1)} %copy-done.2, s32[1,1]{1,0:T(1,128)S(6)} %copy.7.counts_any.counts, ...), custom_call_target="tpu_custom_call" | custom-call | flops 2000000000 | bytes 2000000 | tf_op jit(solution)/shard_map/forward/pallas_call | solution.py:427
  85.8 3.6 %collective-permute-start.22 = (f32[17,16,128]{2,1,0:T(8,128)S(1)}, f32[17,16,128]{2,1,0:T(8,128)S(1)}, u32[]{:S(2)}, u32[]{:S(2)}) collective-permute-start(f32[17,16,128]{2,1,0:T(8,128)S(1)} %get-tuple-element.42), channel_id=1, source_target_pairs={{0,4},{2,6},{4,0},{6,2},{1,5},{3,7},{5,1},{7,3},{8,12},{10,14},{12... | collective-permute-start | bytes 417800 | tf_op jit(solution)/shard_map/ppermute | solution.py:445
  89.5 2.0 %collective-permute-start.23 = (f32[17,16,128]{2,1,0:T(8,128)S(1)}, f32[17,16,128]{2,1,0:T(8,128)S(1)}, u32[]{:S(2)}, u32[]{:S(2)}) collective-permute-start(f32[17,16,128]{2,1,0:T(8,128)S(1)} %get-tuple-element.43), channel_id=1, source_target_pairs={{0,6},{2,0},{4,2},{6,4},{1,7},{3,1},{5,3},{7,5},{8,14},{10,8},{12,... | collective-permute-start | bytes 417800 | tf_op jit(solution)/shard_map/ppermute | solution.py:445
  91.5 4.7 %collective-permute-done.22 = f32[17,16,128]{2,1,0:T(8,128)S(1)} collective-permute-done((f32[17,16,128]{2,1,0:T(8,128)S(1)}, f32[17,16,128]{2,1,0:T(8,128)S(1)}, u32[]{:S(2)}, u32[]{:S(2)}) %collective-permute-start.22) | collective-permute-done | bytes 139296 | tf_op jit(solution)/shard_map/ppermute | solution.py:445
  96.2 5.1 %collective-permute-start.24 = (f32[17,16,128]{2,1,0:T(8,128)S(1)}, f32[17,16,128]{2,1,0:T(8,128)S(1)}, u32[]{:S(2)}, u32[]{:S(2)}) collective-permute-start(f32[17,16,128]{2,1,0:T(8,128)S(1)} %add_add_fusion.mine), channel_id=1, source_target_pairs={{0,1},{1,0},{2,3},{3,2},{4,5},{5,4},{6,7},{7,6},{8,9},{9,8},{10,11... | collective-permute-start | bytes 417800 | tf_op jit(solution)/shard_map/ppermute | solution.py:459
  101.3 3.3 %collective-permute-done.24.theirs = f32[17,16,128]{2,1,0:T(8,128)S(1)} collective-permute-done((f32[17,16,128]{2,1,0:T(8,128)S(1)}, f32[17,16,128]{2,1,0:T(8,128)S(1)}, u32[]{:S(2)}, u32[]{:S(2)}) %collective-permute-start.24) | collective-permute-done | bytes 139296 | tf_op jit(solution)/shard_map/ppermute | solution.py:459
  104.7 1.2 left_second.1
  105.9 2.5 %collective-permute-start.27 = (f32[17,16,128]{2,1,0:T(8,128)S(1)}, f32[17,16,128]{2,1,0:T(8,128)S(1)}, u32[]{:S(2)}, u32[]{:S(2)}) collective-permute-start(f32[17,16,128]{2,1,0:T(8,128)S(1)} %get-tuple-element.45.p0.b0), channel_id=1, source_target_pairs={{0,6},{2,0},{4,2},{6,4},{1,7},{3,1},{5,3},{7,5},{8,14},{10,8},{12,... | collective-permute-start | bytes 417800 | tf_op jit(solution)/shard_map/ppermute | solution.py:445
  108.4 3.6 %collective-permute-start.26 = (f32[17,16,128]{2,1,0:T(8,128)S(1)}, f32[17,16,128]{2,1,0:T(8,128)S(1)}, u32[]{:S(2)}, u32[]{:S(2)}) collective-permute-start(f32[17,16,128]{2,1,0:T(8,128)S(1)} %get-tuple-element.45.p0.b0), channel_id=1, source_target_pairs={{0,4},{2,6},{4,0},{6,2},{1,5},{3,7},{5,1},{7,3},{8,12},{10,14},{12... | collective-permute-start | bytes 417800 | tf_op jit(solution)/shard_map/ppermute | solution.py:445
  112.0 0.8 collective-permute-start.25
  112.7 1.7 collective-permute-done.26.p2.b2
  114.4 4.2 %collective-permute-done.25.p1.b1 = f32[17,16,128]{2,1,0:T(8,128)S(1)} collective-permute-done((f32[17,16,128]{2,1,0:T(8,128)S(1)}, f32[17,16,128]{2,1,0:T(8,128)S(1)}, u32[]{:S(2)}, u32[]{:S(2)}) %collective-permute-start.25) | collective-permute-done | bytes 139296 | tf_op jit(solution)/shard_map/ppermute | solution.py:445
  118.6 2.6 %backward.3 = (f32[36,16,128]{2,1,0:T(8,128)S(1)}, f32[36,16,128]{2,1,0:T(8,128)S(1)}) custom-call(s32[1,320]{1,0:T(1,128)S(1)} %copy-done.1, s32[1,320]{1,0:T(1,128)S(1)} %copy-done.2, s32[1,1]{1,0:T(1,128)S(6)} %copy.7.counts_any.counts, f32[17,16,128]{2,1,0:T(8,128)S(1)} %get-tuple-element.45.p0.b0, f32[17,16,128]{2,1,0:T(8,128)S(1)} %collective-permute-done.25.p1.b1, ...), custom_call_target="tpu_custom_call" | custom-call | flops 2000000000 | bytes 2000000 | tf_op jit(solution)/shard_map/backward/pallas_call | solution.py:427
  121.2 2.1 %collective-permute-start.28 = (f32[36,16,128]{2,1,0:T(8,128)S(1)}, f32[36,16,128]{2,1,0:T(8,128)S(1)}, u32[]{:S(2)}, u32[]{:S(2)}) collective-permute-start(f32[36,16,128]{2,1,0:T(8,128)S(1)} %get-tuple-element.47), channel_id=1, source_target_pairs={{0,8},{8,0},{1,9},{9,1},{2,10},{10,2},{3,11},{11,3},{4,12},{12,4},... | collective-permute-start | bytes 884744 | tf_op jit(solution)/shard_map/ppermute | solution.py:463
  123.3 1.2 collective-permute-done.28
  124.6 2.7 %collective-permute-start.29 = (f32[9,16,128]{2,1,0:T(8,128)S(1)}, f32[9,16,128]{2,1,0:T(8,128)S(1)}, u32[]{:S(2)}, u32[]{:S(2)}) collective-permute-start(f32[9,16,128]{2,1,0:T(8,128)S(1)} %get-tuple-element.56), channel_id=1, source_target_pairs={{0,16},{16,32},{32,48},{48,0},{1,17},{17,33},{33,49},{49,1},{2,18}... | collective-permute-start | bytes 221192 | tf_op jit(solution)/shard_map/ppermute | solution.py:445
  127.3 2.0 %collective-permute-start.30 = (f32[9,16,128]{2,1,0:T(8,128)S(1)}, f32[9,16,128]{2,1,0:T(8,128)S(1)}, u32[]{:S(2)}, u32[]{:S(2)}) collective-permute-start(f32[9,16,128]{2,1,0:T(8,128)S(1)} %get-tuple-element.58), channel_id=1, source_target_pairs={{0,32},{16,48},{32,0},{48,16},{1,33},{17,49},{33,1},{49,17},{2,34}... | collective-permute-start | bytes 221192 | tf_op jit(solution)/shard_map/ppermute | solution.py:445
  129.4 1.1 collective-permute-done.31
  130.5 1.6 collective-permute-done.30
  132.1 4.8 %collective-permute-start.34 = (f32[9,16,128]{2,1,0:T(8,128)S(1)}, f32[9,16,128]{2,1,0:T(8,128)S(1)}, u32[]{:S(2)}, u32[]{:S(2)}) collective-permute-start(f32[9,16,128]{2,1,0:T(8,128)S(1)} %fusion.2.t0), channel_id=1, source_target_pairs={{0,192},{64,0},{128,64},{192,128},{1,193},{65,1},{129,65},{193,129... | collective-permute-start | bytes 221192 | tf_op jit(solution)/shard_map/ppermute | solution.py:445
  136.9 0.6 collective-permute-start.32
  137.5 2.7 %right_prior.1.prior.right1 = bf16[64,48,128]{2,1,0:T(8,128)(2,1)S(1)} custom-call(f32[9,16,128]{2,1,0:T(8,128)S(1)} %get-tuple-element.38.r0.right_raw, f32[9,16,128]{2,1,0:T(8,128)S(1)} %collective-permute-done.14.r1, f32[9,16,128]{2,1,0:T(8,128)S(1)} %collective-permute-done.15.r2, f32[9,16,128]{2,1,0:T(8,128)S(1)} %collective-permute-done.16.r3, ...), custom_call_target="tpu_custom_call" | custom-call | flops 2000000000 | bytes 2000000 | tf_op jit(solution)/shard_map/right_prior/pallas_call | solution.py:427
  140.2 1.4 collective-permute-done.33.t2
  141.6 1.0 collective-permute-done.32.t1
  142.6 1.9 %right_second.1 = (f32[8,16,128]{2,1,0:T(8,128)S(1)}, f32[64,8,128]{2,1,0:T(8,128)}, f32[16,128]{1,0:T(8,128)S(1)}, f32[16,128]{1,0:T(8,128)S(1)}) custom-call(f32[9,16,128]{2,1,0:T(8,128)S(1)} %fusion.2.t0, f32[9,16,128]{2,1,0:T(8,128)S(1)} %collective-permute-done.32.t1, f32[9,16,128]{2,1,0:T(8,128)S(1)} %collective-permute-done.33.t2, ...), custom_call_target="tpu_custom_call" | custom-call | flops 2000000000 | bytes 2000000 | tf_op jit(solution)/shard_map/right_second/pallas_call | solution.py:427
  144.5 12.0 %all-to-all-start = ((f32[64,8,128]{2,1,0:T(8,128)}), f32[64,8,128]{2,1,0:T(8,128)S(1)}, u32[]{:S(2)}, u32[]{:S(2)}) async-start(f32[64,8,128]{2,1,0:T(8,128)} %get-tuple-element.54), calls=%async_computation | async-start | bytes 524288 | tf_op jit(solution)/shard_map/all_to_all | solution.py:517
  156.9 2.8 %collective-permute-start.37 = (f32[8,16,128]{2,1,0:T(8,128)S(1)}, f32[8,16,128]{2,1,0:T(8,128)S(1)}, u32[]{:S(2)}, u32[]{:S(2)}) collective-permute-start(f32[8,16,128]{2,1,0:T(8,128)S(1)} %get-tuple-element.50.r0), channel_id=1, source_target_pairs={{0,32},{16,48},{32,0},{48,16},{1,33},{17,49},{33,1},{49,17},{2,34}... | collective-permute-start | bytes 196616 | tf_op jit(solution)/shard_map/ppermute | solution.py:445
  160.1 2.4 %collective-permute-start.35 = (f32[8,16,128]{2,1,0:T(8,128)S(1)}, f32[8,16,128]{2,1,0:T(8,128)S(1)}, u32[]{:S(2)}, u32[]{:S(2)}) collective-permute-start(f32[8,16,128]{2,1,0:T(8,128)S(1)} %get-tuple-element.50.r0), channel_id=1, source_target_pairs={{0,48},{16,0},{32,16},{48,32},{1,49},{17,1},{33,17},{49,33},{2,50}... | collective-permute-start | bytes 196616 | tf_op jit(solution)/shard_map/ppermute | solution.py:445
  162.4 2.8 %left_result.1 = f32[16,8192]{1,0:T(8,128)} custom-call(f32[17,16,128]{2,1,0:T(8,128)S(1)} %get-tuple-element.33.p0.left_raw.a0, f32[17,16,128]{2,1,0:T(8,128)S(1)} %collective-permute-done.4.p1.a1, f32[17,16,128]{2,1,0:T(8,128)S(1)} %collective-permute-done.5.p2.a2, f32[17,16,128]{2,1,0:T(8,128)S(1)} %collective-permute-done.6.p3.a3, ...), custom_call_target="tpu_custom_call" | custom-call | flops 2000000000 | bytes 2000000 | tf_op jit(solution)/shard_map/left_result/pallas_call | solution.py:427
  165.3 1.2 collective-permute-start.40
  167.9 2.1 %all-to-all-done.ext = f32[64,8,128]{2,1,0:T(8,128)S(1)} async-done(((f32[64,8,128]{2,1,0:T(8,128)}), f32[64,8,128]{2,1,0:T(8,128)S(1)}, u32[]{:S(2)}, u32[]{:S(2)}) %all-to-all-start) | async-done | bytes 262176 | tf_op jit(solution)/shard_map/all_to_all | solution.py:517
  169.9 2.3 %right_result.1 = f32[16,8192]{1,0:T(8,128)} custom-call(f32[64,8,128]{2,1,0:T(8,128)S(1)} %all-to-all-done.ext, f32[8,16,128]{2,1,0:T(8,128)S(1)} %get-tuple-element.50.r0, f32[8,16,128]{2,1,0:T(8,128)S(1)} %collective-permute-done.36.r1, f32[8,16,128]{2,1,0:T(8,128)S(1)} %collective-permute-done.37.r2, f32[8,16,128]{2,1,0:T(8,128)S(1)} %collective-permute-done.35.r3, ...), custom_call_target="tpu_custom_call" | custom-call | flops 2000000000 | bytes 2000000 | tf_op jit(solution)/shard_map/right_result/pallas_call | solution.py:427
  (45 shorter events, 3.4 us)
Async XLA Ops:
  0.6 40.8 %copy-start.2 = (s32[1,320]{1,0:T(1,128)S(1)}, s32[1,320]{1,0:T(1,128)}, u32[]{:S(2)}) copy-start(s32[1,320]{1,0:T(1,128)} %cols.5) | copy-start | bytes 3844
  0.6 40.7 %copy-start.1 = (s32[1,320]{1,0:T(1,128)S(1)}, s32[1,320]{1,0:T(1,128)}, u32[]{:S(2)}) copy-start(s32[1,320]{1,0:T(1,128)} %rows.5) | copy-start | bytes 3844
  7.6 62.7 %copy-start = (f32[16,8192]{1,0:T(8,128)S(1)}, f32[16,8192]{1,0:T(8,128)}, u32[]{:S(2)}) copy-start(f32[16,8192]{1,0:T(8,128)} %start.3) | copy-start | bytes 1572868
  7.7 8.7 %collective-permute-start = (f32[17,16,128]{2,1,0:T(8,128)S(1)}, f32[17,16,128]{2,1,0:T(8,128)S(1)}, u32[]{:S(2)}, u32[]{:S(2)}) collective-permute-start(f32[17,16,128]{2,1,0:T(8,128)S(1)} %get-tuple-element.30), channel_id=1, source_target_pairs={{0,2},{2,4},{4,6},{6,0},{1,3},{3,5},{5,7},{7,1},{8,10},{10,12},{12... | collective-permute-start | bytes 417800 | tf_op jit(solution)/shard_map/ppermute | solution.py:445
  10.3 10.2 %collective-permute-start.1 = (f32[17,16,128]{2,1,0:T(8,128)S(1)}, f32[17,16,128]{2,1,0:T(8,128)S(1)}, u32[]{:S(2)}, u32[]{:S(2)}) collective-permute-start(f32[17,16,128]{2,1,0:T(8,128)S(1)} %get-tuple-element.31), channel_id=1, source_target_pairs={{0,4},{2,6},{4,0},{6,2},{1,5},{3,7},{5,1},{7,3},{8,12},{10,14},{12... | collective-permute-start | bytes 417800 | tf_op jit(solution)/shard_map/ppermute | solution.py:445
  14.4 6.1 %collective-permute-start.2 = (f32[17,16,128]{2,1,0:T(8,128)S(1)}, f32[17,16,128]{2,1,0:T(8,128)S(1)}, u32[]{:S(2)}, u32[]{:S(2)}) collective-permute-start(f32[17,16,128]{2,1,0:T(8,128)S(1)} %get-tuple-element.32), channel_id=1, source_target_pairs={{0,6},{2,0},{4,2},{6,4},{1,7},{3,1},{5,3},{7,5},{8,14},{10,8},{12,... | collective-permute-start | bytes 417800 | tf_op jit(solution)/shard_map/ppermute | solution.py:445
  20.6 8.5 %collective-permute-start.3 = (f32[17,16,128]{2,1,0:T(8,128)S(1)}, f32[17,16,128]{2,1,0:T(8,128)S(1)}, u32[]{:S(2)}, u32[]{:S(2)}) collective-permute-start(f32[17,16,128]{2,1,0:T(8,128)S(1)} %add_add_fusion.1.mine), channel_id=1, source_target_pairs={{0,1},{1,0},{2,3},{3,2},{4,5},{5,4},{6,7},{7,6},{8,9},{9,8},{10,11... | collective-permute-start | bytes 417800 | tf_op jit(solution)/shard_map/ppermute | solution.py:459
  29.9 6.0 %collective-permute-start.6 = (f32[17,16,128]{2,1,0:T(8,128)S(1)}, f32[17,16,128]{2,1,0:T(8,128)S(1)}, u32[]{:S(2)}, u32[]{:S(2)}) collective-permute-start(f32[17,16,128]{2,1,0:T(8,128)S(1)} %get-tuple-element.33.p0.left_raw.a0), channel_id=1, source_target_pairs={{0,6},{2,0},{4,2},{6,4},{1,7},{3,1},{5,3},{7,5},{8,14},{10,8},{12,... | collective-permute-start | bytes 417800 | tf_op jit(solution)/shard_map/ppermute | solution.py:445
  33.8 5.5 %collective-permute-start.5 = (f32[17,16,128]{2,1,0:T(8,128)S(1)}, f32[17,16,128]{2,1,0:T(8,128)S(1)}, u32[]{:S(2)}, u32[]{:S(2)}) collective-permute-start(f32[17,16,128]{2,1,0:T(8,128)S(1)} %get-tuple-element.33.p0.left_raw.a0), channel_id=1, source_target_pairs={{0,4},{2,6},{4,0},{6,2},{1,5},{3,7},{5,1},{7,3},{8,12},{10,14},{12... | collective-permute-start | bytes 417800 | tf_op jit(solution)/shard_map/ppermute | solution.py:445
  35.1 6.2 %collective-permute-start.4 = (f32[17,16,128]{2,1,0:T(8,128)S(1)}, f32[17,16,128]{2,1,0:T(8,128)S(1)}, u32[]{:S(2)}, u32[]{:S(2)}) collective-permute-start(f32[17,16,128]{2,1,0:T(8,128)S(1)} %get-tuple-element.33.p0.left_raw.a0), channel_id=1, source_target_pairs={{0,2},{2,4},{4,6},{6,0},{1,3},{3,5},{5,7},{7,1},{8,10},{10,12},{12... | collective-permute-start | bytes 417800 | tf_op jit(solution)/shard_map/ppermute | solution.py:445
  44.0 4.7 %collective-permute-start.7 = (f32[36,16,128]{2,1,0:T(8,128)S(1)}, f32[36,16,128]{2,1,0:T(8,128)S(1)}, u32[]{:S(2)}, u32[]{:S(2)}) collective-permute-start(f32[36,16,128]{2,1,0:T(8,128)S(1)} %get-tuple-element.36), channel_id=1, source_target_pairs={{0,8},{8,0},{1,9},{9,1},{2,10},{10,2},{3,11},{11,3},{4,12},{12,4},... | collective-permute-start | bytes 884744 | tf_op jit(solution)/shard_map/ppermute | solution.py:463
  48.7 7.6 %collective-permute-start.8 = (f32[9,16,128]{2,1,0:T(8,128)S(1)}, f32[9,16,128]{2,1,0:T(8,128)S(1)}, u32[]{:S(2)}, u32[]{:S(2)}) collective-permute-start(f32[9,16,128]{2,1,0:T(8,128)S(1)} %get-tuple-element.59), channel_id=1, source_target_pairs={{0,16},{16,32},{32,48},{48,0},{1,17},{17,33},{33,49},{49,1},{2,18}... | collective-permute-start | bytes 221192 | tf_op jit(solution)/shard_map/ppermute | solution.py:445
  54.4 3.2 %collective-permute-start.10 = (f32[9,16,128]{2,1,0:T(8,128)S(1)}, f32[9,16,128]{2,1,0:T(8,128)S(1)}, u32[]{:S(2)}, u32[]{:S(2)}) collective-permute-start(f32[9,16,128]{2,1,0:T(8,128)S(1)} %get-tuple-element.60), channel_id=1, source_target_pairs={{0,48},{16,0},{32,16},{48,32},{1,49},{17,1},{33,17},{49,33},{2,50}... | collective-permute-start | bytes 221192 | tf_op jit(solution)/shard_map/ppermute | solution.py:445
  54.4 4.7 %collective-permute-start.9 = (f32[9,16,128]{2,1,0:T(8,128)S(1)}, f32[9,16,128]{2,1,0:T(8,128)S(1)}, u32[]{:S(2)}, u32[]{:S(2)}) collective-permute-start(f32[9,16,128]{2,1,0:T(8,128)S(1)} %get-tuple-element.61), channel_id=1, source_target_pairs={{0,32},{16,48},{32,0},{48,16},{1,33},{17,49},{33,1},{49,17},{2,34}... | collective-permute-start | bytes 221192 | tf_op jit(solution)/shard_map/ppermute | solution.py:445
  59.1 5.9 %collective-permute-start.13 = (f32[9,16,128]{2,1,0:T(8,128)S(1)}, f32[9,16,128]{2,1,0:T(8,128)S(1)}, u32[]{:S(2)}, u32[]{:S(2)}) collective-permute-start(f32[9,16,128]{2,1,0:T(8,128)S(1)} %fusion.5.t0), channel_id=1, source_target_pairs={{0,192},{64,0},{128,64},{192,128},{1,193},{65,1},{129,65},{193,129... | collective-permute-start | bytes 221192 | tf_op jit(solution)/shard_map/ppermute | solution.py:445
  63.3 4.9 %collective-permute-start.12 = (f32[9,16,128]{2,1,0:T(8,128)S(1)}, f32[9,16,128]{2,1,0:T(8,128)S(1)}, u32[]{:S(2)}, u32[]{:S(2)}) collective-permute-start(f32[9,16,128]{2,1,0:T(8,128)S(1)} %fusion.5.t0), channel_id=1, source_target_pairs={{0,128},{64,192},{128,0},{192,64},{1,129},{65,193},{129,1},{193,65... | collective-permute-start | bytes 221192 | tf_op jit(solution)/shard_map/ppermute | solution.py:445
  64.5 5.8 %collective-permute-start.11 = (f32[9,16,128]{2,1,0:T(8,128)S(1)}, f32[9,16,128]{2,1,0:T(8,128)S(1)}, u32[]{:S(2)}, u32[]{:S(2)}) collective-permute-start(f32[9,16,128]{2,1,0:T(8,128)S(1)} %fusion.5.t0), channel_id=1, source_target_pairs={{0,64},{64,128},{128,192},{192,0},{1,65},{65,129},{129,193},{193,1... | collective-permute-start | bytes 221192 | tf_op jit(solution)/shard_map/ppermute | solution.py:445
  71.4 5.5 %collective-permute-start.16 = (f32[9,16,128]{2,1,0:T(8,128)S(1)}, f32[9,16,128]{2,1,0:T(8,128)S(1)}, u32[]{:S(2)}, u32[]{:S(2)}) collective-permute-start(f32[9,16,128]{2,1,0:T(8,128)S(1)} %get-tuple-element.38.r0.right_raw), channel_id=1, source_target_pairs={{0,48},{16,0},{32,16},{48,32},{1,49},{17,1},{33,17},{49,33},{2,50}... | collective-permute-start | bytes 221192 | tf_op jit(solution)/shard_map/ppermute | solution.py:445
  73.4 5.3 %collective-permute-start.15 = (f32[9,16,128]{2,1,0:T(8,128)S(1)}, f32[9,16,128]{2,1,0:T(8,128)S(1)}, u32[]{:S(2)}, u32[]{:S(2)}) collective-permute-start(f32[9,16,128]{2,1,0:T(8,128)S(1)} %get-tuple-element.38.r0.right_raw), channel_id=1, source_target_pairs={{0,32},{16,48},{32,0},{48,16},{1,33},{17,49},{33,1},{49,17},{2,34}... | collective-permute-start | bytes 221192 | tf_op jit(solution)/shard_map/ppermute | solution.py:445
  73.4 8.5 %collective-permute-start.14 = (f32[9,16,128]{2,1,0:T(8,128)S(1)}, f32[9,16,128]{2,1,0:T(8,128)S(1)}, u32[]{:S(2)}, u32[]{:S(2)}) collective-permute-start(f32[9,16,128]{2,1,0:T(8,128)S(1)} %get-tuple-element.38.r0.right_raw), channel_id=1, source_target_pairs={{0,16},{16,32},{32,48},{48,0},{1,17},{17,33},{33,49},{49,1},{2,18}... | collective-permute-start | bytes 221192 | tf_op jit(solution)/shard_map/ppermute | solution.py:445
  74.1 8.3 %collective-permute-start.17 = (f32[9,16,128]{2,1,0:T(8,128)S(1)}, f32[9,16,128]{2,1,0:T(8,128)S(1)}, u32[]{:S(2)}, u32[]{:S(2)}) collective-permute-start(f32[9,16,128]{2,1,0:T(8,128)S(1)} %get-tuple-element.38.r0.right_raw), channel_id=1, source_target_pairs={{0,8},{8,0},{1,9},{9,1},{2,10},{10,2},{3,11},{11,3},{4,12},{12,4},... | collective-permute-start | bytes 221192 | tf_op jit(solution)/shard_map/ppermute | solution.py:471
  77.0 5.4 %collective-permute-start.20 = (f32[9,16,128]{2,1,0:T(8,128)S(1)}, f32[9,16,128]{2,1,0:T(8,128)S(1)}, u32[]{:S(2)}, u32[]{:S(2)}) collective-permute-start(f32[9,16,128]{2,1,0:T(8,128)S(1)} %collective-permute-done.16.r3), channel_id=1, source_target_pairs={{0,8},{8,0},{1,9},{9,1},{2,10},{10,2},{3,11},{11,3},{4,12},{12,4},... | collective-permute-start | bytes 221192 | tf_op jit(solution)/shard_map/ppermute | solution.py:471
  78.7 4.2 %collective-permute-start.19 = (f32[9,16,128]{2,1,0:T(8,128)S(1)}, f32[9,16,128]{2,1,0:T(8,128)S(1)}, u32[]{:S(2)}, u32[]{:S(2)}) collective-permute-start(f32[9,16,128]{2,1,0:T(8,128)S(1)} %collective-permute-done.15.r2), channel_id=1, source_target_pairs={{0,8},{8,0},{1,9},{9,1},{2,10},{10,2},{3,11},{11,3},{4,12},{12,4},... | collective-permute-start | bytes 221192 | tf_op jit(solution)/shard_map/ppermute | solution.py:471
  81.9 1.3 collective-permute-start.18
  85.8 5.7 %collective-permute-start.21 = (f32[17,16,128]{2,1,0:T(8,128)S(1)}, f32[17,16,128]{2,1,0:T(8,128)S(1)}, u32[]{:S(2)}, u32[]{:S(2)}) collective-permute-start(f32[17,16,128]{2,1,0:T(8,128)S(1)} %get-tuple-element.41), channel_id=1, source_target_pairs={{0,2},{2,4},{4,6},{6,0},{1,3},{3,5},{5,7},{7,1},{8,10},{10,12},{12... | collective-permute-start | bytes 417800 | tf_op jit(solution)/shard_map/ppermute | solution.py:445
  85.8 10.3 %collective-permute-start.22 = (f32[17,16,128]{2,1,0:T(8,128)S(1)}, f32[17,16,128]{2,1,0:T(8,128)S(1)}, u32[]{:S(2)}, u32[]{:S(2)}) collective-permute-start(f32[17,16,128]{2,1,0:T(8,128)S(1)} %get-tuple-element.42), channel_id=1, source_target_pairs={{0,4},{2,6},{4,0},{6,2},{1,5},{3,7},{5,1},{7,3},{8,12},{10,14},{12... | collective-permute-start | bytes 417800 | tf_op jit(solution)/shard_map/ppermute | solution.py:445
  89.5 6.7 %collective-permute-start.23 = (f32[17,16,128]{2,1,0:T(8,128)S(1)}, f32[17,16,128]{2,1,0:T(8,128)S(1)}, u32[]{:S(2)}, u32[]{:S(2)}) collective-permute-start(f32[17,16,128]{2,1,0:T(8,128)S(1)} %get-tuple-element.43), channel_id=1, source_target_pairs={{0,6},{2,0},{4,2},{6,4},{1,7},{3,1},{5,3},{7,5},{8,14},{10,8},{12,... | collective-permute-start | bytes 417800 | tf_op jit(solution)/shard_map/ppermute | solution.py:445
  96.2 8.4 %collective-permute-start.24 = (f32[17,16,128]{2,1,0:T(8,128)S(1)}, f32[17,16,128]{2,1,0:T(8,128)S(1)}, u32[]{:S(2)}, u32[]{:S(2)}) collective-permute-start(f32[17,16,128]{2,1,0:T(8,128)S(1)} %add_add_fusion.mine), channel_id=1, source_target_pairs={{0,1},{1,0},{2,3},{3,2},{4,5},{5,4},{6,7},{7,6},{8,9},{9,8},{10,11... | collective-permute-start | bytes 417800 | tf_op jit(solution)/shard_map/ppermute | solution.py:459
  105.9 6.8 %collective-permute-start.27 = (f32[17,16,128]{2,1,0:T(8,128)S(1)}, f32[17,16,128]{2,1,0:T(8,128)S(1)}, u32[]{:S(2)}, u32[]{:S(2)}) collective-permute-start(f32[17,16,128]{2,1,0:T(8,128)S(1)} %get-tuple-element.45.p0.b0), channel_id=1, source_target_pairs={{0,6},{2,0},{4,2},{6,4},{1,7},{3,1},{5,3},{7,5},{8,14},{10,8},{12,... | collective-permute-start | bytes 417800 | tf_op jit(solution)/shard_map/ppermute | solution.py:445
  108.4 6.0 %collective-permute-start.26 = (f32[17,16,128]{2,1,0:T(8,128)S(1)}, f32[17,16,128]{2,1,0:T(8,128)S(1)}, u32[]{:S(2)}, u32[]{:S(2)}) collective-permute-start(f32[17,16,128]{2,1,0:T(8,128)S(1)} %get-tuple-element.45.p0.b0), channel_id=1, source_target_pairs={{0,4},{2,6},{4,0},{6,2},{1,5},{3,7},{5,1},{7,3},{8,12},{10,14},{12... | collective-permute-start | bytes 417800 | tf_op jit(solution)/shard_map/ppermute | solution.py:445
  112.0 6.7 %collective-permute-start.25 = (f32[17,16,128]{2,1,0:T(8,128)S(1)}, f32[17,16,128]{2,1,0:T(8,128)S(1)}, u32[]{:S(2)}, u32[]{:S(2)}) collective-permute-start(f32[17,16,128]{2,1,0:T(8,128)S(1)} %get-tuple-element.45.p0.b0), channel_id=1, source_target_pairs={{0,2},{2,4},{4,6},{6,0},{1,3},{3,5},{5,7},{7,1},{8,10},{10,12},{12... | collective-permute-start | bytes 417800 | tf_op jit(solution)/shard_map/ppermute | solution.py:445
  121.2 3.3 %collective-permute-start.28 = (f32[36,16,128]{2,1,0:T(8,128)S(1)}, f32[36,16,128]{2,1,0:T(8,128)S(1)}, u32[]{:S(2)}, u32[]{:S(2)}) collective-permute-start(f32[36,16,128]{2,1,0:T(8,128)S(1)} %get-tuple-element.47), channel_id=1, source_target_pairs={{0,8},{8,0},{1,9},{9,1},{2,10},{10,2},{3,11},{11,3},{4,12},{12,4},... | collective-permute-start | bytes 884744 | tf_op jit(solution)/shard_map/ppermute | solution.py:463
  124.6 4.8 %collective-permute-start.29 = (f32[9,16,128]{2,1,0:T(8,128)S(1)}, f32[9,16,128]{2,1,0:T(8,128)S(1)}, u32[]{:S(2)}, u32[]{:S(2)}) collective-permute-start(f32[9,16,128]{2,1,0:T(8,128)S(1)} %get-tuple-element.56), channel_id=1, source_target_pairs={{0,16},{16,32},{32,48},{48,0},{1,17},{17,33},{33,49},{49,1},{2,18}... | collective-permute-start | bytes 221192 | tf_op jit(solution)/shard_map/ppermute | solution.py:445
  127.3 3.2 %collective-permute-start.31 = (f32[9,16,128]{2,1,0:T(8,128)S(1)}, f32[9,16,128]{2,1,0:T(8,128)S(1)}, u32[]{:S(2)}, u32[]{:S(2)}) collective-permute-start(f32[9,16,128]{2,1,0:T(8,128)S(1)} %get-tuple-element.57), channel_id=1, source_target_pairs={{0,48},{16,0},{32,16},{48,32},{1,49},{17,1},{33,17},{49,33},{2,50}... | collective-permute-start | bytes 221192 | tf_op jit(solution)/shard_map/ppermute | solution.py:445
  127.3 4.7 %collective-permute-start.30 = (f32[9,16,128]{2,1,0:T(8,128)S(1)}, f32[9,16,128]{2,1,0:T(8,128)S(1)}, u32[]{:S(2)}, u32[]{:S(2)}) collective-permute-start(f32[9,16,128]{2,1,0:T(8,128)S(1)} %get-tuple-element.58), channel_id=1, source_target_pairs={{0,32},{16,48},{32,0},{48,16},{1,33},{17,49},{33,1},{49,17},{2,34}... | collective-permute-start | bytes 221192 | tf_op jit(solution)/shard_map/ppermute | solution.py:445
  132.1 8.1 %collective-permute-start.34 = (f32[9,16,128]{2,1,0:T(8,128)S(1)}, f32[9,16,128]{2,1,0:T(8,128)S(1)}, u32[]{:S(2)}, u32[]{:S(2)}) collective-permute-start(f32[9,16,128]{2,1,0:T(8,128)S(1)} %fusion.2.t0), channel_id=1, source_target_pairs={{0,192},{64,0},{128,64},{192,128},{1,193},{65,1},{129,65},{193,129... | collective-permute-start | bytes 221192 | tf_op jit(solution)/shard_map/ppermute | solution.py:445
  136.9 4.7 %collective-permute-start.33 = (f32[9,16,128]{2,1,0:T(8,128)S(1)}, f32[9,16,128]{2,1,0:T(8,128)S(1)}, u32[]{:S(2)}, u32[]{:S(2)}) collective-permute-start(f32[9,16,128]{2,1,0:T(8,128)S(1)} %fusion.2.t0), channel_id=1, source_target_pairs={{0,128},{64,192},{128,0},{192,64},{1,129},{65,193},{129,1},{193,65... | collective-permute-start | bytes 221192 | tf_op jit(solution)/shard_map/ppermute | solution.py:445
  136.9 5.7 %collective-permute-start.32 = (f32[9,16,128]{2,1,0:T(8,128)S(1)}, f32[9,16,128]{2,1,0:T(8,128)S(1)}, u32[]{:S(2)}, u32[]{:S(2)}) collective-permute-start(f32[9,16,128]{2,1,0:T(8,128)S(1)} %fusion.2.t0), channel_id=1, source_target_pairs={{0,64},{64,128},{128,192},{192,0},{1,65},{65,129},{129,193},{193,1... | collective-permute-start | bytes 221192 | tf_op jit(solution)/shard_map/ppermute | solution.py:445
  144.5 25.4 %all-to-all-start = ((f32[64,8,128]{2,1,0:T(8,128)}), f32[64,8,128]{2,1,0:T(8,128)S(1)}, u32[]{:S(2)}, u32[]{:S(2)}) async-start(f32[64,8,128]{2,1,0:T(8,128)} %get-tuple-element.54), calls=%async_computation | async-start | bytes 524288 | tf_op jit(solution)/shard_map/all_to_all | solution.py:517
  156.5 10.5 %collective-permute-start.38 = (f32[8,16,128]{2,1,0:T(8,128)S(1)}, f32[8,16,128]{2,1,0:T(8,128)S(1)}, u32[]{:S(2)}, u32[]{:S(2)}) collective-permute-start(f32[8,16,128]{2,1,0:T(8,128)S(1)} %get-tuple-element.50.r0), channel_id=1, source_target_pairs={{0,8},{8,0},{1,9},{9,1},{2,10},{10,2},{3,11},{11,3},{4,12},{12,4},... | collective-permute-start | bytes 196616 | tf_op jit(solution)/shard_map/ppermute | solution.py:520
  156.9 8.3 %collective-permute-start.37 = (f32[8,16,128]{2,1,0:T(8,128)S(1)}, f32[8,16,128]{2,1,0:T(8,128)S(1)}, u32[]{:S(2)}, u32[]{:S(2)}) collective-permute-start(f32[8,16,128]{2,1,0:T(8,128)S(1)} %get-tuple-element.50.r0), channel_id=1, source_target_pairs={{0,32},{16,48},{32,0},{48,16},{1,33},{17,49},{33,1},{49,17},{2,34}... | collective-permute-start | bytes 196616 | tf_op jit(solution)/shard_map/ppermute | solution.py:445
  159.8 6.7 %collective-permute-start.36 = (f32[8,16,128]{2,1,0:T(8,128)S(1)}, f32[8,16,128]{2,1,0:T(8,128)S(1)}, u32[]{:S(2)}, u32[]{:S(2)}) collective-permute-start(f32[8,16,128]{2,1,0:T(8,128)S(1)} %get-tuple-element.50.r0), channel_id=1, source_target_pairs={{0,16},{16,32},{32,48},{48,0},{1,17},{17,33},{33,49},{49,1},{2,18}... | collective-permute-start | bytes 196616 | tf_op jit(solution)/shard_map/ppermute | solution.py:445
  160.1 5.2 %collective-permute-start.35 = (f32[8,16,128]{2,1,0:T(8,128)S(1)}, f32[8,16,128]{2,1,0:T(8,128)S(1)}, u32[]{:S(2)}, u32[]{:S(2)}) collective-permute-start(f32[8,16,128]{2,1,0:T(8,128)S(1)} %get-tuple-element.50.r0), channel_id=1, source_target_pairs={{0,48},{16,0},{32,16},{48,32},{1,49},{17,1},{33,17},{49,33},{2,50}... | collective-permute-start | bytes 196616 | tf_op jit(solution)/shard_map/ppermute | solution.py:445
  165.3 2.1 %collective-permute-start.40 = (f32[8,16,128]{2,1,0:T(8,128)S(1)}, f32[8,16,128]{2,1,0:T(8,128)S(1)}, u32[]{:S(2)}, u32[]{:S(2)}) collective-permute-start(f32[8,16,128]{2,1,0:T(8,128)S(1)} %collective-permute-done.37.r2), channel_id=1, source_target_pairs={{0,8},{8,0},{1,9},{9,1},{2,10},{10,2},{3,11},{11,3},{4,12},{12,4},... | collective-permute-start | bytes 196616 | tf_op jit(solution)/shard_map/ppermute | solution.py:520
  166.4 1.3 collective-permute-start.39
  166.5 1.3 collective-permute-start.41

commit v4 on v3

--- a/solution.py
+++ b/solution.py
@@ -14,7 +14,8 @@
 BR = 64
 NB = 320
 GROUP = 32
-SHARERS = 64
+SHARERS = 32
+AHEAD = 1
 DOC = ("zl", "x", "c")
 TERM = ("y", "zh")
 F32 = jnp.float32
@@ -173,12 +174,19 @@
     ]
     for copy in small:
         copy.start()
-    for i in range(groups):
-        part = pl.ds(i * GROUP, GROUP)
-        pltpu.make_async_copy(blocks.at[0, part], held.at[part], sems.at[i]).start()
+    large = [
+        pltpu.make_async_copy(
+            blocks.at[0, pl.ds(i * GROUP, GROUP)], held.at[pl.ds(i * GROUP, GROUP)], sems.at[i]
+        )
+        for i in range(groups)
+    ]
+    for copy in large[:AHEAD]:
+        copy.start()
     acc[...] = jnp.zeros_like(acc)
     for copy in small:
         copy.wait()
+    for copy in large[AHEAD:]:
+        copy.start()
 
     def prepare(i):
         value = stacked(start[:, pl.ds(pl.multiple_of(i * BLK, BLK), BLK)])
@@ -325,9 +333,7 @@
         gram = gram + cross(wide, wide)
         mixed = mixed + cross(wide, prior[first + i])
     both = jnp.concatenate([fold(gram), fold(mixed)], axis=1)
-    ext_out[...] = jnp.broadcast_to(
-        jnp.concatenate([both[0:8], both[8:16], jnp.zeros((8, 64), F32)], axis=1)[None], (SHARERS, 8, BLK)
-    )
+    ext_out[...] = jnp.concatenate([both[0:8], both[8:16], jnp.zeros((8, BLK - 4 * K), F32)], axis=1)
 
 
 def lanes(index):
@@ -510,13 +516,14 @@
     )
     right2_chunk, ext, ml2, h2 = call(
         right_second, (*scatter_doc(own, other), right_chunk, prior),
-        (panel(8), jax.ShapeDtypeStruct((SHARERS, 8, BLK), F32), SMALL, SMALL),
+        (panel(8), jax.ShapeDtypeStruct((8, BLK), F32), SMALL, SMALL),
         [VMEM((4, 9, K, BLK), F32)], docs=docs,
     )
     mine = gather(right2_chunk, "x")
-    ext = lax.all_to_all(ext, ("c", "x", "y", "zh"), 0, 0)
     left_out = call(left_result, (*left1, *left2, ml1, ml2, h2), WIDE)
-    mine[3], left_out = lax.optimization_barrier((mine[3], left_out))
+    ext = ext + lax.ppermute(ext, "zh", SWAP)
+    ext, left_out, *mine = lax.optimization_barrier((ext, left_out, *mine))
+    ext = lax.all_to_all(jnp.broadcast_to(ext[None], (SHARERS, 8, BLK)), ("c", "x", "y"), 0, 0)
     right2 = mine + [lax.ppermute(m, "c", SWAP) for m in mine]
     right_out = call(right_result, (ext, *right2, prior), WIDE, terms=terms)
     return left_out, right_out

time: 172 us -> 173 us (level)
  starting transfers between devices: 97.6 us -> 77.7 us
  waiting for transfers between devices: 46.1 us -> 58.7 us
  Pallas kernels: 26.8 us -> 34.7 us
    ppermute x30, starting transfers between devices: 58.6 us -> 36.6 us  [shift(): return lax.ppermute(value, axis, [(i, (i + k) % 4) for i in range(4)])]
    pallas_call x11, Pallas kernels: 26.8 us -> 34.7 us  [call(): pl.pallas_call(functools.partial(body, **constants) if constants else bod...]
    ppermute x30, waiting for transfers between devices: 34 us -> 41 us  [shift(): return lax.ppermute(value, axis, [(i, (i + k) % 4) for i in range(4)])]
    all_to_all x1, waiting for transfers between devices: 2.07 us -> 5.45 us  [local(): lax.all_to_all(jnp.broadcast_to(ext[None], (SHARERS, 8, BLK)), ('c', 'x',...]
    all_to_all x1, starting transfers between devices: 12 us -> 9.99 us  [local(): lax.all_to_all(jnp.broadcast_to(ext[None], (SHARERS, 8, BLK)), ('c', 'x',...]
    ppermute x0 -> x1, starting transfers between devices: none -> 1.76 us  [local(): ext = ext + lax.ppermute(ext, 'zh', SWAP)]
    ppermute x0 -> x1, waiting for transfers between devices: none -> 1.76 us  [local(): ext = ext + lax.ppermute(ext, 'zh', SWAP)]
  transfers between devices with their start and end apart: 43 -> 44, of which waited for: 25 -> 30; matrix products, arithmetic and copies ran while one was open for 0% -> 0% of each run, Pallas kernels for 3% -> 3%
where the time goes in v4:
time: 173 us
  starting transfers between devices  77.7 us (45%)
  waiting for transfers between devices  58.7 us (34%)
  Pallas kernels  34.7 us (20%)
    ppermute x30, waiting for transfers between devices, shift(): return lax.ppermute(value, axis, [(i, (i + k) % 4) for i in range(4)])  41 us
    ppermute x30, starting transfers between devices, shift(): return lax.ppermute(value, axis, [(i, (i + k) % 4) for i in range(4)])  36.6 us
    pallas_call x11, Pallas kernels, call(): pl.pallas_call(functools.partial(body, **constants) if constants else bod...  34.7 us
    ppermute x2, starting transfers between devices, scatter_term(): return (mine, lax.ppermute(mine, 'zh', SWAP))  12.5 us
    all_to_all x1, starting transfers between devices, local(): lax.all_to_all(jnp.broadcast_to(ext[None], (SHARERS, 8, BLK)), ('c', 'x',...  9.99 us
    ppermute x4, starting transfers between devices, gather_doc(): return mine + [lax.ppermute(m, 'c', SWAP) for m in mine]  9.24 us
    ppermute x2, starting transfers between devices, scatter_doc(): got = lax.ppermute(other, 'c', SWAP)  6.52 us
    ppermute x2, waiting for transfers between devices, scatter_term(): return (mine, lax.ppermute(mine, 'zh', SWAP))  6.21 us
  transfers between devices with their start and end apart: 44, of which 30 were waited for; matrix products, arithmetic and copies ran while one was open for 0% of the time, Pallas kernels for 3%

profile of v4, /device:TPU:1, one launch (start us, length us, event | category | flops | bytes accessed | tf_op | source)
XLA Modules:
  0.0 173.4 jit_solution(15890575689321130675)
XLA Ops:
  1.3 7.3 %first_forward.1 = (f32[17,16,128]{2,1,0:T(8,128)S(1)}, f32[17,16,128]{2,1,0:T(8,128)S(1)}, f32[17,16,128]{2,1,0:T(8,128)S(1)}, f32[17,16,128]{2,1,0:T(8,128)S(1...) custom-call(s32[1,320]{1,0:T(1,128)} %rows.5, s32[1,320]{1,0:T(1,128)} %cols.5, ...), custom_call_target="tpu_custom_call" | custom-call | flops 2000000000 | bytes 2000000 | tf_op jit(solution)/shard_map/first_forward/pallas_call | solution.py:433
  8.7 2.4 %collective-permute-start.1 = (f32[17,16,128]{2,1,0:T(8,128)S(1)}, f32[17,16,128]{2,1,0:T(8,128)S(1)}, u32[]{:S(2)}, u32[]{:S(2)}) collective-permute-start(f32[17,16,128]{2,1,0:T(8,128)S(1)} %get-tuple-element.35), channel_id=1, source_target_pairs={{0,4},{2,6},{4,0},{6,2},{1,5},{3,7},{5,1},{7,3},{8,12},{10,14},{12... | collective-permute-start | bytes 417800 | tf_op jit(solution)/shard_map/ppermute | solution.py:451
  11.1 1.1 collective-permute-start.2
  12.2 3.1 %collective-permute-done = f32[17,16,128]{2,1,0:T(8,128)S(1)} collective-permute-done((f32[17,16,128]{2,1,0:T(8,128)S(1)}, f32[17,16,128]{2,1,0:T(8,128)S(1)}, u32[]{:S(2)}, u32[]{:S(2)}) %collective-permute-start) | collective-permute-done | bytes 139296 | tf_op jit(solution)/shard_map/ppermute | solution.py:451
  15.3 0.6 collective-permute-done.2
  15.9 8.3 %collective-permute-start.3 = (f32[17,16,128]{2,1,0:T(8,128)S(1)}, f32[17,16,128]{2,1,0:T(8,128)S(1)}, u32[]{:S(2)}, u32[]{:S(2)}) collective-permute-start(f32[17,16,128]{2,1,0:T(8,128)S(1)} %add_add_fusion.1.mine), channel_id=1, source_target_pairs={{0,1},{1,0},{2,3},{3,2},{4,5},{5,4},{6,7},{7,6},{8,9},{9,8},{10,11... | collective-permute-start | bytes 417800 | tf_op jit(solution)/shard_map/ppermute | solution.py:465
  24.3 2.4 %collective-permute-done.3.theirs = f32[17,16,128]{2,1,0:T(8,128)S(1)} collective-permute-done((f32[17,16,128]{2,1,0:T(8,128)S(1)}, f32[17,16,128]{2,1,0:T(8,128)S(1)}, u32[]{:S(2)}, u32[]{:S(2)}) %collective-permute-start.3) | collective-permute-done | bytes 139296 | tf_op jit(solution)/shard_map/ppermute | solution.py:465
  26.7 0.8 left_first.1
  27.5 2.2 %collective-permute-start.6 = (f32[17,16,128]{2,1,0:T(8,128)S(1)}, f32[17,16,128]{2,1,0:T(8,128)S(1)}, u32[]{:S(2)}, u32[]{:S(2)}) collective-permute-start(f32[17,16,128]{2,1,0:T(8,128)S(1)} %get-tuple-element.37.p0.left_raw.a0), channel_id=1, source_target_pairs={{0,6},{2,0},{4,2},{6,4},{1,7},{3,1},{5,3},{7,5},{8,14},{10,8},{12,... | collective-permute-start | bytes 417800 | tf_op jit(solution)/shard_map/ppermute | solution.py:451
  29.7 0.9 collective-permute-start.5
  30.6 2.6 %collective-permute-done.6.p3.a3 = f32[17,16,128]{2,1,0:T(8,128)S(1)} collective-permute-done((f32[17,16,128]{2,1,0:T(8,128)S(1)}, f32[17,16,128]{2,1,0:T(8,128)S(1)}, u32[]{:S(2)}, u32[]{:S(2)}) %collective-permute-start.6) | collective-permute-done | bytes 139296 | tf_op jit(solution)/shard_map/ppermute | solution.py:451
  33.2 2.0 %collective-permute-done.5.p2.a2 = f32[17,16,128]{2,1,0:T(8,128)S(1)} collective-permute-done((f32[17,16,128]{2,1,0:T(8,128)S(1)}, f32[17,16,128]{2,1,0:T(8,128)S(1)}, u32[]{:S(2)}, u32[]{:S(2)}) %collective-permute-start.5) | collective-permute-done | bytes 139296 | tf_op jit(solution)/shard_map/ppermute | solution.py:451
  35.2 1.4 collective-permute-done.4.p1.a1
  36.6 5.1 %backward.2 = (f32[36,16,128]{2,1,0:T(8,128)S(1)}, f32[36,16,128]{2,1,0:T(8,128)S(1)}) custom-call(s32[1,320]{1,0:T(1,128)S(1)} %copy-done.1, s32[1,320]{1,0:T(1,128)S(1)} %copy-done.2, s32[1,1]{1,0:T(1,128)S(6)} %copy.7.counts_any.counts, f32[17,16,128]{2,1,0:T(8,128)S(1)} %get-tuple-element.37.p0.left_raw.a0, ...), custom_call_target="tpu_custom_call" | custom-call | flops 2000000000 | bytes 2000000 | tf_op jit(solution)/shard_map/backward/pallas_call | solution.py:433
  41.7 5.6 %collective-permute-start.7 = (f32[36,16,128]{2,1,0:T(8,128)S(1)}, f32[36,16,128]{2,1,0:T(8,128)S(1)}, u32[]{:S(2)}, u32[]{:S(2)}) collective-permute-start(f32[36,16,128]{2,1,0:T(8,128)S(1)} %get-tuple-element.40), channel_id=1, source_target_pairs={{0,8},{8,0},{1,9},{9,1},{2,10},{10,2},{3,11},{11,3},{4,12},{12,4},... | collective-permute-start | bytes 884744 | tf_op jit(solution)/shard_map/ppermute | solution.py:469
  47.3 1.2 collective-permute-done.7
  48.6 3.9 %collective-permute-start.10 = (f32[9,16,128]{2,1,0:T(8,128)S(1)}, f32[9,16,128]{2,1,0:T(8,128)S(1)}, u32[]{:S(2)}, u32[]{:S(2)}) collective-permute-start(f32[9,16,128]{2,1,0:T(8,128)S(1)} %get-tuple-element.68), channel_id=1, source_target_pairs={{0,48},{16,0},{32,16},{48,32},{1,49},{17,1},{33,17},{49,33},{2,50}... | collective-permute-start | bytes 221192 | tf_op jit(solution)/shard_map/ppermute | solution.py:451
  52.5 1.1 collective-permute-start.9
  53.6 1.2 collective-permute-done.8
  54.8 2.5 %collective-permute-done.9 = f32[9,16,128]{2,1,0:T(8,128)S(1)} collective-permute-done((f32[9,16,128]{2,1,0:T(8,128)S(1)}, f32[9,16,128]{2,1,0:T(8,128)S(1)}, u32[]{:S(2)}, u32[]{:S(2)}) %collective-permute-start.9) | collective-permute-done | bytes 73760 | tf_op jit(solution)/shard_map/ppermute | solution.py:451
  57.3 0.6 collective-permute-start.13
  57.9 4.4 %collective-permute-start.12 = (f32[9,16,128]{2,1,0:T(8,128)S(1)}, f32[9,16,128]{2,1,0:T(8,128)S(1)}, u32[]{:S(2)}, u32[]{:S(2)}) collective-permute-start(f32[9,16,128]{2,1,0:T(8,128)S(1)} %fusion.5.t0), channel_id=1, source_target_pairs={{0,128},{64,192},{128,0},{192,64},{1,129},{65,193},{129,1},{193,65... | collective-permute-start | bytes 221192 | tf_op jit(solution)/shard_map/ppermute | solution.py:451
  62.3 0.3 collective-permute-start.11
  62.8 2.8 %collective-permute-done.12.t2 = f32[9,16,128]{2,1,0:T(8,128)S(1)} collective-permute-done((f32[9,16,128]{2,1,0:T(8,128)S(1)}, f32[9,16,128]{2,1,0:T(8,128)S(1)}, u32[]{:S(2)}, u32[]{:S(2)}) %collective-permute-start.12) | collective-permute-done | bytes 73760 | tf_op jit(solution)/shard_map/ppermute | solution.py:451
  65.6 2.4 %collective-permute-done.11.t1 = f32[9,16,128]{2,1,0:T(8,128)S(1)} collective-permute-done((f32[9,16,128]{2,1,0:T(8,128)S(1)}, f32[9,16,128]{2,1,0:T(8,128)S(1)}, u32[]{:S(2)}, u32[]{:S(2)}) %collective-permute-start.11) | collective-permute-done | bytes 73760 | tf_op jit(solution)/shard_map/ppermute | solution.py:451
  68.0 1.1 right_first.1
  69.1 1.2 collective-permute-start.16
  70.4 0.8 collective-permute-start.15
  71.2 3.5 %collective-permute-start.17 = (f32[9,16,128]{2,1,0:T(8,128)S(1)}, f32[9,16,128]{2,1,0:T(8,128)S(1)}, u32[]{:S(2)}, u32[]{:S(2)}) collective-permute-start(f32[9,16,128]{2,1,0:T(8,128)S(1)} %get-tuple-element.42.r0.right_raw), channel_id=1, source_target_pairs={{0,8},{8,0},{1,9},{9,1},{2,10},{10,2},{3,11},{11,3},{4,12},{12,4},... | collective-permute-start | bytes 221192 | tf_op jit(solution)/shard_map/ppermute | solution.py:477
  74.8 1.8 %collective-permute-start.20 = (f32[9,16,128]{2,1,0:T(8,128)S(1)}, f32[9,16,128]{2,1,0:T(8,128)S(1)}, u32[]{:S(2)}, u32[]{:S(2)}) collective-permute-start(f32[9,16,128]{2,1,0:T(8,128)S(1)} %collective-permute-done.16.r3), channel_id=1, source_target_pairs={{0,8},{8,0},{1,9},{9,1},{2,10},{10,2},{3,11},{11,3},{4,12},{12,4},... | collective-permute-start | bytes 221192 | tf_op jit(solution)/shard_map/ppermute | solution.py:477
  76.5 3.2 %collective-permute-start.19 = (f32[9,16,128]{2,1,0:T(8,128)S(1)}, f32[9,16,128]{2,1,0:T(8,128)S(1)}, u32[]{:S(2)}, u32[]{:S(2)}) collective-permute-start(f32[9,16,128]{2,1,0:T(8,128)S(1)} %collective-permute-done.15.r2), channel_id=1, source_target_pairs={{0,8},{8,0},{1,9},{9,1},{2,10},{10,2},{3,11},{11,3},{4,12},{12,4},... | collective-permute-start | bytes 221192 | tf_op jit(solution)/shard_map/ppermute | solution.py:477
  79.7 0.7 collective-permute-start.18
  80.6 0.7 collective-permute-done.18.w1
  81.4 5.0 %forward.1 = (f32[17,16,128]{2,1,0:T(8,128)S(1)}, f32[17,16,128]{2,1,0:T(8,128)S(1)}, f32[17,16,128]{2,1,0:T(8,128)S(1)}, f32[17,16,128]{2,1,0:T(8,128)S(1)}) custom-call(s32[1,320]{1,0:T(1,128)S(1)} %copy-done.1, s32[1,320]{1,0:T(1,128)S(1)} %copy-done.2, s32[1,1]{1,0:T(1,128)S(6)} %copy.7.counts_any.counts, ...), custom_call_target="tpu_custom_call" | custom-call | flops 2000000000 | bytes 2000000 | tf_op jit(solution)/shard_map/forward/pallas_call | solution.py:433
  86.6 2.6 %collective-permute-start.23 = (f32[17,16,128]{2,1,0:T(8,128)S(1)}, f32[17,16,128]{2,1,0:T(8,128)S(1)}, u32[]{:S(2)}, u32[]{:S(2)}) collective-permute-start(f32[17,16,128]{2,1,0:T(8,128)S(1)} %get-tuple-element.47), channel_id=1, source_target_pairs={{0,6},{2,0},{4,2},{6,4},{1,7},{3,1},{5,3},{7,5},{8,14},{10,8},{12,... | collective-permute-start | bytes 417800 | tf_op jit(solution)/shard_map/ppermute | solution.py:451
  89.2 6.7 %collective-permute-done.21 = f32[17,16,128]{2,1,0:T(8,128)S(1)} collective-permute-done((f32[17,16,128]{2,1,0:T(8,128)S(1)}, f32[17,16,128]{2,1,0:T(8,128)S(1)}, u32[]{:S(2)}, u32[]{:S(2)}) %collective-permute-start.21) | collective-permute-done | bytes 139296 | tf_op jit(solution)/shard_map/ppermute | solution.py:451
  96.0 4.1 %collective-permute-start.24 = (f32[17,16,128]{2,1,0:T(8,128)S(1)}, f32[17,16,128]{2,1,0:T(8,128)S(1)}, u32[]{:S(2)}, u32[]{:S(2)}) collective-permute-start(f32[17,16,128]{2,1,0:T(8,128)S(1)} %add_add_fusion.mine), channel_id=1, source_target_pairs={{0,1},{1,0},{2,3},{3,2},{4,5},{5,4},{6,7},{7,6},{8,9},{9,8},{10,11... | collective-permute-start | bytes 417800 | tf_op jit(solution)/shard_map/ppermute | solution.py:465
  100.1 3.8 %collective-permute-done.24.theirs = f32[17,16,128]{2,1,0:T(8,128)S(1)} collective-permute-done((f32[17,16,128]{2,1,0:T(8,128)S(1)}, f32[17,16,128]{2,1,0:T(8,128)S(1)}, u32[]{:S(2)}, u32[]{:S(2)}) %collective-permute-start.24) | collective-permute-done | bytes 139296 | tf_op jit(solution)/shard_map/ppermute | solution.py:465
  103.9 1.3 left_second.1
  105.2 7.2 %collective-permute-start.27 = (f32[17,16,128]{2,1,0:T(8,128)S(1)}, f32[17,16,128]{2,1,0:T(8,128)S(1)}, u32[]{:S(2)}, u32[]{:S(2)}) collective-permute-start(f32[17,16,128]{2,1,0:T(8,128)S(1)} %get-tuple-element.49.p0.b0), channel_id=1, source_target_pairs={{0,6},{2,0},{4,2},{6,4},{1,7},{3,1},{5,3},{7,5},{8,14},{10,8},{12,... | collective-permute-start | bytes 417800 | tf_op jit(solution)/shard_map/ppermute | solution.py:451
  112.4 0.7 collective-permute-start.25
  113.0 4.8 %collective-permute-done.27.p3.b3 = f32[17,16,128]{2,1,0:T(8,128)S(1)} collective-permute-done((f32[17,16,128]{2,1,0:T(8,128)S(1)}, f32[17,16,128]{2,1,0:T(8,128)S(1)}, u32[]{:S(2)}, u32[]{:S(2)}) %collective-permute-start.27) | collective-permute-done | bytes 139296 | tf_op jit(solution)/shard_map/ppermute | solution.py:451
  117.9 3.9 %collective-permute-done.25.p1.b1 = f32[17,16,128]{2,1,0:T(8,128)S(1)} collective-permute-done((f32[17,16,128]{2,1,0:T(8,128)S(1)}, f32[17,16,128]{2,1,0:T(8,128)S(1)}, u32[]{:S(2)}, u32[]{:S(2)}) %collective-permute-start.25) | collective-permute-done | bytes 139296 | tf_op jit(solution)/shard_map/ppermute | solution.py:451
  121.8 5.1 %backward.3 = (f32[36,16,128]{2,1,0:T(8,128)S(1)}, f32[36,16,128]{2,1,0:T(8,128)S(1)}) custom-call(s32[1,320]{1,0:T(1,128)S(1)} %copy-done.1, s32[1,320]{1,0:T(1,128)S(1)} %copy-done.2, s32[1,1]{1,0:T(1,128)S(6)} %copy.7.counts_any.counts, f32[17,16,128]{2,1,0:T(8,128)S(1)} %get-tuple-element.49.p0.b0, f32[17,16,128]{2,1,0:T(8,128)S(1)} %collective-permute-done.25.p1.b1, ...), custom_call_target="tpu_custom_call" | custom-call | flops 2000000000 | bytes 2000000 | tf_op jit(solution)/shard_map/backward/pallas_call | solution.py:433
  126.9 1.0 collective-permute-start.28
  127.9 1.2 collective-permute-done.28
  129.2 2.7 %collective-permute-start.31 = (f32[9,16,128]{2,1,0:T(8,128)S(1)}, f32[9,16,128]{2,1,0:T(8,128)S(1)}, u32[]{:S(2)}, u32[]{:S(2)}) collective-permute-start(f32[9,16,128]{2,1,0:T(8,128)S(1)} %get-tuple-element.65), channel_id=1, source_target_pairs={{0,48},{16,0},{32,16},{48,32},{1,49},{17,1},{33,17},{49,33},{2,50}... | collective-permute-start | bytes 221192 | tf_op jit(solution)/shard_map/ppermute | solution.py:451
  131.9 1.7 collective-permute-done.29
  133.6 1.3 collective-permute-done.31
  134.9 1.7 collective-permute-done.30
  136.8 1.4 collective-permute-start.32
  138.1 2.7 %right_prior.1.prior.right1 = bf16[64,48,128]{2,1,0:T(8,128)(2,1)S(1)} custom-call(f32[9,16,128]{2,1,0:T(8,128)S(1)} %get-tuple-element.42.r0.right_raw, f32[9,16,128]{2,1,0:T(8,128)S(1)} %collective-permute-done.14.r1, f32[9,16,128]{2,1,0:T(8,128)S(1)} %collective-permute-done.15.r2, f32[9,16,128]{2,1,0:T(8,128)S(1)} %collective-permute-done.16.r3, ...), custom_call_target="tpu_custom_call" | custom-call | flops 2000000000 | bytes 2000000 | tf_op jit(solution)/shard_map/right_prior/pallas_call | solution.py:433
  140.9 2.0 %collective-permute-done.32.t1 = f32[9,16,128]{2,1,0:T(8,128)S(1)} collective-permute-done((f32[9,16,128]{2,1,0:T(8,128)S(1)}, f32[9,16,128]{2,1,0:T(8,128)S(1)}, u32[]{:S(2)}, u32[]{:S(2)}) %collective-permute-start.32) | collective-permute-done | bytes 73760 | tf_op jit(solution)/shard_map/ppermute | solution.py:451
  142.9 1.1 right_second.1
  144.0 1.9 %collective-permute-start.38 = (f32[8,16,128]{2,1,0:T(8,128)S(1)}, f32[8,16,128]{2,1,0:T(8,128)S(1)}, u32[]{:S(2)}, u32[]{:S(2)}) collective-permute-start(f32[8,16,128]{2,1,0:T(8,128)S(1)} %get-tuple-element.60.r0), channel_id=1, source_target_pairs={{0,48},{16,0},{32,16},{48,32},{1,49},{17,1},{33,17},{49,33},{2,50}... | collective-permute-start | bytes 196616 | tf_op jit(solution)/shard_map/ppermute | solution.py:451
  145.9 0.6 collective-permute-start.36
  146.5 1.8 %collective-permute-start.35 = (f32[8,128]{1,0:T(8,128)S(1)}, f32[8,128]{1,0:T(8,128)S(1)}, u32[]{:S(2)}, u32[]{:S(2)}) collective-permute-start(f32[8,128]{1,0:T(8,128)S(1)} %get-tuple-element.54), channel_id=1, source_target_pairs={{0,1},{1,0},{2,3},{3,2},{4,5},{5,4},{6,7},{7,6},{8,9},{9,8},{10,11... | collective-permute-start | bytes 12296 | tf_op jit(solution)/shard_map/ppermute | solution.py:524
  148.3 2.8 %left_result.1 = f32[16,8192]{1,0:T(8,128)} custom-call(f32[17,16,128]{2,1,0:T(8,128)S(1)} %get-tuple-element.37.p0.left_raw.a0, f32[17,16,128]{2,1,0:T(8,128)S(1)} %collective-permute-done.4.p1.a1, f32[17,16,128]{2,1,0:T(8,128)S(1)} %collective-permute-done.5.p2.a2, f32[17,16,128]{2,1,0:T(8,128)S(1)} %collective-permute-done.6.p3.a3, ...), custom_call_target="tpu_custom_call" | custom-call | flops 2000000000 | bytes 2000000 | tf_op jit(solution)/shard_map/left_result/pallas_call | solution.py:433
  151.2 1.8 %collective-permute-done.35 = f32[8,128]{1,0:T(8,128)S(1)} collective-permute-done((f32[8,128]{1,0:T(8,128)S(1)}, f32[8,128]{1,0:T(8,128)S(1)}, u32[]{:S(2)}, u32[]{:S(2)}) %collective-permute-start.35) | collective-permute-done | bytes 4128 | tf_op jit(solution)/shard_map/ppermute | solution.py:524
  152.9 0.7 broadcast_in_dim.2
  153.6 10.0 %all-to-all-start = ((f32[32,8,128]{2,1,0:T(8,128)}), f32[32,8,128]{2,1,0:T(8,128)S(1)}, u32[]{:S(2)}, u32[]{:S(2)}) async-start(f32[32,8,128]{2,1,0:T(8,128)} %broadcast_in_dim.2), calls=%async_computation | async-start | bytes 262144 | tf_op jit(solution)/shard_map/all_to_all | solution.py:526
  163.6 0.3 collective-permute-start.39
  165.7 5.5 %all-to-all-done.ext = f32[32,8,128]{2,1,0:T(8,128)S(1)} async-done(((f32[32,8,128]{2,1,0:T(8,128)}), f32[32,8,128]{2,1,0:T(8,128)S(1)}, u32[]{:S(2)}, u32[]{:S(2)}) %all-to-all-start) | async-done | bytes 131104 | tf_op jit(solution)/shard_map/all_to_all | solution.py:526
  171.1 2.3 %right_result.1 = f32[16,8192]{1,0:T(8,128)} custom-call(f32[32,8,128]{2,1,0:T(8,128)S(1)} %all-to-all-done.ext, f32[8,16,128]{2,1,0:T(8,128)S(1)} %get-tuple-element.60.r0, f32[8,16,128]{2,1,0:T(8,128)S(1)} %collective-permute-done.36.r1, f32[8,16,128]{2,1,0:T(8,128)S(1)} %collective-permute-done.37.r2, f32[8,16,128]{2,1,0:T(8,128)S(1)} %collective-permute-done.38.r3, ...), custom_call_target="tpu_custom_call" | custom-call | flops 2000000000 | bytes 2000000 | tf_op jit(solution)/shard_map/right_result/pallas_call | solution.py:433
  (49 shorter events, 3.1 us)
Async XLA Ops:
  0.6 36.0 %copy-start.2 = (s32[1,320]{1,0:T(1,128)S(1)}, s32[1,320]{1,0:T(1,128)}, u32[]{:S(2)}) copy-start(s32[1,320]{1,0:T(1,128)} %cols.5) | copy-start | bytes 3844
  0.6 36.0 %copy-start.1 = (s32[1,320]{1,0:T(1,128)S(1)}, s32[1,320]{1,0:T(1,128)}, u32[]{:S(2)}) copy-start(s32[1,320]{1,0:T(1,128)} %rows.5) | copy-start | bytes 3844
  8.6 59.4 %copy-start = (f32[16,8192]{1,0:T(8,128)S(1)}, f32[16,8192]{1,0:T(8,128)}, u32[]{:S(2)}) copy-start(f32[16,8192]{1,0:T(8,128)} %start.3) | copy-start | bytes 1572868
  8.6 6.7 %collective-permute-start = (f32[17,16,128]{2,1,0:T(8,128)S(1)}, f32[17,16,128]{2,1,0:T(8,128)S(1)}, u32[]{:S(2)}, u32[]{:S(2)}) collective-permute-start(f32[17,16,128]{2,1,0:T(8,128)S(1)} %get-tuple-element.34), channel_id=1, source_target_pairs={{0,2},{2,4},{4,6},{6,0},{1,3},{3,5},{5,7},{7,1},{8,10},{10,12},{12... | collective-permute-start | bytes 417800 | tf_op jit(solution)/shard_map/ppermute | solution.py:451
  8.7 6.6 %collective-permute-start.1 = (f32[17,16,128]{2,1,0:T(8,128)S(1)}, f32[17,16,128]{2,1,0:T(8,128)S(1)}, u32[]{:S(2)}, u32[]{:S(2)}) collective-permute-start(f32[17,16,128]{2,1,0:T(8,128)S(1)} %get-tuple-element.35), channel_id=1, source_target_pairs={{0,4},{2,6},{4,0},{6,2},{1,5},{3,7},{5,1},{7,3},{8,12},{10,14},{12... | collective-permute-start | bytes 417800 | tf_op jit(solution)/shard_map/ppermute | solution.py:451
  11.1 4.7 %collective-permute-start.2 = (f32[17,16,128]{2,1,0:T(8,128)S(1)}, f32[17,16,128]{2,1,0:T(8,128)S(1)}, u32[]{:S(2)}, u32[]{:S(2)}) collective-permute-start(f32[17,16,128]{2,1,0:T(8,128)S(1)} %get-tuple-element.36), channel_id=1, source_target_pairs={{0,6},{2,0},{4,2},{6,4},{1,7},{3,1},{5,3},{7,5},{8,14},{10,8},{12,... | collective-permute-start | bytes 417800 | tf_op jit(solution)/shard_map/ppermute | solution.py:451
  15.9 10.8 %collective-permute-start.3 = (f32[17,16,128]{2,1,0:T(8,128)S(1)}, f32[17,16,128]{2,1,0:T(8,128)S(1)}, u32[]{:S(2)}, u32[]{:S(2)}) collective-permute-start(f32[17,16,128]{2,1,0:T(8,128)S(1)} %add_add_fusion.1.mine), channel_id=1, source_target_pairs={{0,1},{1,0},{2,3},{3,2},{4,5},{5,4},{6,7},{7,6},{8,9},{9,8},{10,11... | collective-permute-start | bytes 417800 | tf_op jit(solution)/shard_map/ppermute | solution.py:465
  27.5 5.7 %collective-permute-start.6 = (f32[17,16,128]{2,1,0:T(8,128)S(1)}, f32[17,16,128]{2,1,0:T(8,128)S(1)}, u32[]{:S(2)}, u32[]{:S(2)}) collective-permute-start(f32[17,16,128]{2,1,0:T(8,128)S(1)} %get-tuple-element.37.p0.left_raw.a0), channel_id=1, source_target_pairs={{0,6},{2,0},{4,2},{6,4},{1,7},{3,1},{5,3},{7,5},{8,14},{10,8},{12,... | collective-permute-start | bytes 417800 | tf_op jit(solution)/shard_map/ppermute | solution.py:451
  29.7 5.5 %collective-permute-start.5 = (f32[17,16,128]{2,1,0:T(8,128)S(1)}, f32[17,16,128]{2,1,0:T(8,128)S(1)}, u32[]{:S(2)}, u32[]{:S(2)}) collective-permute-start(f32[17,16,128]{2,1,0:T(8,128)S(1)} %get-tuple-element.37.p0.left_raw.a0), channel_id=1, source_target_pairs={{0,4},{2,6},{4,0},{6,2},{1,5},{3,7},{5,1},{7,3},{8,12},{10,14},{12... | collective-permute-start | bytes 417800 | tf_op jit(solution)/shard_map/ppermute | solution.py:451
  30.6 6.0 %collective-permute-start.4 = (f32[17,16,128]{2,1,0:T(8,128)S(1)}, f32[17,16,128]{2,1,0:T(8,128)S(1)}, u32[]{:S(2)}, u32[]{:S(2)}) collective-permute-start(f32[17,16,128]{2,1,0:T(8,128)S(1)} %get-tuple-element.37.p0.left_raw.a0), channel_id=1, source_target_pairs={{0,2},{2,4},{4,6},{6,0},{1,3},{3,5},{5,7},{7,1},{8,10},{10,12},{12... | collective-permute-start | bytes 417800 | tf_op jit(solution)/shard_map/ppermute | solution.py:451
  41.7 6.8 %collective-permute-start.7 = (f32[36,16,128]{2,1,0:T(8,128)S(1)}, f32[36,16,128]{2,1,0:T(8,128)S(1)}, u32[]{:S(2)}, u32[]{:S(2)}) collective-permute-start(f32[36,16,128]{2,1,0:T(8,128)S(1)} %get-tuple-element.40), channel_id=1, source_target_pairs={{0,8},{8,0},{1,9},{9,1},{2,10},{10,2},{3,11},{11,3},{4,12},{12,4},... | collective-permute-start | bytes 884744 | tf_op jit(solution)/shard_map/ppermute | solution.py:469
  48.5 6.3 %collective-permute-start.8 = (f32[9,16,128]{2,1,0:T(8,128)S(1)}, f32[9,16,128]{2,1,0:T(8,128)S(1)}, u32[]{:S(2)}, u32[]{:S(2)}) collective-permute-start(f32[9,16,128]{2,1,0:T(8,128)S(1)} %get-tuple-element.67), channel_id=1, source_target_pairs={{0,16},{16,32},{32,48},{48,0},{1,17},{17,33},{33,49},{49,1},{2,18}... | collective-permute-start | bytes 221192 | tf_op jit(solution)/shard_map/ppermute | solution.py:451
  48.6 6.2 %collective-permute-start.10 = (f32[9,16,128]{2,1,0:T(8,128)S(1)}, f32[9,16,128]{2,1,0:T(8,128)S(1)}, u32[]{:S(2)}, u32[]{:S(2)}) collective-permute-start(f32[9,16,128]{2,1,0:T(8,128)S(1)} %get-tuple-element.68), channel_id=1, source_target_pairs={{0,48},{16,0},{32,16},{48,32},{1,49},{17,1},{33,17},{49,33},{2,50}... | collective-permute-start | bytes 221192 | tf_op jit(solution)/shard_map/ppermute | solution.py:451
  52.5 4.7 %collective-permute-start.9 = (f32[9,16,128]{2,1,0:T(8,128)S(1)}, f32[9,16,128]{2,1,0:T(8,128)S(1)}, u32[]{:S(2)}, u32[]{:S(2)}) collective-permute-start(f32[9,16,128]{2,1,0:T(8,128)S(1)} %get-tuple-element.69), channel_id=1, source_target_pairs={{0,32},{16,48},{32,0},{48,16},{1,33},{17,49},{33,1},{49,17},{2,34}... | collective-permute-start | bytes 221192 | tf_op jit(solution)/shard_map/ppermute | solution.py:451
  57.3 5.5 %collective-permute-start.13 = (f32[9,16,128]{2,1,0:T(8,128)S(1)}, f32[9,16,128]{2,1,0:T(8,128)S(1)}, u32[]{:S(2)}, u32[]{:S(2)}) collective-permute-start(f32[9,16,128]{2,1,0:T(8,128)S(1)} %fusion.5.t0), channel_id=1, source_target_pairs={{0,192},{64,0},{128,64},{192,128},{1,193},{65,1},{129,65},{193,129... | collective-permute-start | bytes 221192 | tf_op jit(solution)/shard_map/ppermute | solution.py:451
  57.9 7.8 %collective-permute-start.12 = (f32[9,16,128]{2,1,0:T(8,128)S(1)}, f32[9,16,128]{2,1,0:T(8,128)S(1)}, u32[]{:S(2)}, u32[]{:S(2)}) collective-permute-start(f32[9,16,128]{2,1,0:T(8,128)S(1)} %fusion.5.t0), channel_id=1, source_target_pairs={{0,128},{64,192},{128,0},{192,64},{1,129},{65,193},{129,1},{193,65... | collective-permute-start | bytes 221192 | tf_op jit(solution)/shard_map/ppermute | solution.py:451
  62.3 5.7 %collective-permute-start.11 = (f32[9,16,128]{2,1,0:T(8,128)S(1)}, f32[9,16,128]{2,1,0:T(8,128)S(1)}, u32[]{:S(2)}, u32[]{:S(2)}) collective-permute-start(f32[9,16,128]{2,1,0:T(8,128)S(1)} %fusion.5.t0), channel_id=1, source_target_pairs={{0,64},{64,128},{128,192},{192,0},{1,65},{65,129},{129,193},{193,1... | collective-permute-start | bytes 221192 | tf_op jit(solution)/shard_map/ppermute | solution.py:451
  69.1 5.6 %collective-permute-start.16 = (f32[9,16,128]{2,1,0:T(8,128)S(1)}, f32[9,16,128]{2,1,0:T(8,128)S(1)}, u32[]{:S(2)}, u32[]{:S(2)}) collective-permute-start(f32[9,16,128]{2,1,0:T(8,128)S(1)} %get-tuple-element.42.r0.right_raw), channel_id=1, source_target_pairs={{0,48},{16,0},{32,16},{48,32},{1,49},{17,1},{33,17},{49,33},{2,50}... | collective-permute-start | bytes 221192 | tf_op jit(solution)/shard_map/ppermute | solution.py:451
  70.4 6.2 %collective-permute-start.15 = (f32[9,16,128]{2,1,0:T(8,128)S(1)}, f32[9,16,128]{2,1,0:T(8,128)S(1)}, u32[]{:S(2)}, u32[]{:S(2)}) collective-permute-start(f32[9,16,128]{2,1,0:T(8,128)S(1)} %get-tuple-element.42.r0.right_raw), channel_id=1, source_target_pairs={{0,32},{16,48},{32,0},{48,16},{1,33},{17,49},{33,1},{49,17},{2,34}... | collective-permute-start | bytes 221192 | tf_op jit(solution)/shard_map/ppermute | solution.py:451
  71.2 8.5 %collective-permute-start.14 = (f32[9,16,128]{2,1,0:T(8,128)S(1)}, f32[9,16,128]{2,1,0:T(8,128)S(1)}, u32[]{:S(2)}, u32[]{:S(2)}) collective-permute-start(f32[9,16,128]{2,1,0:T(8,128)S(1)} %get-tuple-element.42.r0.right_raw), channel_id=1, source_target_pairs={{0,16},{16,32},{32,48},{48,0},{1,17},{17,33},{33,49},{49,1},{2,18}... | collective-permute-start | bytes 221192 | tf_op jit(solution)/shard_map/ppermute | solution.py:451
  71.2 9.3 %collective-permute-start.17 = (f32[9,16,128]{2,1,0:T(8,128)S(1)}, f32[9,16,128]{2,1,0:T(8,128)S(1)}, u32[]{:S(2)}, u32[]{:S(2)}) collective-permute-start(f32[9,16,128]{2,1,0:T(8,128)S(1)} %get-tuple-element.42.r0.right_raw), channel_id=1, source_target_pairs={{0,8},{8,0},{1,9},{9,1},{2,10},{10,2},{3,11},{11,3},{4,12},{12,4},... | collective-permute-start | bytes 221192 | tf_op jit(solution)/shard_map/ppermute | solution.py:477
  74.8 5.7 %collective-permute-start.20 = (f32[9,16,128]{2,1,0:T(8,128)S(1)}, f32[9,16,128]{2,1,0:T(8,128)S(1)}, u32[]{:S(2)}, u32[]{:S(2)}) collective-permute-start(f32[9,16,128]{2,1,0:T(8,128)S(1)} %collective-permute-done.16.r3), channel_id=1, source_target_pairs={{0,8},{8,0},{1,9},{9,1},{2,10},{10,2},{3,11},{11,3},{4,12},{12,4},... | collective-permute-start | bytes 221192 | tf_op jit(solution)/shard_map/ppermute | solution.py:477
  76.5 4.1 %collective-permute-start.19 = (f32[9,16,128]{2,1,0:T(8,128)S(1)}, f32[9,16,128]{2,1,0:T(8,128)S(1)}, u32[]{:S(2)}, u32[]{:S(2)}) collective-permute-start(f32[9,16,128]{2,1,0:T(8,128)S(1)} %collective-permute-done.15.r2), channel_id=1, source_target_pairs={{0,8},{8,0},{1,9},{9,1},{2,10},{10,2},{3,11},{11,3},{4,12},{12,4},... | collective-permute-start | bytes 221192 | tf_op jit(solution)/shard_map/ppermute | solution.py:477
  79.7 1.7 collective-permute-start.18
  86.4 9.5 %collective-permute-start.21 = (f32[17,16,128]{2,1,0:T(8,128)S(1)}, f32[17,16,128]{2,1,0:T(8,128)S(1)}, u32[]{:S(2)}, u32[]{:S(2)}) collective-permute-start(f32[17,16,128]{2,1,0:T(8,128)S(1)} %get-tuple-element.45), channel_id=1, source_target_pairs={{0,2},{2,4},{4,6},{6,0},{1,3},{3,5},{5,7},{7,1},{8,10},{10,12},{12... | collective-permute-start | bytes 417800 | tf_op jit(solution)/shard_map/ppermute | solution.py:451
  86.5 9.4 %collective-permute-start.22 = (f32[17,16,128]{2,1,0:T(8,128)S(1)}, f32[17,16,128]{2,1,0:T(8,128)S(1)}, u32[]{:S(2)}, u32[]{:S(2)}) collective-permute-start(f32[17,16,128]{2,1,0:T(8,128)S(1)} %get-tuple-element.46), channel_id=1, source_target_pairs={{0,4},{2,6},{4,0},{6,2},{1,5},{3,7},{5,1},{7,3},{8,12},{10,14},{12... | collective-permute-start | bytes 417800 | tf_op jit(solution)/shard_map/ppermute | solution.py:451
  86.6 9.3 %collective-permute-start.23 = (f32[17,16,128]{2,1,0:T(8,128)S(1)}, f32[17,16,128]{2,1,0:T(8,128)S(1)}, u32[]{:S(2)}, u32[]{:S(2)}) collective-permute-start(f32[17,16,128]{2,1,0:T(8,128)S(1)} %get-tuple-element.47), channel_id=1, source_target_pairs={{0,6},{2,0},{4,2},{6,4},{1,7},{3,1},{5,3},{7,5},{8,14},{10,8},{12,... | collective-permute-start | bytes 417800 | tf_op jit(solution)/shard_map/ppermute | solution.py:451
  96.0 7.9 %collective-permute-start.24 = (f32[17,16,128]{2,1,0:T(8,128)S(1)}, f32[17,16,128]{2,1,0:T(8,128)S(1)}, u32[]{:S(2)}, u32[]{:S(2)}) collective-permute-start(f32[17,16,128]{2,1,0:T(8,128)S(1)} %add_add_fusion.mine), channel_id=1, source_target_pairs={{0,1},{1,0},{2,3},{3,2},{4,5},{5,4},{6,7},{7,6},{8,9},{9,8},{10,11... | collective-permute-start | bytes 417800 | tf_op jit(solution)/shard_map/ppermute | solution.py:465
  105.2 12.7 %collective-permute-start.27 = (f32[17,16,128]{2,1,0:T(8,128)S(1)}, f32[17,16,128]{2,1,0:T(8,128)S(1)}, u32[]{:S(2)}, u32[]{:S(2)}) collective-permute-start(f32[17,16,128]{2,1,0:T(8,128)S(1)} %get-tuple-element.49.p0.b0), channel_id=1, source_target_pairs={{0,6},{2,0},{4,2},{6,4},{1,7},{3,1},{5,3},{7,5},{8,14},{10,8},{12,... | collective-permute-start | bytes 417800 | tf_op jit(solution)/shard_map/ppermute | solution.py:451
  112.4 5.5 %collective-permute-start.26 = (f32[17,16,128]{2,1,0:T(8,128)S(1)}, f32[17,16,128]{2,1,0:T(8,128)S(1)}, u32[]{:S(2)}, u32[]{:S(2)}) collective-permute-start(f32[17,16,128]{2,1,0:T(8,128)S(1)} %get-tuple-element.49.p0.b0), channel_id=1, source_target_pairs={{0,4},{2,6},{4,0},{6,2},{1,5},{3,7},{5,1},{7,3},{8,12},{10,14},{12... | collective-permute-start | bytes 417800 | tf_op jit(solution)/shard_map/ppermute | solution.py:451
  112.4 9.4 %collective-permute-start.25 = (f32[17,16,128]{2,1,0:T(8,128)S(1)}, f32[17,16,128]{2,1,0:T(8,128)S(1)}, u32[]{:S(2)}, u32[]{:S(2)}) collective-permute-start(f32[17,16,128]{2,1,0:T(8,128)S(1)} %get-tuple-element.49.p0.b0), channel_id=1, source_target_pairs={{0,2},{2,4},{4,6},{6,0},{1,3},{3,5},{5,7},{7,1},{8,10},{10,12},{12... | collective-permute-start | bytes 417800 | tf_op jit(solution)/shard_map/ppermute | solution.py:451
  126.9 2.2 %collective-permute-start.28 = (f32[36,16,128]{2,1,0:T(8,128)S(1)}, f32[36,16,128]{2,1,0:T(8,128)S(1)}, u32[]{:S(2)}, u32[]{:S(2)}) collective-permute-start(f32[36,16,128]{2,1,0:T(8,128)S(1)} %get-tuple-element.51), channel_id=1, source_target_pairs={{0,8},{8,0},{1,9},{9,1},{2,10},{10,2},{3,11},{11,3},{4,12},{12,4},... | collective-permute-start | bytes 884744 | tf_op jit(solution)/shard_map/ppermute | solution.py:469
  129.1 4.5 %collective-permute-start.29 = (f32[9,16,128]{2,1,0:T(8,128)S(1)}, f32[9,16,128]{2,1,0:T(8,128)S(1)}, u32[]{:S(2)}, u32[]{:S(2)}) collective-permute-start(f32[9,16,128]{2,1,0:T(8,128)S(1)} %get-tuple-element.64), channel_id=1, source_target_pairs={{0,16},{16,32},{32,48},{48,0},{1,17},{17,33},{33,49},{49,1},{2,18}... | collective-permute-start | bytes 221192 | tf_op jit(solution)/shard_map/ppermute | solution.py:451
  129.2 5.7 %collective-permute-start.31 = (f32[9,16,128]{2,1,0:T(8,128)S(1)}, f32[9,16,128]{2,1,0:T(8,128)S(1)}, u32[]{:S(2)}, u32[]{:S(2)}) collective-permute-start(f32[9,16,128]{2,1,0:T(8,128)S(1)} %get-tuple-element.65), channel_id=1, source_target_pairs={{0,48},{16,0},{32,16},{48,32},{1,49},{17,1},{33,17},{49,33},{2,50}... | collective-permute-start | bytes 221192 | tf_op jit(solution)/shard_map/ppermute | solution.py:451
  131.9 4.7 %collective-permute-start.30 = (f32[9,16,128]{2,1,0:T(8,128)S(1)}, f32[9,16,128]{2,1,0:T(8,128)S(1)}, u32[]{:S(2)}, u32[]{:S(2)}) collective-permute-start(f32[9,16,128]{2,1,0:T(8,128)S(1)} %get-tuple-element.66), channel_id=1, source_target_pairs={{0,32},{16,48},{32,0},{48,16},{1,33},{17,49},{33,1},{49,17},{2,34}... | collective-permute-start | bytes 221192 | tf_op jit(solution)/shard_map/ppermute | solution.py:451
  136.6 4.2 %collective-permute-start.34 = (f32[9,16,128]{2,1,0:T(8,128)S(1)}, f32[9,16,128]{2,1,0:T(8,128)S(1)}, u32[]{:S(2)}, u32[]{:S(2)}) collective-permute-start(f32[9,16,128]{2,1,0:T(8,128)S(1)} %fusion.2.t0), channel_id=1, source_target_pairs={{0,192},{64,0},{128,64},{192,128},{1,193},{65,1},{129,65},{193,129... | collective-permute-start | bytes 221192 | tf_op jit(solution)/shard_map/ppermute | solution.py:451
  136.7 4.2 %collective-permute-start.33 = (f32[9,16,128]{2,1,0:T(8,128)S(1)}, f32[9,16,128]{2,1,0:T(8,128)S(1)}, u32[]{:S(2)}, u32[]{:S(2)}) collective-permute-start(f32[9,16,128]{2,1,0:T(8,128)S(1)} %fusion.2.t0), channel_id=1, source_target_pairs={{0,128},{64,192},{128,0},{192,64},{1,129},{65,193},{129,1},{193,65... | collective-permute-start | bytes 221192 | tf_op jit(solution)/shard_map/ppermute | solution.py:451
  136.8 6.1 %collective-permute-start.32 = (f32[9,16,128]{2,1,0:T(8,128)S(1)}, f32[9,16,128]{2,1,0:T(8,128)S(1)}, u32[]{:S(2)}, u32[]{:S(2)}) collective-permute-start(f32[9,16,128]{2,1,0:T(8,128)S(1)} %fusion.2.t0), channel_id=1, source_target_pairs={{0,64},{64,128},{128,192},{192,0},{1,65},{65,129},{129,193},{193,1... | collective-permute-start | bytes 221192 | tf_op jit(solution)/shard_map/ppermute | solution.py:451
  144.0 8.9 %collective-permute-start.38 = (f32[8,16,128]{2,1,0:T(8,128)S(1)}, f32[8,16,128]{2,1,0:T(8,128)S(1)}, u32[]{:S(2)}, u32[]{:S(2)}) collective-permute-start(f32[8,16,128]{2,1,0:T(8,128)S(1)} %get-tuple-element.60.r0), channel_id=1, source_target_pairs={{0,48},{16,0},{32,16},{48,32},{1,49},{17,1},{33,17},{49,33},{2,50}... | collective-permute-start | bytes 196616 | tf_op jit(solution)/shard_map/ppermute | solution.py:451
  145.9 7.0 %collective-permute-start.37 = (f32[8,16,128]{2,1,0:T(8,128)S(1)}, f32[8,16,128]{2,1,0:T(8,128)S(1)}, u32[]{:S(2)}, u32[]{:S(2)}) collective-permute-start(f32[8,16,128]{2,1,0:T(8,128)S(1)} %get-tuple-element.60.r0), channel_id=1, source_target_pairs={{0,32},{16,48},{32,0},{48,16},{1,33},{17,49},{33,1},{49,17},{2,34}... | collective-permute-start | bytes 196616 | tf_op jit(solution)/shard_map/ppermute | solution.py:451
  145.9 7.0 %collective-permute-start.36 = (f32[8,16,128]{2,1,0:T(8,128)S(1)}, f32[8,16,128]{2,1,0:T(8,128)S(1)}, u32[]{:S(2)}, u32[]{:S(2)}) collective-permute-start(f32[8,16,128]{2,1,0:T(8,128)S(1)} %get-tuple-element.60.r0), channel_id=1, source_target_pairs={{0,16},{16,32},{32,48},{48,0},{1,17},{17,33},{33,49},{49,1},{2,18}... | collective-permute-start | bytes 196616 | tf_op jit(solution)/shard_map/ppermute | solution.py:451
  146.5 6.4 %collective-permute-start.35 = (f32[8,128]{1,0:T(8,128)S(1)}, f32[8,128]{1,0:T(8,128)S(1)}, u32[]{:S(2)}, u32[]{:S(2)}) collective-permute-start(f32[8,128]{1,0:T(8,128)S(1)} %get-tuple-element.54), channel_id=1, source_target_pairs={{0,1},{1,0},{2,3},{3,2},{4,5},{5,4},{6,7},{7,6},{8,9},{9,8},{10,11... | collective-permute-start | bytes 12296 | tf_op jit(solution)/shard_map/ppermute | solution.py:524
  153.6 17.5 %all-to-all-start = ((f32[32,8,128]{2,1,0:T(8,128)}), f32[32,8,128]{2,1,0:T(8,128)S(1)}, u32[]{:S(2)}, u32[]{:S(2)}) async-start(f32[32,8,128]{2,1,0:T(8,128)} %broadcast_in_dim.2), calls=%async_computation | async-start | bytes 262144 | tf_op jit(solution)/shard_map/all_to_all | solution.py:526
  163.6 1.3 collective-permute-start.39
  163.9 1.3 collective-permute-start.40
  164.2 1.3 collective-permute-start.41
  164.4 1.3 collective-permute-start.42

commit v5 on v4

--- a/solution.py
+++ b/solution.py
@@ -14,6 +14,7 @@
 BR = 64
 NB = 320
 GROUP = 32
+WIDER = 64
 SHARERS = 32
 AHEAD = 1
 DOC = ("zl", "x", "c")
@@ -87,7 +88,7 @@
     split_ref[index, 32:48, :] = low
 
 
-def each(count, body, unroll=4):
+def each(count, body, unroll=2):
     def step(i, carry):
         body(i)
         return carry
@@ -96,7 +97,7 @@
 
 
 def split_all(split_ref, base, piece, count):
-    each(count, lambda i: split_store(split_ref, base + i, piece[i]), 8)
+    each(count, lambda i: split_store(split_ref, base + i, piece[i]), 4)
 
 
 def cross(left, right):
@@ -117,9 +118,9 @@
     return jnp.bitwise_and(index - step, 3)
 
 
-def group_of(base, live, src_ref, tgt_ref, block, split, acc, place, spare):
+def group_of(size, base, live, src_ref, tgt_ref, block, split, acc, place, spare):
     spots, values = [], []
-    for u in range(GROUP):
+    for u in range(size):
         slot = base + u
         wide = jnp.dot(split[src_ref[0, slot]], block(slot), preferred_element_type=F32)
         values.append((wide[32:48, :] + wide[16:32, :]) + wide[0:16, :])
@@ -147,10 +148,10 @@
 
 def multiply(live, src_ref, tgt_ref, held, split, acc, place, spare):
     def step(g, carry):
-        group_of(g * GROUP, live, src_ref, tgt_ref, lambda s: held[s], split, acc, place, spare)
+        group_of(WIDER, g * WIDER, live, src_ref, tgt_ref, lambda s: held[s], split, acc, place, spare)
         return carry
 
-    lax.fori_loop(0, lax.div(live + (GROUP - 1), GROUP), step, 0)
+    lax.fori_loop(0, lax.div(live + (WIDER - 1), WIDER), step, 0)
 
 
 def gram_step(count, value_of, total, unroll=8):
@@ -193,7 +194,7 @@
         split[i] = value
         return value
 
-    ext = pad_lanes(fold(gram_step(BR, prepare, jnp.zeros((48, 48), F32), 16)))
+    ext = pad_lanes(fold(gram_step(BR, prepare, jnp.zeros((48, 48), F32), 8)))
     live = counts[0, 0]
     place = term_place(lax.axis_index("y"))
 
@@ -208,7 +209,7 @@
 
         @pl.when(i * GROUP < live)
         def _():
-            group_of(i * GROUP, live, cols, rows, turn, split, acc, place, 16)
+            group_of(GROUP, i * GROUP, live, cols, rows, turn, split, acc, place, 16)
 
         return carry
 
@@ -360,7 +361,7 @@
         def result(i, base=base, first=first, second=second):
             out[:, lanes(base + i)] = mix(factors, stacked(second[i]), stacked(first[i]))
 
-        each(16, result, 8)
+        each(16, result, 4)
 
 
 def by_side(pieces):

time: 173 us -> 172 us (level)
  starting transfers between devices: 77.7 us -> 96.2 us
  waiting for transfers between devices: 58.7 us -> 48.6 us
  Pallas kernels: 34.7 us -> 25.6 us
    pallas_call x11, Pallas kernels: 34.7 us -> 25.6 us  [call(): pl.pallas_call(functools.partial(body, **constants) if constants else bod...]
    ppermute x30, starting transfers between devices: 36.6 us -> 44.7 us  [shift(): return lax.ppermute(value, axis, [(i, (i + k) % 4) for i in range(4)])]
    ppermute x30, waiting for transfers between devices: 41 us -> 33.8 us  [shift(): return lax.ppermute(value, axis, [(i, (i + k) % 4) for i in range(4)])]
    ppermute x2, starting transfers between devices: 6.52 us -> 13.5 us  [scatter_doc(): got = lax.ppermute(other, 'c', SWAP)]
    ppermute x1, starting transfers between devices: 1.76 us -> 6.01 us  [local(): ext = ext + lax.ppermute(ext, 'zh', SWAP)]
    ppermute x1, waiting for transfers between devices: 1.76 us -> 0.01 us  [local(): ext = ext + lax.ppermute(ext, 'zh', SWAP)]
  transfers between devices with their start and end apart: 44 -> 44, of which waited for: 30 -> 26; matrix products, arithmetic and copies ran while one was open for 0% -> 0% of each run, Pallas kernels for 3% -> 4%
where the time goes in v5:
time: 172 us; the launch traced here: 173 us
  starting transfers between devices  96.2 us (56%)
  waiting for transfers between devices  48.6 us (28%)
  Pallas kernels  25.6 us (15%)
    ppermute x30, starting transfers between devices, shift(): return lax.ppermute(value, axis, [(i, (i + k) % 4) for i in range(4)])  44.7 us
    ppermute x30, waiting for transfers between devices, shift(): return lax.ppermute(value, axis, [(i, (i + k) % 4) for i in range(4)])  33.8 us
    pallas_call x11, Pallas kernels, call(): pl.pallas_call(functools.partial(body, **constants) if constants else bod...  25.6 us
    ppermute x2, starting transfers between devices, scatter_doc(): got = lax.ppermute(other, 'c', SWAP)  13.5 us
    ppermute x2, starting transfers between devices, scatter_term(): return (mine, lax.ppermute(mine, 'zh', SWAP))  13.2 us
    ppermute x4, starting transfers between devices, gather_doc(): return mine + [lax.ppermute(m, 'c', SWAP) for m in mine]  9.19 us
    all_to_all x1, starting transfers between devices, local(): lax.all_to_all(jnp.broadcast_to(ext[None], (SHARERS, 8, BLK)), ('c', 'x',...  8.49 us
    ppermute x1, starting transfers between devices, local(): ext = ext + lax.ppermute(ext, 'zh', SWAP)  6.01 us
  transfers between devices with their start and end apart: 44, of which 26 were waited for; matrix products, arithmetic and copies ran while one was open for 0% of the time, Pallas kernels for 4%

profile of v5, /device:TPU:1, one launch (start us, length us, event | category | flops | bytes accessed | tf_op | source)
XLA Modules:
  0.0 172.8 jit_solution(2518066779363044364)
XLA Ops:
  1.3 5.0 %first_forward.1 = (f32[17,16,128]{2,1,0:T(8,128)S(1)}, f32[17,16,128]{2,1,0:T(8,128)S(1)}, f32[17,16,128]{2,1,0:T(8,128)S(1)}, f32[17,16,128]{2,1,0:T(8,128)S(1...) custom-call(s32[1,320]{1,0:T(1,128)} %rows.5, s32[1,320]{1,0:T(1,128)} %cols.5, ...), custom_call_target="tpu_custom_call" | custom-call | flops 2000000000 | bytes 2000000 | tf_op jit(solution)/shard_map/first_forward/pallas_call | solution.py:434
  6.3 5.1 %collective-permute-start = (f32[17,16,128]{2,1,0:T(8,128)S(1)}, f32[17,16,128]{2,1,0:T(8,128)S(1)}, u32[]{:S(2)}, u32[]{:S(2)}) collective-permute-start(f32[17,16,128]{2,1,0:T(8,128)S(1)} %get-tuple-element.34), channel_id=1, source_target_pairs={{0,2},{2,4},{4,6},{6,0},{1,3},{3,5},{5,7},{7,1},{8,10},{10,12},{12... | collective-permute-start | bytes 417800 | tf_op jit(solution)/shard_map/ppermute | solution.py:452
  11.4 2.5 %collective-permute-start.2 = (f32[17,16,128]{2,1,0:T(8,128)S(1)}, f32[17,16,128]{2,1,0:T(8,128)S(1)}, u32[]{:S(2)}, u32[]{:S(2)}) collective-permute-start(f32[17,16,128]{2,1,0:T(8,128)S(1)} %get-tuple-element.36), channel_id=1, source_target_pairs={{0,6},{2,0},{4,2},{6,4},{1,7},{3,1},{5,3},{7,5},{8,14},{10,8},{12,... | collective-permute-start | bytes 417800 | tf_op jit(solution)/shard_map/ppermute | solution.py:452
  13.9 3.7 %collective-permute-done.1 = f32[17,16,128]{2,1,0:T(8,128)S(1)} collective-permute-done((f32[17,16,128]{2,1,0:T(8,128)S(1)}, f32[17,16,128]{2,1,0:T(8,128)S(1)}, u32[]{:S(2)}, u32[]{:S(2)}) %collective-permute-start.1) | collective-permute-done | bytes 139296 | tf_op jit(solution)/shard_map/ppermute | solution.py:452
  17.6 6.2 %collective-permute-start.3 = (f32[17,16,128]{2,1,0:T(8,128)S(1)}, f32[17,16,128]{2,1,0:T(8,128)S(1)}, u32[]{:S(2)}, u32[]{:S(2)}) collective-permute-start(f32[17,16,128]{2,1,0:T(8,128)S(1)} %add_add_fusion.1.mine), channel_id=1, source_target_pairs={{0,1},{1,0},{2,3},{3,2},{4,5},{5,4},{6,7},{7,6},{8,9},{9,8},{10,11... | collective-permute-start | bytes 417800 | tf_op jit(solution)/shard_map/ppermute | solution.py:466
  23.8 2.5 %collective-permute-done.3.theirs = f32[17,16,128]{2,1,0:T(8,128)S(1)} collective-permute-done((f32[17,16,128]{2,1,0:T(8,128)S(1)}, f32[17,16,128]{2,1,0:T(8,128)S(1)}, u32[]{:S(2)}, u32[]{:S(2)}) %collective-permute-start.3) | collective-permute-done | bytes 139296 | tf_op jit(solution)/shard_map/ppermute | solution.py:466
  26.3 0.8 left_first.1
  27.2 2.7 %collective-permute-start.6 = (f32[17,16,128]{2,1,0:T(8,128)S(1)}, f32[17,16,128]{2,1,0:T(8,128)S(1)}, u32[]{:S(2)}, u32[]{:S(2)}) collective-permute-start(f32[17,16,128]{2,1,0:T(8,128)S(1)} %get-tuple-element.37.p0.left_raw.a0), channel_id=1, source_target_pairs={{0,6},{2,0},{4,2},{6,4},{1,7},{3,1},{5,3},{7,5},{8,14},{10,8},{12,... | collective-permute-start | bytes 417800 | tf_op jit(solution)/shard_map/ppermute | solution.py:452
  29.9 0.9 collective-permute-start.5
  30.8 2.6 %collective-permute-done.6.p3.a3 = f32[17,16,128]{2,1,0:T(8,128)S(1)} collective-permute-done((f32[17,16,128]{2,1,0:T(8,128)S(1)}, f32[17,16,128]{2,1,0:T(8,128)S(1)}, u32[]{:S(2)}, u32[]{:S(2)}) %collective-permute-start.6) | collective-permute-done | bytes 139296 | tf_op jit(solution)/shard_map/ppermute | solution.py:452
  33.3 2.0 %collective-permute-done.5.p2.a2 = f32[17,16,128]{2,1,0:T(8,128)S(1)} collective-permute-done((f32[17,16,128]{2,1,0:T(8,128)S(1)}, f32[17,16,128]{2,1,0:T(8,128)S(1)}, u32[]{:S(2)}, u32[]{:S(2)}) %collective-permute-start.5) | collective-permute-done | bytes 139296 | tf_op jit(solution)/shard_map/ppermute | solution.py:452
  35.4 1.4 collective-permute-done.4.p1.a1
  36.8 2.3 %backward.2 = (f32[36,16,128]{2,1,0:T(8,128)S(1)}, f32[36,16,128]{2,1,0:T(8,128)S(1)}) custom-call(s32[1,320]{1,0:T(1,128)S(1)} %copy-done.1, s32[1,320]{1,0:T(1,128)S(1)} %copy-done.2, s32[1,1]{1,0:T(1,128)S(6)} %copy.7.counts_any.counts, f32[17,16,128]{2,1,0:T(8,128)S(1)} %get-tuple-element.37.p0.left_raw.a0, ...), custom_call_target="tpu_custom_call" | custom-call | flops 2000000000 | bytes 2000000 | tf_op jit(solution)/shard_map/backward/pallas_call | solution.py:434
  39.1 7.0 %collective-permute-start.7 = (f32[36,16,128]{2,1,0:T(8,128)S(1)}, f32[36,16,128]{2,1,0:T(8,128)S(1)}, u32[]{:S(2)}, u32[]{:S(2)}) collective-permute-start(f32[36,16,128]{2,1,0:T(8,128)S(1)} %get-tuple-element.40), channel_id=1, source_target_pairs={{0,8},{8,0},{1,9},{9,1},{2,10},{10,2},{3,11},{11,3},{4,12},{12,4},... | collective-permute-start | bytes 884744 | tf_op jit(solution)/shard_map/ppermute | solution.py:470
  46.1 1.2 collective-permute-done.7
  47.4 2.2 %collective-permute-start.8 = (f32[9,16,128]{2,1,0:T(8,128)S(1)}, f32[9,16,128]{2,1,0:T(8,128)S(1)}, u32[]{:S(2)}, u32[]{:S(2)}) collective-permute-start(f32[9,16,128]{2,1,0:T(8,128)S(1)} %get-tuple-element.67), channel_id=1, source_target_pairs={{0,16},{16,32},{32,48},{48,0},{1,17},{17,33},{33,49},{49,1},{2,18}... | collective-permute-start | bytes 221192 | tf_op jit(solution)/shard_map/ppermute | solution.py:452
  49.5 2.6 %collective-permute-start.10 = (f32[9,16,128]{2,1,0:T(8,128)S(1)}, f32[9,16,128]{2,1,0:T(8,128)S(1)}, u32[]{:S(2)}, u32[]{:S(2)}) collective-permute-start(f32[9,16,128]{2,1,0:T(8,128)S(1)} %get-tuple-element.68), channel_id=1, source_target_pairs={{0,48},{16,0},{32,16},{48,32},{1,49},{17,1},{33,17},{49,33},{2,50}... | collective-permute-start | bytes 221192 | tf_op jit(solution)/shard_map/ppermute | solution.py:452
  52.1 1.1 collective-permute-start.9
  53.2 1.2 collective-permute-done.8
  54.4 2.5 %collective-permute-done.9 = f32[9,16,128]{2,1,0:T(8,128)S(1)} collective-permute-done((f32[9,16,128]{2,1,0:T(8,128)S(1)}, f32[9,16,128]{2,1,0:T(8,128)S(1)}, u32[]{:S(2)}, u32[]{:S(2)}) %collective-permute-start.9) | collective-permute-done | bytes 73760 | tf_op jit(solution)/shard_map/ppermute | solution.py:452
  56.9 4.2 %collective-permute-start.13 = (f32[9,16,128]{2,1,0:T(8,128)S(1)}, f32[9,16,128]{2,1,0:T(8,128)S(1)}, u32[]{:S(2)}, u32[]{:S(2)}) collective-permute-start(f32[9,16,128]{2,1,0:T(8,128)S(1)} %fusion.5.t0), channel_id=1, source_target_pairs={{0,192},{64,0},{128,64},{192,128},{1,193},{65,1},{129,65},{193,129... | collective-permute-start | bytes 221192 | tf_op jit(solution)/shard_map/ppermute | solution.py:452
  61.1 1.2 collective-permute-start.12
  62.3 1.4 collective-permute-start.11
  63.7 2.6 %collective-permute-done.12.t2 = f32[9,16,128]{2,1,0:T(8,128)S(1)} collective-permute-done((f32[9,16,128]{2,1,0:T(8,128)S(1)}, f32[9,16,128]{2,1,0:T(8,128)S(1)}, u32[]{:S(2)}, u32[]{:S(2)}) %collective-permute-start.12) | collective-permute-done | bytes 73760 | tf_op jit(solution)/shard_map/ppermute | solution.py:452
  66.3 1.9 %collective-permute-done.11.t1 = f32[9,16,128]{2,1,0:T(8,128)S(1)} collective-permute-done((f32[9,16,128]{2,1,0:T(8,128)S(1)}, f32[9,16,128]{2,1,0:T(8,128)S(1)}, u32[]{:S(2)}, u32[]{:S(2)}) %collective-permute-start.11) | collective-permute-done | bytes 73760 | tf_op jit(solution)/shard_map/ppermute | solution.py:452
  68.2 1.1 right_first.1
  69.3 1.3 collective-permute-start.16
  70.5 1.1 collective-permute-start.15
  71.7 3.6 %collective-permute-start.17 = (f32[9,16,128]{2,1,0:T(8,128)S(1)}, f32[9,16,128]{2,1,0:T(8,128)S(1)}, u32[]{:S(2)}, u32[]{:S(2)}) collective-permute-start(f32[9,16,128]{2,1,0:T(8,128)S(1)} %get-tuple-element.42.r0.right_raw), channel_id=1, source_target_pairs={{0,8},{8,0},{1,9},{9,1},{2,10},{10,2},{3,11},{11,3},{4,12},{12,4},... | collective-permute-start | bytes 221192 | tf_op jit(solution)/shard_map/ppermute | solution.py:478
  75.3 0.7 collective-permute-start.20
  76.1 3.4 %collective-permute-start.19 = (f32[9,16,128]{2,1,0:T(8,128)S(1)}, f32[9,16,128]{2,1,0:T(8,128)S(1)}, u32[]{:S(2)}, u32[]{:S(2)}) collective-permute-start(f32[9,16,128]{2,1,0:T(8,128)S(1)} %collective-permute-done.15.r2), channel_id=1, source_target_pairs={{0,8},{8,0},{1,9},{9,1},{2,10},{10,2},{3,11},{11,3},{4,12},{12,4},... | collective-permute-start | bytes 221192 | tf_op jit(solution)/shard_map/ppermute | solution.py:478
  79.5 1.4 collective-permute-start.18
  80.9 0.9 collective-permute-done.18.w1
  81.8 2.3 %forward.1 = (f32[17,16,128]{2,1,0:T(8,128)S(1)}, f32[17,16,128]{2,1,0:T(8,128)S(1)}, f32[17,16,128]{2,1,0:T(8,128)S(1)}, f32[17,16,128]{2,1,0:T(8,128)S(1)}) custom-call(s32[1,320]{1,0:T(1,128)S(1)} %copy-done.1, s32[1,320]{1,0:T(1,128)S(1)} %copy-done.2, s32[1,1]{1,0:T(1,128)S(6)} %copy.7.counts_any.counts, ...), custom_call_target="tpu_custom_call" | custom-call | flops 2000000000 | bytes 2000000 | tf_op jit(solution)/shard_map/forward/pallas_call | solution.py:434
  84.1 0.7 collective-permute-start.21
  84.9 1.2 collective-permute-start.22
  86.0 1.3 collective-permute-start.23
  87.3 3.4 %collective-permute-done.21 = f32[17,16,128]{2,1,0:T(8,128)S(1)} collective-permute-done((f32[17,16,128]{2,1,0:T(8,128)S(1)}, f32[17,16,128]{2,1,0:T(8,128)S(1)}, u32[]{:S(2)}, u32[]{:S(2)}) %collective-permute-start.21) | collective-permute-done | bytes 139296 | tf_op jit(solution)/shard_map/ppermute | solution.py:452
  90.8 0.9 collective-permute-done.23
  91.7 7.0 %collective-permute-start.24 = (f32[17,16,128]{2,1,0:T(8,128)S(1)}, f32[17,16,128]{2,1,0:T(8,128)S(1)}, u32[]{:S(2)}, u32[]{:S(2)}) collective-permute-start(f32[17,16,128]{2,1,0:T(8,128)S(1)} %add_add_fusion.mine), channel_id=1, source_target_pairs={{0,1},{1,0},{2,3},{3,2},{4,5},{5,4},{6,7},{7,6},{8,9},{9,8},{10,11... | collective-permute-start | bytes 417800 | tf_op jit(solution)/shard_map/ppermute | solution.py:466
  98.7 2.5 %collective-permute-done.24.theirs = f32[17,16,128]{2,1,0:T(8,128)S(1)} collective-permute-done((f32[17,16,128]{2,1,0:T(8,128)S(1)}, f32[17,16,128]{2,1,0:T(8,128)S(1)}, u32[]{:S(2)}, u32[]{:S(2)}) %collective-permute-start.24) | collective-permute-done | bytes 139296 | tf_op jit(solution)/shard_map/ppermute | solution.py:466
  101.3 1.3 left_second.1
  102.5 2.8 %collective-permute-start.27 = (f32[17,16,128]{2,1,0:T(8,128)S(1)}, f32[17,16,128]{2,1,0:T(8,128)S(1)}, u32[]{:S(2)}, u32[]{:S(2)}) collective-permute-start(f32[17,16,128]{2,1,0:T(8,128)S(1)} %get-tuple-element.49.p0.b0), channel_id=1, source_target_pairs={{0,6},{2,0},{4,2},{6,4},{1,7},{3,1},{5,3},{7,5},{8,14},{10,8},{12,... | collective-permute-start | bytes 417800 | tf_op jit(solution)/shard_map/ppermute | solution.py:452
  106.0 2.8 %collective-permute-done.27.p3.b3 = f32[17,16,128]{2,1,0:T(8,128)S(1)} collective-permute-done((f32[17,16,128]{2,1,0:T(8,128)S(1)}, f32[17,16,128]{2,1,0:T(8,128)S(1)}, u32[]{:S(2)}, u32[]{:S(2)}) %collective-permute-start.27) | collective-permute-done | bytes 139296 | tf_op jit(solution)/shard_map/ppermute | solution.py:452
  108.8 2.0 %collective-permute-done.26.p2.b2 = f32[17,16,128]{2,1,0:T(8,128)S(1)} collective-permute-done((f32[17,16,128]{2,1,0:T(8,128)S(1)}, f32[17,16,128]{2,1,0:T(8,128)S(1)}, u32[]{:S(2)}, u32[]{:S(2)}) %collective-permute-start.26) | collective-permute-done | bytes 139296 | tf_op jit(solution)/shard_map/ppermute | solution.py:452
  110.8 1.1 collective-permute-done.25.p1.b1
  111.9 2.3 %backward.3 = (f32[36,16,128]{2,1,0:T(8,128)S(1)}, f32[36,16,128]{2,1,0:T(8,128)S(1)}) custom-call(s32[1,320]{1,0:T(1,128)S(1)} %copy-done.1, s32[1,320]{1,0:T(1,128)S(1)} %copy-done.2, s32[1,1]{1,0:T(1,128)S(6)} %copy.7.counts_any.counts, f32[17,16,128]{2,1,0:T(8,128)S(1)} %get-tuple-element.49.p0.b0, f32[17,16,128]{2,1,0:T(8,128)S(1)} %collective-permute-done.25.p1.b1, ...), custom_call_target="tpu_custom_call" | custom-call | flops 2000000000 | bytes 2000000 | tf_op jit(solution)/shard_map/backward/pallas_call | solution.py:434
  114.2 6.5 %collective-permute-start.28 = (f32[36,16,128]{2,1,0:T(8,128)S(1)}, f32[36,16,128]{2,1,0:T(8,128)S(1)}, u32[]{:S(2)}, u32[]{:S(2)}) collective-permute-start(f32[36,16,128]{2,1,0:T(8,128)S(1)} %get-tuple-element.51), channel_id=1, source_target_pairs={{0,8},{8,0},{1,9},{9,1},{2,10},{10,2},{3,11},{11,3},{4,12},{12,4},... | collective-permute-start | bytes 884744 | tf_op jit(solution)/shard_map/ppermute | solution.py:470
  120.7 1.2 collective-permute-done.28
  121.9 1.6 collective-permute-start.29
  123.6 2.2 %collective-permute-start.31 = (f32[9,16,128]{2,1,0:T(8,128)S(1)}, f32[9,16,128]{2,1,0:T(8,128)S(1)}, u32[]{:S(2)}, u32[]{:S(2)}) collective-permute-start(f32[9,16,128]{2,1,0:T(8,128)S(1)} %get-tuple-element.65), channel_id=1, source_target_pairs={{0,48},{16,0},{32,16},{48,32},{1,49},{17,1},{33,17},{49,33},{2,50}... | collective-permute-start | bytes 221192 | tf_op jit(solution)/shard_map/ppermute | solution.py:452
  125.7 1.1 collective-permute-start.30
  126.8 1.2 collective-permute-done.29
  128.0 2.5 %collective-permute-done.30 = f32[9,16,128]{2,1,0:T(8,128)S(1)} collective-permute-done((f32[9,16,128]{2,1,0:T(8,128)S(1)}, f32[9,16,128]{2,1,0:T(8,128)S(1)}, u32[]{:S(2)}, u32[]{:S(2)}) %collective-permute-start.30) | collective-permute-done | bytes 73760 | tf_op jit(solution)/shard_map/ppermute | solution.py:452
  130.6 4.1 %collective-permute-start.33 = (f32[9,16,128]{2,1,0:T(8,128)S(1)}, f32[9,16,128]{2,1,0:T(8,128)S(1)}, u32[]{:S(2)}, u32[]{:S(2)}) collective-permute-start(f32[9,16,128]{2,1,0:T(8,128)S(1)} %fusion.2.t0), channel_id=1, source_target_pairs={{0,128},{64,192},{128,0},{192,64},{1,129},{65,193},{129,1},{193,65... | collective-permute-start | bytes 221192 | tf_op jit(solution)/shard_map/ppermute | solution.py:452
  135.3 3.0 %right_prior.1.prior.right1 = bf16[64,48,128]{2,1,0:T(8,128)(2,1)S(1)} custom-call(f32[9,16,128]{2,1,0:T(8,128)S(1)} %get-tuple-element.42.r0.right_raw, f32[9,16,128]{2,1,0:T(8,128)S(1)} %collective-permute-done.14.r1, f32[9,16,128]{2,1,0:T(8,128)S(1)} %collective-permute-done.15.r2, f32[9,16,128]{2,1,0:T(8,128)S(1)} %collective-permute-done.16.r3, ...), custom_call_target="tpu_custom_call" | custom-call | flops 2000000000 | bytes 2000000 | tf_op jit(solution)/shard_map/right_prior/pallas_call | solution.py:434
  138.4 2.2 %collective-permute-done.32.t1 = f32[9,16,128]{2,1,0:T(8,128)S(1)} collective-permute-done((f32[9,16,128]{2,1,0:T(8,128)S(1)}, f32[9,16,128]{2,1,0:T(8,128)S(1)}, u32[]{:S(2)}, u32[]{:S(2)}) %collective-permute-start.32) | collective-permute-done | bytes 73760 | tf_op jit(solution)/shard_map/ppermute | solution.py:452
  140.5 1.1 right_second.1
  141.7 1.4 collective-permute-start.38
  143.7 6.0 %collective-permute-start.35 = (f32[8,128]{1,0:T(8,128)S(1)}, f32[8,128]{1,0:T(8,128)S(1)}, u32[]{:S(2)}, u32[]{:S(2)}) collective-permute-start(f32[8,128]{1,0:T(8,128)S(1)} %get-tuple-element.54), channel_id=1, source_target_pairs={{0,1},{1,0},{2,3},{3,2},{4,5},{5,4},{6,7},{7,6},{8,9},{9,8},{10,11... | collective-permute-start | bytes 12296 | tf_op jit(solution)/shard_map/ppermute | solution.py:525
  149.7 4.0 %left_result.1 = f32[16,8192]{1,0:T(8,128)} custom-call(f32[17,16,128]{2,1,0:T(8,128)S(1)} %get-tuple-element.37.p0.left_raw.a0, f32[17,16,128]{2,1,0:T(8,128)S(1)} %collective-permute-done.4.p1.a1, f32[17,16,128]{2,1,0:T(8,128)S(1)} %collective-permute-done.5.p2.a2, f32[17,16,128]{2,1,0:T(8,128)S(1)} %collective-permute-done.6.p3.a3, ...), custom_call_target="tpu_custom_call" | custom-call | flops 2000000000 | bytes 2000000 | tf_op jit(solution)/shard_map/left_result/pallas_call | solution.py:434
  154.4 8.5 %all-to-all-start = ((f32[32,8,128]{2,1,0:T(8,128)}), f32[32,8,128]{2,1,0:T(8,128)S(1)}, u32[]{:S(2)}, u32[]{:S(2)}) async-start(f32[32,8,128]{2,1,0:T(8,128)} %broadcast_in_dim.2), calls=%async_computation | async-start | bytes 262144 | tf_op jit(solution)/shard_map/all_to_all | solution.py:527
  165.0 5.5 %all-to-all-done.ext = f32[32,8,128]{2,1,0:T(8,128)S(1)} async-done(((f32[32,8,128]{2,1,0:T(8,128)}), f32[32,8,128]{2,1,0:T(8,128)S(1)}, u32[]{:S(2)}, u32[]{:S(2)}) %all-to-all-start) | async-done | bytes 131104 | tf_op jit(solution)/shard_map/all_to_all | solution.py:527
  170.4 2.3 %right_result.1 = f32[16,8192]{1,0:T(8,128)} custom-call(f32[32,8,128]{2,1,0:T(8,128)S(1)} %all-to-all-done.ext, f32[8,16,128]{2,1,0:T(8,128)S(1)} %get-tuple-element.60.r0, f32[8,16,128]{2,1,0:T(8,128)S(1)} %collective-permute-done.36.r1, f32[8,16,128]{2,1,0:T(8,128)S(1)} %collective-permute-done.37.r2, f32[8,16,128]{2,1,0:T(8,128)S(1)} %collective-permute-done.38.r3, ...), custom_call_target="tpu_custom_call" | custom-call | flops 2000000000 | bytes 2000000 | tf_op jit(solution)/shard_map/right_result/pallas_call | solution.py:434
  (49 shorter events, 5.1 us)
Async XLA Ops:
  0.6 36.1 %copy-start.2 = (s32[1,320]{1,0:T(1,128)S(1)}, s32[1,320]{1,0:T(1,128)}, u32[]{:S(2)}) copy-start(s32[1,320]{1,0:T(1,128)} %cols.5) | copy-start | bytes 3844
  0.6 36.1 %copy-start.1 = (s32[1,320]{1,0:T(1,128)S(1)}, s32[1,320]{1,0:T(1,128)}, u32[]{:S(2)}) copy-start(s32[1,320]{1,0:T(1,128)} %rows.5) | copy-start | bytes 3844
  6.3 61.9 %copy-start = (f32[16,8192]{1,0:T(8,128)S(1)}, f32[16,8192]{1,0:T(8,128)}, u32[]{:S(2)}) copy-start(f32[16,8192]{1,0:T(8,128)} %start.3) | copy-start | bytes 1572868
  6.3 7.6 %collective-permute-start = (f32[17,16,128]{2,1,0:T(8,128)S(1)}, f32[17,16,128]{2,1,0:T(8,128)S(1)}, u32[]{:S(2)}, u32[]{:S(2)}) collective-permute-start(f32[17,16,128]{2,1,0:T(8,128)S(1)} %get-tuple-element.34), channel_id=1, source_target_pairs={{0,2},{2,4},{4,6},{6,0},{1,3},{3,5},{5,7},{7,1},{8,10},{10,12},{12... | collective-permute-start | bytes 417800 | tf_op jit(solution)/shard_map/ppermute | solution.py:452
  11.4 6.1 %collective-permute-start.1 = (f32[17,16,128]{2,1,0:T(8,128)S(1)}, f32[17,16,128]{2,1,0:T(8,128)S(1)}, u32[]{:S(2)}, u32[]{:S(2)}) collective-permute-start(f32[17,16,128]{2,1,0:T(8,128)S(1)} %get-tuple-element.35), channel_id=1, source_target_pairs={{0,4},{2,6},{4,0},{6,2},{1,5},{3,7},{5,1},{7,3},{8,12},{10,14},{12... | collective-permute-start | bytes 417800 | tf_op jit(solution)/shard_map/ppermute | solution.py:452
  11.4 6.1 %collective-permute-start.2 = (f32[17,16,128]{2,1,0:T(8,128)S(1)}, f32[17,16,128]{2,1,0:T(8,128)S(1)}, u32[]{:S(2)}, u32[]{:S(2)}) collective-permute-start(f32[17,16,128]{2,1,0:T(8,128)S(1)} %get-tuple-element.36), channel_id=1, source_target_pairs={{0,6},{2,0},{4,2},{6,4},{1,7},{3,1},{5,3},{7,5},{8,14},{10,8},{12,... | collective-permute-start | bytes 417800 | tf_op jit(solution)/shard_map/ppermute | solution.py:452
  17.6 8.7 %collective-permute-start.3 = (f32[17,16,128]{2,1,0:T(8,128)S(1)}, f32[17,16,128]{2,1,0:T(8,128)S(1)}, u32[]{:S(2)}, u32[]{:S(2)}) collective-permute-start(f32[17,16,128]{2,1,0:T(8,128)S(1)} %add_add_fusion.1.mine), channel_id=1, source_target_pairs={{0,1},{1,0},{2,3},{3,2},{4,5},{5,4},{6,7},{7,6},{8,9},{9,8},{10,11... | collective-permute-start | bytes 417800 | tf_op jit(solution)/shard_map/ppermute | solution.py:466
  27.2 6.2 %collective-permute-start.6 = (f32[17,16,128]{2,1,0:T(8,128)S(1)}, f32[17,16,128]{2,1,0:T(8,128)S(1)}, u32[]{:S(2)}, u32[]{:S(2)}) collective-permute-start(f32[17,16,128]{2,1,0:T(8,128)S(1)} %get-tuple-element.37.p0.left_raw.a0), channel_id=1, source_target_pairs={{0,6},{2,0},{4,2},{6,4},{1,7},{3,1},{5,3},{7,5},{8,14},{10,8},{12,... | collective-permute-start | bytes 417800 | tf_op jit(solution)/shard_map/ppermute | solution.py:452
  29.9 5.5 %collective-permute-start.5 = (f32[17,16,128]{2,1,0:T(8,128)S(1)}, f32[17,16,128]{2,1,0:T(8,128)S(1)}, u32[]{:S(2)}, u32[]{:S(2)}) collective-permute-start(f32[17,16,128]{2,1,0:T(8,128)S(1)} %get-tuple-element.37.p0.left_raw.a0), channel_id=1, source_target_pairs={{0,4},{2,6},{4,0},{6,2},{1,5},{3,7},{5,1},{7,3},{8,12},{10,14},{12... | collective-permute-start | bytes 417800 | tf_op jit(solution)/shard_map/ppermute | solution.py:452
  30.7 6.0 %collective-permute-start.4 = (f32[17,16,128]{2,1,0:T(8,128)S(1)}, f32[17,16,128]{2,1,0:T(8,128)S(1)}, u32[]{:S(2)}, u32[]{:S(2)}) collective-permute-start(f32[17,16,128]{2,1,0:T(8,128)S(1)} %get-tuple-element.37.p0.left_raw.a0), channel_id=1, source_target_pairs={{0,2},{2,4},{4,6},{6,0},{1,3},{3,5},{5,7},{7,1},{8,10},{10,12},{12... | collective-permute-start | bytes 417800 | tf_op jit(solution)/shard_map/ppermute | solution.py:452
  39.1 8.3 %collective-permute-start.7 = (f32[36,16,128]{2,1,0:T(8,128)S(1)}, f32[36,16,128]{2,1,0:T(8,128)S(1)}, u32[]{:S(2)}, u32[]{:S(2)}) collective-permute-start(f32[36,16,128]{2,1,0:T(8,128)S(1)} %get-tuple-element.40), channel_id=1, source_target_pairs={{0,8},{8,0},{1,9},{9,1},{2,10},{10,2},{3,11},{11,3},{4,12},{12,4},... | collective-permute-start | bytes 884744 | tf_op jit(solution)/shard_map/ppermute | solution.py:470
  47.4 7.0 %collective-permute-start.8 = (f32[9,16,128]{2,1,0:T(8,128)S(1)}, f32[9,16,128]{2,1,0:T(8,128)S(1)}, u32[]{:S(2)}, u32[]{:S(2)}) collective-permute-start(f32[9,16,128]{2,1,0:T(8,128)S(1)} %get-tuple-element.67), channel_id=1, source_target_pairs={{0,16},{16,32},{32,48},{48,0},{1,17},{17,33},{33,49},{49,1},{2,18}... | collective-permute-start | bytes 221192 | tf_op jit(solution)/shard_map/ppermute | solution.py:452
  49.5 4.9 %collective-permute-start.10 = (f32[9,16,128]{2,1,0:T(8,128)S(1)}, f32[9,16,128]{2,1,0:T(8,128)S(1)}, u32[]{:S(2)}, u32[]{:S(2)}) collective-permute-start(f32[9,16,128]{2,1,0:T(8,128)S(1)} %get-tuple-element.68), channel_id=1, source_target_pairs={{0,48},{16,0},{32,16},{48,32},{1,49},{17,1},{33,17},{49,33},{2,50}... | collective-permute-start | bytes 221192 | tf_op jit(solution)/shard_map/ppermute | solution.py:452
  52.1 4.7 %collective-permute-start.9 = (f32[9,16,128]{2,1,0:T(8,128)S(1)}, f32[9,16,128]{2,1,0:T(8,128)S(1)}, u32[]{:S(2)}, u32[]{:S(2)}) collective-permute-start(f32[9,16,128]{2,1,0:T(8,128)S(1)} %get-tuple-element.69), channel_id=1, source_target_pairs={{0,32},{16,48},{32,0},{48,16},{1,33},{17,49},{33,1},{49,17},{2,34}... | collective-permute-start | bytes 221192 | tf_op jit(solution)/shard_map/ppermute | solution.py:452
  56.9 6.8 %collective-permute-start.13 = (f32[9,16,128]{2,1,0:T(8,128)S(1)}, f32[9,16,128]{2,1,0:T(8,128)S(1)}, u32[]{:S(2)}, u32[]{:S(2)}) collective-permute-start(f32[9,16,128]{2,1,0:T(8,128)S(1)} %fusion.5.t0), channel_id=1, source_target_pairs={{0,192},{64,0},{128,64},{192,128},{1,193},{65,1},{129,65},{193,129... | collective-permute-start | bytes 221192 | tf_op jit(solution)/shard_map/ppermute | solution.py:452
  61.1 5.2 %collective-permute-start.12 = (f32[9,16,128]{2,1,0:T(8,128)S(1)}, f32[9,16,128]{2,1,0:T(8,128)S(1)}, u32[]{:S(2)}, u32[]{:S(2)}) collective-permute-start(f32[9,16,128]{2,1,0:T(8,128)S(1)} %fusion.5.t0), channel_id=1, source_target_pairs={{0,128},{64,192},{128,0},{192,64},{1,129},{65,193},{129,1},{193,65... | collective-permute-start | bytes 221192 | tf_op jit(solution)/shard_map/ppermute | solution.py:452
  62.3 5.9 %collective-permute-start.11 = (f32[9,16,128]{2,1,0:T(8,128)S(1)}, f32[9,16,128]{2,1,0:T(8,128)S(1)}, u32[]{:S(2)}, u32[]{:S(2)}) collective-permute-start(f32[9,16,128]{2,1,0:T(8,128)S(1)} %fusion.5.t0), channel_id=1, source_target_pairs={{0,64},{64,128},{128,192},{192,0},{1,65},{65,129},{129,193},{193,1... | collective-permute-start | bytes 221192 | tf_op jit(solution)/shard_map/ppermute | solution.py:452
  69.3 6.0 %collective-permute-start.16 = (f32[9,16,128]{2,1,0:T(8,128)S(1)}, f32[9,16,128]{2,1,0:T(8,128)S(1)}, u32[]{:S(2)}, u32[]{:S(2)}) collective-permute-start(f32[9,16,128]{2,1,0:T(8,128)S(1)} %get-tuple-element.42.r0.right_raw), channel_id=1, source_target_pairs={{0,48},{16,0},{32,16},{48,32},{1,49},{17,1},{33,17},{49,33},{2,50}... | collective-permute-start | bytes 221192 | tf_op jit(solution)/shard_map/ppermute | solution.py:452
  70.5 5.5 %collective-permute-start.15 = (f32[9,16,128]{2,1,0:T(8,128)S(1)}, f32[9,16,128]{2,1,0:T(8,128)S(1)}, u32[]{:S(2)}, u32[]{:S(2)}) collective-permute-start(f32[9,16,128]{2,1,0:T(8,128)S(1)} %get-tuple-element.42.r0.right_raw), channel_id=1, source_target_pairs={{0,32},{16,48},{32,0},{48,16},{1,33},{17,49},{33,1},{49,17},{2,34}... | collective-permute-start | bytes 221192 | tf_op jit(solution)/shard_map/ppermute | solution.py:452
  71.7 7.8 %collective-permute-start.14 = (f32[9,16,128]{2,1,0:T(8,128)S(1)}, f32[9,16,128]{2,1,0:T(8,128)S(1)}, u32[]{:S(2)}, u32[]{:S(2)}) collective-permute-start(f32[9,16,128]{2,1,0:T(8,128)S(1)} %get-tuple-element.42.r0.right_raw), channel_id=1, source_target_pairs={{0,16},{16,32},{32,48},{48,0},{1,17},{17,33},{33,49},{49,1},{2,18}... | collective-permute-start | bytes 221192 | tf_op jit(solution)/shard_map/ppermute | solution.py:452
  71.7 9.2 %collective-permute-start.17 = (f32[9,16,128]{2,1,0:T(8,128)S(1)}, f32[9,16,128]{2,1,0:T(8,128)S(1)}, u32[]{:S(2)}, u32[]{:S(2)}) collective-permute-start(f32[9,16,128]{2,1,0:T(8,128)S(1)} %get-tuple-element.42.r0.right_raw), channel_id=1, source_target_pairs={{0,8},{8,0},{1,9},{9,1},{2,10},{10,2},{3,11},{11,3},{4,12},{12,4},... | collective-permute-start | bytes 221192 | tf_op jit(solution)/shard_map/ppermute | solution.py:478
  75.3 5.6 %collective-permute-start.20 = (f32[9,16,128]{2,1,0:T(8,128)S(1)}, f32[9,16,128]{2,1,0:T(8,128)S(1)}, u32[]{:S(2)}, u32[]{:S(2)}) collective-permute-start(f32[9,16,128]{2,1,0:T(8,128)S(1)} %collective-permute-done.16.r3), channel_id=1, source_target_pairs={{0,8},{8,0},{1,9},{9,1},{2,10},{10,2},{3,11},{11,3},{4,12},{12,4},... | collective-permute-start | bytes 221192 | tf_op jit(solution)/shard_map/ppermute | solution.py:478
  76.1 4.8 %collective-permute-start.19 = (f32[9,16,128]{2,1,0:T(8,128)S(1)}, f32[9,16,128]{2,1,0:T(8,128)S(1)}, u32[]{:S(2)}, u32[]{:S(2)}) collective-permute-start(f32[9,16,128]{2,1,0:T(8,128)S(1)} %collective-permute-done.15.r2), channel_id=1, source_target_pairs={{0,8},{8,0},{1,9},{9,1},{2,10},{10,2},{3,11},{11,3},{4,12},{12,4},... | collective-permute-start | bytes 221192 | tf_op jit(solution)/shard_map/ppermute | solution.py:478
  79.5 2.3 %collective-permute-start.18 = (f32[9,16,128]{2,1,0:T(8,128)S(1)}, f32[9,16,128]{2,1,0:T(8,128)S(1)}, u32[]{:S(2)}, u32[]{:S(2)}) collective-permute-start(f32[9,16,128]{2,1,0:T(8,128)S(1)} %collective-permute-done.14.r1), channel_id=1, source_target_pairs={{0,8},{8,0},{1,9},{9,1},{2,10},{10,2},{3,11},{11,3},{4,12},{12,4},... | collective-permute-start | bytes 221192 | tf_op jit(solution)/shard_map/ppermute | solution.py:478
  84.1 6.7 %collective-permute-start.21 = (f32[17,16,128]{2,1,0:T(8,128)S(1)}, f32[17,16,128]{2,1,0:T(8,128)S(1)}, u32[]{:S(2)}, u32[]{:S(2)}) collective-permute-start(f32[17,16,128]{2,1,0:T(8,128)S(1)} %get-tuple-element.45), channel_id=1, source_target_pairs={{0,2},{2,4},{4,6},{6,0},{1,3},{3,5},{5,7},{7,1},{8,10},{10,12},{12... | collective-permute-start | bytes 417800 | tf_op jit(solution)/shard_map/ppermute | solution.py:452
  84.9 5.9 %collective-permute-start.22 = (f32[17,16,128]{2,1,0:T(8,128)S(1)}, f32[17,16,128]{2,1,0:T(8,128)S(1)}, u32[]{:S(2)}, u32[]{:S(2)}) collective-permute-start(f32[17,16,128]{2,1,0:T(8,128)S(1)} %get-tuple-element.46), channel_id=1, source_target_pairs={{0,4},{2,6},{4,0},{6,2},{1,5},{3,7},{5,1},{7,3},{8,12},{10,14},{12... | collective-permute-start | bytes 417800 | tf_op jit(solution)/shard_map/ppermute | solution.py:452
  86.0 5.7 %collective-permute-start.23 = (f32[17,16,128]{2,1,0:T(8,128)S(1)}, f32[17,16,128]{2,1,0:T(8,128)S(1)}, u32[]{:S(2)}, u32[]{:S(2)}) collective-permute-start(f32[17,16,128]{2,1,0:T(8,128)S(1)} %get-tuple-element.47), channel_id=1, source_target_pairs={{0,6},{2,0},{4,2},{6,4},{1,7},{3,1},{5,3},{7,5},{8,14},{10,8},{12,... | collective-permute-start | bytes 417800 | tf_op jit(solution)/shard_map/ppermute | solution.py:452
  91.7 9.5 %collective-permute-start.24 = (f32[17,16,128]{2,1,0:T(8,128)S(1)}, f32[17,16,128]{2,1,0:T(8,128)S(1)}, u32[]{:S(2)}, u32[]{:S(2)}) collective-permute-start(f32[17,16,128]{2,1,0:T(8,128)S(1)} %add_add_fusion.mine), channel_id=1, source_target_pairs={{0,1},{1,0},{2,3},{3,2},{4,5},{5,4},{6,7},{7,6},{8,9},{9,8},{10,11... | collective-permute-start | bytes 417800 | tf_op jit(solution)/shard_map/ppermute | solution.py:466
  102.5 6.3 %collective-permute-start.27 = (f32[17,16,128]{2,1,0:T(8,128)S(1)}, f32[17,16,128]{2,1,0:T(8,128)S(1)}, u32[]{:S(2)}, u32[]{:S(2)}) collective-permute-start(f32[17,16,128]{2,1,0:T(8,128)S(1)} %get-tuple-element.49.p0.b0), channel_id=1, source_target_pairs={{0,6},{2,0},{4,2},{6,4},{1,7},{3,1},{5,3},{7,5},{8,14},{10,8},{12,... | collective-permute-start | bytes 417800 | tf_op jit(solution)/shard_map/ppermute | solution.py:452
  105.3 5.5 %collective-permute-start.26 = (f32[17,16,128]{2,1,0:T(8,128)S(1)}, f32[17,16,128]{2,1,0:T(8,128)S(1)}, u32[]{:S(2)}, u32[]{:S(2)}) collective-permute-start(f32[17,16,128]{2,1,0:T(8,128)S(1)} %get-tuple-element.49.p0.b0), channel_id=1, source_target_pairs={{0,4},{2,6},{4,0},{6,2},{1,5},{3,7},{5,1},{7,3},{8,12},{10,14},{12... | collective-permute-start | bytes 417800 | tf_op jit(solution)/shard_map/ppermute | solution.py:452
  105.3 6.6 %collective-permute-start.25 = (f32[17,16,128]{2,1,0:T(8,128)S(1)}, f32[17,16,128]{2,1,0:T(8,128)S(1)}, u32[]{:S(2)}, u32[]{:S(2)}) collective-permute-start(f32[17,16,128]{2,1,0:T(8,128)S(1)} %get-tuple-element.49.p0.b0), channel_id=1, source_target_pairs={{0,2},{2,4},{4,6},{6,0},{1,3},{3,5},{5,7},{7,1},{8,10},{10,12},{12... | collective-permute-start | bytes 417800 | tf_op jit(solution)/shard_map/ppermute | solution.py:452
  114.2 7.7 %collective-permute-start.28 = (f32[36,16,128]{2,1,0:T(8,128)S(1)}, f32[36,16,128]{2,1,0:T(8,128)S(1)}, u32[]{:S(2)}, u32[]{:S(2)}) collective-permute-start(f32[36,16,128]{2,1,0:T(8,128)S(1)} %get-tuple-element.51), channel_id=1, source_target_pairs={{0,8},{8,0},{1,9},{9,1},{2,10},{10,2},{3,11},{11,3},{4,12},{12,4},... | collective-permute-start | bytes 884744 | tf_op jit(solution)/shard_map/ppermute | solution.py:470
  121.9 6.1 %collective-permute-start.29 = (f32[9,16,128]{2,1,0:T(8,128)S(1)}, f32[9,16,128]{2,1,0:T(8,128)S(1)}, u32[]{:S(2)}, u32[]{:S(2)}) collective-permute-start(f32[9,16,128]{2,1,0:T(8,128)S(1)} %get-tuple-element.64), channel_id=1, source_target_pairs={{0,16},{16,32},{32,48},{48,0},{1,17},{17,33},{33,49},{49,1},{2,18}... | collective-permute-start | bytes 221192 | tf_op jit(solution)/shard_map/ppermute | solution.py:452
  123.6 4.4 %collective-permute-start.31 = (f32[9,16,128]{2,1,0:T(8,128)S(1)}, f32[9,16,128]{2,1,0:T(8,128)S(1)}, u32[]{:S(2)}, u32[]{:S(2)}) collective-permute-start(f32[9,16,128]{2,1,0:T(8,128)S(1)} %get-tuple-element.65), channel_id=1, source_target_pairs={{0,48},{16,0},{32,16},{48,32},{1,49},{17,1},{33,17},{49,33},{2,50}... | collective-permute-start | bytes 221192 | tf_op jit(solution)/shard_map/ppermute | solution.py:452
  125.7 4.7 %collective-permute-start.30 = (f32[9,16,128]{2,1,0:T(8,128)S(1)}, f32[9,16,128]{2,1,0:T(8,128)S(1)}, u32[]{:S(2)}, u32[]{:S(2)}) collective-permute-start(f32[9,16,128]{2,1,0:T(8,128)S(1)} %get-tuple-element.66), channel_id=1, source_target_pairs={{0,32},{16,48},{32,0},{48,16},{1,33},{17,49},{33,1},{49,17},{2,34}... | collective-permute-start | bytes 221192 | tf_op jit(solution)/shard_map/ppermute | solution.py:452
  130.5 7.9 %collective-permute-start.34 = (f32[9,16,128]{2,1,0:T(8,128)S(1)}, f32[9,16,128]{2,1,0:T(8,128)S(1)}, u32[]{:S(2)}, u32[]{:S(2)}) collective-permute-start(f32[9,16,128]{2,1,0:T(8,128)S(1)} %fusion.2.t0), channel_id=1, source_target_pairs={{0,192},{64,0},{128,64},{192,128},{1,193},{65,1},{129,65},{193,129... | collective-permute-start | bytes 221192 | tf_op jit(solution)/shard_map/ppermute | solution.py:452
  130.6 7.8 %collective-permute-start.33 = (f32[9,16,128]{2,1,0:T(8,128)S(1)}, f32[9,16,128]{2,1,0:T(8,128)S(1)}, u32[]{:S(2)}, u32[]{:S(2)}) collective-permute-start(f32[9,16,128]{2,1,0:T(8,128)S(1)} %fusion.2.t0), channel_id=1, source_target_pairs={{0,128},{64,192},{128,0},{192,64},{1,129},{65,193},{129,1},{193,65... | collective-permute-start | bytes 221192 | tf_op jit(solution)/shard_map/ppermute | solution.py:452
  134.7 5.9 %collective-permute-start.32 = (f32[9,16,128]{2,1,0:T(8,128)S(1)}, f32[9,16,128]{2,1,0:T(8,128)S(1)}, u32[]{:S(2)}, u32[]{:S(2)}) collective-permute-start(f32[9,16,128]{2,1,0:T(8,128)S(1)} %fusion.2.t0), channel_id=1, source_target_pairs={{0,64},{64,128},{128,192},{192,0},{1,65},{65,129},{129,193},{193,1... | collective-permute-start | bytes 221192 | tf_op jit(solution)/shard_map/ppermute | solution.py:452
  141.7 12.1 %collective-permute-start.38 = (f32[8,16,128]{2,1,0:T(8,128)S(1)}, f32[8,16,128]{2,1,0:T(8,128)S(1)}, u32[]{:S(2)}, u32[]{:S(2)}) collective-permute-start(f32[8,16,128]{2,1,0:T(8,128)S(1)} %get-tuple-element.60.r0), channel_id=1, source_target_pairs={{0,48},{16,0},{32,16},{48,32},{1,49},{17,1},{33,17},{49,33},{2,50}... | collective-permute-start | bytes 196616 | tf_op jit(solution)/shard_map/ppermute | solution.py:452
  143.1 10.6 %collective-permute-start.37 = (f32[8,16,128]{2,1,0:T(8,128)S(1)}, f32[8,16,128]{2,1,0:T(8,128)S(1)}, u32[]{:S(2)}, u32[]{:S(2)}) collective-permute-start(f32[8,16,128]{2,1,0:T(8,128)S(1)} %get-tuple-element.60.r0), channel_id=1, source_target_pairs={{0,32},{16,48},{32,0},{48,16},{1,33},{17,49},{33,1},{49,17},{2,34}... | collective-permute-start | bytes 196616 | tf_op jit(solution)/shard_map/ppermute | solution.py:452
  143.1 10.6 %collective-permute-start.36 = (f32[8,16,128]{2,1,0:T(8,128)S(1)}, f32[8,16,128]{2,1,0:T(8,128)S(1)}, u32[]{:S(2)}, u32[]{:S(2)}) collective-permute-start(f32[8,16,128]{2,1,0:T(8,128)S(1)} %get-tuple-element.60.r0), channel_id=1, source_target_pairs={{0,16},{16,32},{32,48},{48,0},{1,17},{17,33},{33,49},{49,1},{2,18}... | collective-permute-start | bytes 196616 | tf_op jit(solution)/shard_map/ppermute | solution.py:452
  143.7 10.0 %collective-permute-start.35 = (f32[8,128]{1,0:T(8,128)S(1)}, f32[8,128]{1,0:T(8,128)S(1)}, u32[]{:S(2)}, u32[]{:S(2)}) collective-permute-start(f32[8,128]{1,0:T(8,128)S(1)} %get-tuple-element.54), channel_id=1, source_target_pairs={{0,1},{1,0},{2,3},{3,2},{4,5},{5,4},{6,7},{7,6},{8,9},{9,8},{10,11... | collective-permute-start | bytes 12296 | tf_op jit(solution)/shard_map/ppermute | solution.py:525
  154.4 16.0 %all-to-all-start = ((f32[32,8,128]{2,1,0:T(8,128)}), f32[32,8,128]{2,1,0:T(8,128)S(1)}, u32[]{:S(2)}, u32[]{:S(2)}) async-start(f32[32,8,128]{2,1,0:T(8,128)} %broadcast_in_dim.2), calls=%async_computation | async-start | bytes 262144 | tf_op jit(solution)/shard_map/all_to_all | solution.py:527
  162.9 1.3 collective-permute-start.39
  163.2 1.3 collective-permute-start.40
  163.5 1.3 collective-permute-start.41
  163.7 1.3 collective-permute-start.42
